TPU v7x, 32 devices: a whole 2x2x4 slice. The times are simulated.
32 devices in a mesh: fsdp: 2 (over y), ckpt: 4 (over z), dp: 4 (over x, core).
Axes of the slice: x: 2, y: 2, z: 4, core: 2. Of those that a mesh axis runs over, the one named last changes fastest.
Arguments:
- activations: bfloat16 [4, 1536, 4096], P('ckpt', 'dp', 'fsdp'), may hold values from -6 to 6
- gate_weight: bfloat16 [4, 4096, 14336], P('ckpt', 'dp', 'fsdp'), may hold values from -0.09375 to 0.09375
- cotangent: bfloat16 [4, 1536, 14336], P('ckpt', 'dp', 'fsdp'), may hold values from -6 to 6
- sketch_left: bfloat16 [32, 4096], replicated, may hold values from -0.09375 to 0.09375
- sketch_right: bfloat16 [32, 14336], P(None, 'fsdp'), may hold values from -0.046875 to 0.046875
- landmarks: bfloat16 [4, 2048, 1024], P('ckpt', 'dp', 'fsdp'), may hold values from -0.01171875 to 0.01171875
Outputs:
- scores: float32 [12, 2048], P('dp', ('fsdp', 'ckpt'))
All inputs are finite; a program needn't handle non-finite values.
Results may differ from a plain program's by a relative error of at most 0.0042.
Values may be sent and summed in bfloat16 or wider, within the bound.
No kernel may reach another device: no remote copies, remote signals or barrier semaphores. Data moves between devices by JAX's collectives and lax.ppermute only.
A program may use at most 192 MiB of HBM per device.

v0:
```python
import jax
import jax.numpy as jnp
from jax import lax
from jax.sharding import PartitionSpec as P

KA = 32
KB = 32
SEQ = 128


def per_device(activations, gate_weight, cotangent, sketch_left, sketch_right, landmarks):
    local_rows = activations[0]
    full_rows = lax.all_gather(local_rows, "fsdp", axis=1, tiled=True)
    weight = gate_weight[0]
    token_count = local_rows.shape[0]
    preact = jnp.dot(
        full_rows,
        lax.all_gather(weight, "dp", axis=0, tiled=True),
        preferred_element_type=jnp.float32,
    )
    grad_up = (cotangent[0] * jax.nn.silu(preact)).astype(jnp.bfloat16)
    left_sketch = lax.dot_general(
        full_rows, sketch_left, (((1,), (1,)), ((), ())), preferred_element_type=jnp.float32
    )
    right_part = lax.dot_general(
        grad_up, sketch_right, (((1,), (1,)), ((), ())), preferred_element_type=jnp.float32
    )
    examples = token_count // SEQ
    left_three = left_sketch.reshape(examples, SEQ, KA)
    right_sketch = lax.psum(right_part, "fsdp")
    right_three = right_sketch.reshape(examples, SEQ, KB)
    features = jnp.einsum("esa,esb->eab", left_three, right_three, precision=lax.Precision.HIGHEST)
    features = features.reshape(examples, KA * KB)
    share_width = features.shape[1] // lax.axis_size("fsdp")
    features = lax.dynamic_slice_in_dim(
        features, lax.axis_index("fsdp") * share_width, share_width, 1
    )
    features_low = features.astype(jnp.bfloat16)
    panels = lax.dot_general(
        features_low,
        lax.all_gather(landmarks[0], "dp", axis=0, tiled=True),
        (((1,), (1,)), ((), ())),
        preferred_element_type=jnp.float32,
    )
    return lax.psum_scatter(panels, ("fsdp", "ckpt"), scatter_dimension=1, tiled=True)


def solution(mesh):
    in_specs = (
        P("ckpt", "dp", "fsdp"),
        P("ckpt", "dp", "fsdp"),
        P("ckpt", "dp", "fsdp"),
        P(),
        P(None, "fsdp"),
        P("ckpt", "dp", "fsdp"),
    )
    out_specs = P("dp", ("fsdp", "ckpt"))
    return jax.shard_map(
        per_device, mesh=mesh, in_specs=in_specs, out_specs=out_specs, check_vma=False
    )
```

profile of v0, /device:TPU:0, one launch (start us, length us, event | category | flops | bytes accessed | tf_op | source)
XLA Modules:
  0.0 523.1 jit_solution(12853262689414706244)
XLA Ops:
  6.5 0.0 copy-start
  6.5 0.0 copy-start.1
  6.5 0.0 all-gather.7.cloned.1.call-start
  6.5 0.7 all-gather.7.cloned.1.call-update
  7.3 0.0 all-gather.9.cloned.1.call-start
  7.3 0.7 all-gather.9.cloned.1.call-update
  8.0 0.0 all-gather.11.cloned.1.call-start
  8.1 0.7 all-gather.11.cloned.1.call-update
  8.7 0.0 reduce-scatter.4.cloned.1.call-start
  8.8 47.8 %all-gather.7.cloned.1.call-done = bf16[1,384,4096]{2,1,0:T(8,128)(2,1)} async-done(((bf16[1,384,2048]{2,1,0:T(8,128)(2,1)}), bf16[1,384,4096]{2,1,0:T(8,128)(2,1)}) %all-gather.7.cloned.1.call-update) | async-done | bytes 3145744 | tf_op jit(solution)/shard_map/all_gather | solution.py:13
  56.6 0.0 copy-done.1
  56.6 2.9 fusion.9
  59.5 344.7 %all-gather.9.cloned.1.call-done = bf16[1,4096,7168]{2,1,0:T(8,128)(2,1)} async-done(((bf16[1,1024,7168]{2,1,0:T(8,128)(2,1)}), bf16[1,4096,7168]{2,1,0:T(8,128)(2,1)}) %all-gather.9.cloned.1.call-update) | async-done | bytes 58720272 | tf_op jit(solution)/shard_map/all_gather | solution.py:18
  404.2 30.9 %fusion = f32[384,7168]{1,0:T(8,128)S(1)} fusion(bf16[1,4096,7168]{2,1,0:T(8,128)(2,1)} %all-gather.9.cloned.1.call-done, bf16[1,384,4096]{2,1,0:T(8,128)(2,1)} %all-gather.7.cloned.1.call-done), kind=kOutput, calls=%fused_computation | convolution fusion | flops 22548578304 | bytes 72876032 | tf_op jit(solution)/shard_map/dot_general | solution.py:16
  435.1 0.0 copy-done
  435.1 5.0 fusion.12
  440.1 8.6 %psum.7 = f32[3,128,32]{1,2,0:T(8,128)S(1)} all-reduce(f32[3,128,32]{1,2,0:T(8,128)S(1)} %bitcast.35), channel_id=1, replica_groups=mesh['fsdp'=2,'ckpt'=4,'dp'=4] {'fsdp'}, use_global_device_ids=true, to_apply=%region_0.1 | all-reduce | flops 12288 | bytes 98304 | tf_op jit(solution)/shard_map/psum | solution.py:30
  448.7 0.2 fusion.15
  448.9 0.1 reshape.13
  449.0 0.0 all-gather.11.cloned.1.call-done
  449.0 3.2 convolution_bitcast_fusion
  452.3 0.0 reduce-scatter.4.cloned.1.call-update
  452.3 62.7 %reduce-scatter.4.cloned.1.call-done = f32[256,3]{1,0:T(8,128)} async-done(((f32[2048,3]{1,0:T(8,128)}), f32[256,3]{1,0:T(8,128)}) %reduce-scatter.4.cloned.1.call-update) | async-done | bytes 3088
  515.0 1.6 copy.14
  (1 shorter events, 0.0 us)
Async XLA Ops:
  6.5 428.5 %copy-start = (bf16[32,7168]{1,0:T(8,128)(2,1)S(1)}, bf16[32,7168]{1,0:T(8,128)(2,1)}, u32[]{:S(2)}) copy-start(bf16[32,7168]{1,0:T(8,128)(2,1)} %param.10) | copy-start | bytes 1376260
  6.5 50.0 %copy-start.1 = (bf16[32,4096]{1,0:T(8,128)(2,1)S(1)}, bf16[32,4096]{1,0:T(8,128)(2,1)}, u32[]{:S(2)}) copy-start(bf16[32,4096]{1,0:T(8,128)(2,1)} %param.9) | copy-start | bytes 786436
  6.5 50.0 %all-gather.7.cloned.1.call-start = ((), (), s32[]{:S(2)}) async-start(), calls=%async_computation.1 | async-start | bytes 4718592 | tf_op jit(solution)/shard_map/all_gather | solution.py:13
  7.3 396.9 %all-gather.9.cloned.1.call-start = ((), (), s32[]{:S(2)}) async-start(), calls=%async_computation.2 | async-start | bytes 73400320 | tf_op jit(solution)/shard_map/all_gather | solution.py:18
  8.0 441.0 %all-gather.11.cloned.1.call-start = ((), (), s32[]{:S(2)}) async-start(), calls=%async_computation.3 | async-start | bytes 2621440 | tf_op jit(solution)/shard_map/all_gather | solution.py:41
  8.7 506.3 %reduce-scatter.4.cloned.1.call-start = ((), (), s32[]{:S(2)}) async-start(), calls=%async_computation.4 | async-start | bytes 1179648
Sparse Core Ops, SparseCore 0:
  8.9 47.6 all-gather.6
  58.1 345.9 all-gather.8
  405.8 22.5 all-gather.10
  452.4 62.5 reduce-scatter.3
where the time goes:
time: 523 us
  waiting for transfers between devices  457 us (87%)
  matrix products  42.2 us (8%)
  between operations  13.2 us (3%)
  blocking collectives  8.6 us (2%)
    all_gather x1, waiting for transfers between devices, per_device(): lax.all_gather(weight, 'dp', axis=0, tiled=True)  345 us
    unnamed x5, waiting for transfers between devices  64.8 us
    all_gather x1, waiting for transfers between devices, per_device(): full_rows = lax.all_gather(local_rows, 'fsdp', axis=1, tiled=True)  47.8 us
    dot_general x1, matrix products, per_device(): jnp.dot(full_rows, lax.all_gather(weight, 'dp', axis=0, tiled=True), pref...  30.9 us
  transfers between devices with their start and end apart: 4, of which 3 were waited for; matrix products, arithmetic and copies ran while one was open for 7% of the time, Pallas kernels for 0%

commit v1 on v0

v1 whole, which is shorter than its diff:
```python
import jax
import jax.numpy as jnp
from jax import lax
from jax.sharding import PartitionSpec as P

KA = 32
KB = 32
SEQ = 128
F32 = jnp.float32


def dot(a, b, dims):
    return lax.dot_general(a, b, (dims, ((), ())), preferred_element_type=F32)


def make_per_device(n_fsdp, n_ckpt, n_dp):
    n_x = n_dp // 2
    core_pairs = [(i, i ^ 1) for i in range(n_dp)]

    def x_pairs(shift):
        return [(i, (i + 2 * shift) % n_dp) for i in range(n_dp)]

    def swap_core(value):
        return lax.ppermute(value, "dp", core_pairs)

    def shift_x(value, shift):
        return lax.ppermute(value, "dp", x_pairs(shift % n_x))

    square = n_x == 2 and n_fsdp == 2
    both = ("fsdp", "dp")
    off_pairs, on_pairs, y_pairs, y_on_pairs = [], [], [], []
    if square:
        for f in range(2):
            for d in range(n_dp):
                here = f * n_dp + d
                x_target = f * n_dp + (d + 2) % n_dp
                y_target = (1 - f) * n_dp + d
                y_pairs.append((here, y_target))
                if d // 2 == f:
                    on_pairs.append((here, x_target))
                    y_on_pairs.append((here, y_target))
                else:
                    off_pairs.append((here, x_target))

    def spread_square(rows, aligned):
        half = rows.shape[1] // 2
        first, second = rows[:, :half], rows[:, half:]
        direct = lax.ppermute(first, both, off_pairs)
        beside = lax.ppermute(second, both, y_pairs)
        passed = lax.ppermute(beside, both, on_pairs)
        got = jnp.where(aligned, direct, passed)
        partner = lax.ppermute(got, both, y_pairs)
        other = jnp.where(
            aligned,
            jnp.concatenate([got, partner], axis=1),
            jnp.concatenate([partner, got], axis=1),
        )
        own_first = lax.ppermute(first, both, y_on_pairs)
        own = jnp.where(aligned, rows, jnp.concatenate([own_first, beside], axis=1))
        return own, [other]

    def spread_general(rows, x_index, width):
        full = lax.all_gather(rows, "fsdp", axis=1, tiled=True)
        own = lax.dynamic_slice_in_dim(full, x_index * width, width, 1)
        others = []
        for shift in range(1, n_x):
            part = lax.dynamic_slice_in_dim(full, lax.rem(x_index + shift, n_x) * width, width, 1)
            others.append(shift_x(part, shift))
        return own, others

    def scatter_sum(value, axis_name, size):
        index = lax.axis_index(axis_name)
        total = lax.dynamic_index_in_dim(value, index, 1, keepdims=False)
        for shift in range(1, size):
            block = lax.dynamic_index_in_dim(value, lax.rem(index + shift, size), 1, keepdims=False)
            total = total + lax.ppermute(
                block, axis_name, [(i, (i + shift) % size) for i in range(size)]
            )
        return total

    def per_device(activations, gate_weight, cotangent, sketch_left, sketch_right, landmarks):
        f_index = lax.axis_index("fsdp")
        d_index = lax.axis_index("dp")
        x_index, core = d_index // 2, lax.rem(d_index, 2)
        rows = activations[0]
        weight = gate_weight[0]
        tokens, part = rows.shape
        depth, hidden = weight.shape
        quarter = hidden // 2
        width = 2 * depth
        examples = tokens // SEQ

        weight_mine = lax.dynamic_slice_in_dim(weight, core * quarter, quarter, 1)
        weight_theirs = swap_core(
            lax.dynamic_slice_in_dim(weight, (1 - core) * quarter, quarter, 1)
        )
        cot = cotangent[0]
        cot_mine = lax.dynamic_slice_in_dim(cot, core * quarter, quarter, 1)
        cot_theirs = swap_core(lax.dynamic_slice_in_dim(cot, (1 - core) * quarter, quarter, 1))
        right_rows = lax.dynamic_slice_in_dim(sketch_right, core * quarter, quarter, 1)

        marks = lax.all_gather(landmarks[0], "dp", axis=0, tiled=True)
        marks = lax.all_gather(marks, "fsdp", axis=1, tiled=True)

        left_part = dot(
            rows, lax.dynamic_slice_in_dim(sketch_left, f_index * part, part, 1), ((1,), (1,))
        )
        left_mine = lax.psum(left_part, "fsdp") if n_fsdp != 2 else left_part + lax.ppermute(
            left_part, "fsdp", [(0, 1), (1, 0)]
        )
        left_theirs = swap_core(left_mine)

        def product(block):
            low, high = block[:, :depth], block[:, depth:]
            mine = jnp.where(core == 0, low, high)
            theirs = jnp.where(core == 0, high, low)
            return dot(mine, weight_mine, ((1,), (0,))) + dot(theirs, weight_theirs, ((1,), (0,)))

        aligned = x_index == f_index
        own_blocks, received = [], []
        for e in range(examples):
            piece = lax.slice_in_dim(rows, e * SEQ, (e + 1) * SEQ, axis=0)
            if square:
                own, others = spread_square(piece, aligned)
            else:
                own, others = spread_general(piece, x_index, width)
            own_blocks.append(jnp.concatenate([own, swap_core(own)], axis=0))
            arrived = []
            for shift, other in enumerate(others, start=1):
                other_low = product(other).astype(jnp.bfloat16)
                arrived.append([shift_x(other_low, -shift)])
                sibling = product(swap_core(other)).astype(jnp.bfloat16)
                arrived[-1].append(shift_x(sibling, -shift))
            received.append(arrived)

        own_parts = lax.optimization_barrier([product(block) for block in own_blocks])

        features = [[], []]
        for e in range(examples):
            for side, (cot_side, left_side) in enumerate(
                ((cot_mine, left_mine), (cot_theirs, left_theirs))
            ):
                preact = own_parts[e][side * SEQ : (side + 1) * SEQ]
                for arrived in received[e]:
                    preact = preact + arrived[side].astype(F32)
                grad_up = (
                    cot_side[e * SEQ : (e + 1) * SEQ].astype(F32) * jax.nn.silu(preact)
                ).astype(jnp.bfloat16)
                right = dot(grad_up, right_rows, ((1,), (1,)))
                feature = lax.dot_general(
                    left_side[e * SEQ : (e + 1) * SEQ],
                    right,
                    (((0,), (0,)), ((), ())),
                    precision=lax.Precision.HIGHEST,
                )
                features[side].append(feature.reshape(1, KA * KB))
        stacked = jnp.concatenate(features[0] + features[1], axis=0)
        high = stacked.astype(jnp.bfloat16)
        low = (stacked - high.astype(F32)).astype(jnp.bfloat16)
        panels = dot(jnp.concatenate([high, low], axis=0), marks, ((1,), (1,)))
        panels = panels[: 2 * examples] + panels[2 * examples :]

        scores = panels[:examples] + swap_core(panels[examples:])
        marks_here = scores.shape[1] // (n_fsdp * n_ckpt)
        scores = scatter_sum(
            scores.reshape(examples, n_fsdp, n_ckpt * marks_here), "fsdp", n_fsdp
        )
        return scatter_sum(scores.reshape(examples, n_ckpt, marks_here), "ckpt", n_ckpt)

    return per_device


def solution(mesh):
    in_specs = (
        P("ckpt", "dp", "fsdp"),
        P("ckpt", "dp", "fsdp"),
        P("ckpt", "dp", "fsdp"),
        P(),
        P(None, "fsdp"),
        P("ckpt", "dp", "fsdp"),
    )
    out_specs = P("dp", ("fsdp", "ckpt"))
    per_device = make_per_device(mesh.shape["fsdp"], mesh.shape["ckpt"], mesh.shape["dp"])
    return jax.shard_map(
        per_device, mesh=mesh, in_specs=in_specs, out_specs=out_specs, check_vma=False
    )
```

time: 523 us -> 293 us (0.56)
  waiting for transfers between devices: 457 us -> 113 us
  matrix products: 42.2 us -> 96.7 us
  starting transfers between devices: 0.12 us -> 49.6 us
  local copies, waits for them, and re-layouts: 1.7 us -> 14.6 us
  blocking collectives: 8.6 us -> 0 us
    all_gather x3 -> x2, waiting for transfers between devices: 392 us -> 0.02 us  [the longest x1 0.02 us: per_device(): marks = lax.all_gather(marks, 'fsdp', axis=1, tiled=True)]
    ppermute x0 -> x36, waiting for transfers between devices: none -> 113 us  [the longest x6 77.4 us: shift_x(): return lax.ppermute(value, 'dp', x_pairs(shift % n_x))]
    unnamed x5 -> x2, waiting for transfers between devices: 64.8 us -> 0.03 us
    dot_general x4 -> x32, matrix products: 39 us -> 96.7 us  [the longest x26 95.7 us: dot(): return lax.dot_general(a, b, (dims, ((), ())), preferred_element_type=F32)]
    ppermute x0 -> x36, starting transfers between devices: none -> 49.5 us  [the longest x3 10.9 us: spread_square(): own_first = lax.ppermute(first, both, y_on_pairs)]
    dynamic_slice x0 -> x3, local copies, waits for them, and re-layouts: none -> 10.4 us  [the longest x1 6.7 us: per_device(): lax.dynamic_slice_in_dim(weight, (1 - core) * quarter, quarter, 1)]
    psum x1 -> x0, blocking collectives: 8.6 us -> none  [per_device(): right_sketch = lax.psum(right_part, 'fsdp')]
  transfers between devices with their start and end apart: 4 -> 38, of which waited for: 3 -> 16; matrix products, arithmetic and copies ran while one was open for 7% -> 36% of each run, Pallas kernels for 0% -> 0%
where the time goes in v1:
time: 293 us; the launch traced here: 292 us
  waiting for transfers between devices  113 us (39%)
  matrix products  96.7 us (33%)
  starting transfers between devices  49.6 us (17%)
  local copies, waits for them, and re-layouts  14.6 us (5%)
  between operations  14.1 us (5%)
  other arithmetic  4.19 us (1%)
    dot_general x26, matrix products, dot(): return lax.dot_general(a, b, (dims, ((), ())), preferred_element_type=F32)  95.7 us
    ppermute x6, waiting for transfers between devices, shift_x(): return lax.ppermute(value, 'dp', x_pairs(shift % n_x))  77.4 us
    ppermute x1, waiting for transfers between devices, per_device(): lax.ppermute(left_part, 'fsdp', [(0, 1), (1, 0)])  11.4 us
    ppermute x3, starting transfers between devices, spread_square(): own_first = lax.ppermute(first, both, y_on_pairs)  10.9 us
    ppermute x3, starting transfers between devices, spread_square(): passed = lax.ppermute(beside, both, on_pairs)  10.1 us
    ppermute x3, waiting for transfers between devices, spread_square(): beside = lax.ppermute(second, both, y_pairs)  7.91 us
    ppermute x3, waiting for transfers between devices, spread_square(): partner = lax.ppermute(got, both, y_pairs)  7.17 us
    ppermute x6, starting transfers between devices, shift_x(): return lax.ppermute(value, 'dp', x_pairs(shift % n_x))  7.09 us
  transfers between devices with their start and end apart: 38, of which 16 were waited for; matrix products, arithmetic and copies ran while one was open for 36% of the time, Pallas kernels for 0%

profile of v1, /device:TPU:0, one launch (start us, length us, event | category | flops | bytes accessed | tf_op | source)
XLA Modules:
  0.0 292.4 jit_solution(15412802142278626819)
XLA Ops:
  6.5 6.7 %dynamic-slice_bitcast_fusion = bf16[1024,3584]{1,0:T(8,128)(2,1)} fusion(bf16[1,1024,7168]{2,1,0:T(8,128)(2,1)} %param.7, s32[]{:T(128)S(6)} %select_n.167), kind=kLoop, calls=%fused_computation.18 | loop fusion | bytes 14680068 | tf_op jit(solution)/shard_map/dynamic_slice | solution.py:95
  13.8 0.9 fusion.206
  14.7 4.4 %collective-permute-start.1 = (bf16[128,1024]{1,0:T(8,128)(2,1)}, bf16[128,1024]{1,0:T(8,128)(2,1)S(1)}, u32[]{:S(2)}, u32[]{:S(2)}) collective-permute-start(bf16[128,1024]{1,0:T(8,128)(2,1)} %get-tuple-element.24), channel_id=1, source_target_pairs={{0,16},{1,17},{18,2},{19,3},{4,20},{5,21},{22,6},{23,7},{8,24},{9,... | collective-permute-start | bytes 786440 | tf_op jit(solution)/shard_map/ppermute | solution.py:58
  20.0 3.9 %collective-permute-start.5 = (bf16[128,1024]{1,0:T(8,128)(2,1)}, bf16[128,1024]{1,0:T(8,128)(2,1)S(1)}, u32[]{:S(2)}, u32[]{:S(2)}) collective-permute-start(bf16[128,1024]{1,0:T(8,128)(2,1)} %get-tuple-element.21), channel_id=1, source_target_pairs={{0,16},{1,17},{18,2},{19,3},{4,20},{5,21},{22,6},{23,7},{8,24},{9,... | collective-permute-start | bytes 786440 | tf_op jit(solution)/shard_map/ppermute | solution.py:58
  24.0 1.5 fusion.55
  26.4 11.4 %collective-permute-done = f32[384,32]{0,1:T(8,128)S(1)} collective-permute-done((f32[384,32]{0,1:T(8,128)S(1)}, f32[384,32]{0,1:T(8,128)S(1)}, u32[]{:S(2)}, u32[]{:S(2)}) %collective-permute-start) | collective-permute-done | bytes 49184 | tf_op jit(solution)/shard_map/ppermute | solution.py:108
  37.9 2.5 collective-permute-start.6
  40.3 2.6 collective-permute-start.8
  43.0 3.7 %dynamic-slice_bitcast_fusion.1 = bf16[384,3584]{1,0:T(8,128)(2,1)} fusion(bf16[1,384,7168]{2,1,0:T(8,128)(2,1)} %param.8, s32[]{:T(128)S(6)} %select_n.167), kind=kLoop, calls=%fused_computation.36 | loop fusion | bytes 5505028 | tf_op jit(solution)/shard_map/dynamic_slice | solution.py:99
  46.7 1.6 collective-permute-start.19
  48.3 1.3 collective-permute-start.15
  49.6 7.9 %collective-permute-done.9 = bf16[128,1024]{1,0:T(8,128)(2,1)} collective-permute-done((bf16[128,1024]{1,0:T(8,128)(2,1)}, bf16[128,1024]{1,0:T(8,128)(2,1)}, u32[]{:S(2)}, u32[]{:S(2)}) %collective-permute-start.9) | collective-permute-done | bytes 262176 | tf_op jit(solution)/shard_map/ppermute | solution.py:49
  57.5 4.4 %collective-permute-start.20 = (bf16[128,1024]{1,0:T(8,128)(2,1)}, bf16[128,1024]{1,0:T(8,128)(2,1)S(1)}, u32[]{:S(2)}, u32[]{:S(2)}) collective-permute-start(bf16[128,1024]{1,0:T(8,128)(2,1)} %collective-permute-done.9), channel_id=1, source_target_pairs={{0,2},{1,3},{18,16},{19,17},{4,6},{5,7},{22,20},{23,21},{8,10},{9,... | collective-permute-start | bytes 786440 | tf_op jit(solution)/shard_map/ppermute | solution.py:50
  61.8 1.3 collective-permute-start.16
  63.2 3.1 %maximum_select_fusion.2 = (bf16[128,2048]{1,0:T(8,128)(2,1)}, bf16[128,2048]{1,0:T(8,128)(2,1)}, bf16[128,2048]{1,0:T(8,128)(2,1)}) fusion(bf16[128,1024]{1,0:T(8,128)(2,1)} %collective-permute-done.9, bf16[128,1024]{1,0:T(8,128)(2,1)} %collective-permute-done.8, pred[]{:T(512)S(6)} %eq.5, bf16[1,384,2048]{2,1,0:T(8,128)(2,1)} %param.6, ...), kind=kLoop, calls=%fused_computation.72 | loop fusion | flops 3932160 | bytes 4718593 | tf_op jit(solution)/shard_map/jit(_where)/select_n | solution.py:59
  66.2 1.3 collective-permute-start.11
  67.5 1.4 collective-permute-done.20
  68.9 4.5 %collective-permute-start.12 = (bf16[128,1024]{1,0:T(8,128)(2,1)S(1)}, bf16[128,1024]{1,0:T(8,128)(2,1)S(1)}, u32[]{:S(2)}, u32[]{:S(2)}) collective-permute-start(bf16[128,1024]{1,0:T(8,128)(2,1)S(1)} %collective-permute-done.2), channel_id=1, source_target_pairs={{0,2},{1,3},{18,16},{19,17},{4,6},{5,7},{22,20},{23,21},{8,10},{9,... | collective-permute-start | bytes 786440 | tf_op jit(solution)/shard_map/ppermute | solution.py:50
  74.1 2.4 collective-permute-start.21
  76.6 1.3 collective-permute-done.12
  78.0 2.5 collective-permute-start.17
  80.5 3.2 %collective-permute-done.21 = bf16[128,1024]{1,0:T(8,128)(2,1)S(1)} collective-permute-done((bf16[128,1024]{1,0:T(8,128)(2,1)S(1)}, bf16[128,1024]{1,0:T(8,128)(2,1)S(1)}, u32[]{:S(2)}, u32[]{:S(2)}) %collective-permute-start.21) | collective-permute-done | bytes 262176 | tf_op jit(solution)/shard_map/ppermute | solution.py:52
  83.9 3.9 %collective-permute-done.17 = bf16[128,1024]{1,0:T(8,128)(2,1)S(1)} collective-permute-done((bf16[128,1024]{1,0:T(8,128)(2,1)S(1)}, bf16[128,1024]{1,0:T(8,128)(2,1)S(1)}, u32[]{:S(2)}, u32[]{:S(2)}) %collective-permute-start.17) | collective-permute-done | bytes 262176 | tf_op jit(solution)/shard_map/ppermute | solution.py:52
  88.7 5.7 %fusion.6 = f32[128,3584]{1,0:T(8,128)} fusion(bf16[1,1024,7168]{2,1,0:T(8,128)(2,1)} %param.7, s32[]{:T(128)S(6)} %select_n.160, pred[]{:T(512)S(6)} %eq.4, bf16[128,2048]{1,0:T(8,128)(2,1)S(1)} %maximum_select_fusion.5), kind=kOutput, calls=%fused_computation.6 | convolution fusion | flops 939655168 | bytes 9699333 | tf_op jit(solution)/shard_map/dot_general | solution.py:13
  94.3 5.6 %fusion.8 = f32[128,3584]{1,0:T(8,128)} fusion(bf16[1,1024,7168]{2,1,0:T(8,128)(2,1)} %param.7, s32[]{:T(128)S(6)} %select_n.160, pred[]{:T(512)S(6)} %eq.4, bf16[128,2048]{1,0:T(8,128)(2,1)S(1)} %maximum_select_fusion.4), kind=kOutput, calls=%fused_computation.8 | convolution fusion | flops 939655168 | bytes 9699333 | tf_op jit(solution)/shard_map/dot_general | solution.py:13
  100.9 2.3 fusion.10
  104.0 5.5 %fusion.70 = f32[256,3584]{1,0:T(8,128)S(1)} fusion(bf16[1024,3584]{1,0:T(8,128)(2,1)} %collective-permute-done.4, pred[]{:T(512)S(6)} %eq.4, bf16[128,2048]{1,0:T(8,128)(2,1)} %collective-permute-done.10, bf16[128,2048]{1,0:T(8,128)(2,1)} %get-tuple-element.13), kind=kOutput, calls=%fused_computation.76 | convolution fusion | flops 1881407488 | bytes 12058625 | tf_op jit(solution)/shard_map/dot_general | solution.py:13
  109.5 8.6 %fusion.24 = f32[256,3584]{1,0:T(8,128)} fusion(f32[256,3584]{1,0:T(8,128)S(1)} %fusion.70, pred[]{:T(512)S(6)} %eq.4, bf16[1,1024,7168]{2,1,0:T(8,128)(2,1)} %param.7, s32[]{:T(128)S(6)} %select_n.160, bf16[128,2048]{1,0:T(8,128)(2,1)} %collective-permute-done.10, bf16[128,2048]{1,0:T(8,128)(2,1)} %get-tuple-element.13), kind=kOutput, calls=%fused_computation.21 | convolution fusion | flops 1882324992 | bytes 15728645 | tf_op jit(solution)/shard_map/dot_general | solution.py:13
  118.6 6.2 %fusion.73 = f32[256,3584]{1,0:T(8,128)S(1)} fusion(bf16[1024,3584]{1,0:T(8,128)(2,1)} %collective-permute-done.4, pred[]{:T(512)S(6)} %eq.4, bf16[128,2048]{1,0:T(8,128)(2,1)} %collective-permute-done.7, bf16[128,2048]{1,0:T(8,128)(2,1)} %get-tuple-element.14), kind=kOutput, calls=%fused_computation.80 | convolution fusion | flops 1881407488 | bytes 12058625 | tf_op jit(solution)/shard_map/dot_general | solution.py:13
  124.9 3.4 %fusion.21 = f32[256,3584]{1,0:T(8,128)S(1)} fusion(f32[256,3584]{1,0:T(8,128)S(1)} %fusion.73, pred[]{:T(512)S(6)} %eq.4, bf16[1,1024,7168]{2,1,0:T(8,128)(2,1)S(1)} %bitcast.117, s32[]{:T(128)S(6)} %select_n.160, bf16[128,2048]{1,0:T(8,128)(2,1)} %collective-permute-done.7, bf16[128,2048]{1,0:T(8,128)(2,1)} %get-tuple-element.14), kind=kOutput, calls=%fused_computation.20 | convolution fusion | flops 1882324992 | bytes 15728645 | tf_op jit(solution)/shard_map/dot_general | solution.py:13
  128.6 6.3 %fusion.76 = f32[256,3584]{1,0:T(8,128)S(1)} fusion(bf16[1024,3584]{1,0:T(8,128)(2,1)} %collective-permute-done.4, pred[]{:T(512)S(6)} %eq.4, bf16[128,2048]{1,0:T(8,128)(2,1)S(1)} %collective-permute-done.3, bf16[128,2048]{1,0:T(8,128)(2,1)S(1)} %copy-done.9), kind=kOutput, calls=%fused_computation.84 | convolution fusion | flops 1881407488 | bytes 12058625 | tf_op jit(solution)/shard_map/dot_general | solution.py:13
  134.8 4.3 %fusion.18 = f32[256,3584]{1,0:T(8,128)} fusion(f32[256,3584]{1,0:T(8,128)S(1)} %fusion.76, pred[]{:T(512)S(6)} %eq.4, bf16[1,1024,7168]{2,1,0:T(8,128)(2,1)S(1)} %bitcast.117, s32[]{:T(128)S(6)} %select_n.160, bf16[128,2048]{1,0:T(8,128)(2,1)S(1)} %collective-permute-done.3, bf16[128,2048]{1,0:T(8,128)(2,1)S(1)} %copy-done.9), kind=kOutput, calls=%fused_computation.19 | convolution fusion | flops 1882324992 | bytes 15728645 | tf_op jit(solution)/shard_map/dot_general | solution.py:13
  139.1 4.2 %fusion.94 = f32[128,3584]{1,0:T(8,128)S(1)} fusion(bf16[1024,3584]{1,0:T(8,128)(2,1)} %collective-permute-done.4, pred[]{:T(512)S(6)} %eq.4, bf16[128,2048]{1,0:T(8,128)(2,1)S(1)} %collective-permute-done.29), kind=kOutput, calls=%fused_computation.103 | convolution fusion | flops 939655168 | bytes 9699329 | tf_op jit(solution)/shard_map/dot_general | solution.py:13
  143.3 1.3 fusion.36
  144.6 1.5 collective-permute-start.30
  146.1 4.2 %fusion.97 = f32[128,3584]{1,0:T(8,128)S(1)} fusion(bf16[1024,3584]{1,0:T(8,128)(2,1)} %collective-permute-done.4, pred[]{:T(512)S(6)} %eq.4, bf16[128,2048]{1,0:T(8,128)(2,1)S(1)} %collective-permute-done.27), kind=kOutput, calls=%fused_computation.106 | convolution fusion | flops 939655168 | bytes 9699329 | tf_op jit(solution)/shard_map/dot_general | solution.py:13
  150.3 1.3 fusion.39
  152.3 4.2 %fusion.100 = f32[128,3584]{1,0:T(8,128)S(1)} fusion(bf16[1024,3584]{1,0:T(8,128)(2,1)} %collective-permute-done.4, pred[]{:T(512)S(6)} %eq.4, bf16[128,2048]{1,0:T(8,128)(2,1)S(1)} %collective-permute-done.25), kind=kOutput, calls=%fused_computation.109 | convolution fusion | flops 939655168 | bytes 9699329 | tf_op jit(solution)/shard_map/dot_general | solution.py:13
  156.5 1.3 fusion.42
  157.8 1.5 collective-permute-start.26
  159.3 4.3 %fusion.47 = bf16[128,3584]{1,0:T(8,128)(2,1)S(1)} fusion(f32[128,3584]{1,0:T(8,128)S(1)} %copy-done.3, bf16[1024,3584]{1,0:T(8,128)(2,1)} %collective-permute-done.4, pred[]{:T(512)S(6)} %eq.4, bf16[128,2048]{1,0:T(8,128)(2,1)S(1)} %maximum_select_fusion.5), kind=kOutput, calls=%fused_computation.33 | convolution fusion | flops 940572672 | bytes 10616833 | tf_op jit(solution)/shard_map/dot_general | solution.py:13
  163.7 4.5 %fusion.46 = bf16[128,3584]{1,0:T(8,128)(2,1)S(1)} fusion(f32[128,3584]{1,0:T(8,128)S(1)} %copy-done.2, bf16[1024,3584]{1,0:T(8,128)(2,1)} %collective-permute-done.4, pred[]{:T(512)S(6)} %eq.4, bf16[128,2048]{1,0:T(8,128)(2,1)S(1)} %copy-done.6), kind=kOutput, calls=%fused_computation.32 | convolution fusion | flops 940572672 | bytes 10616833 | tf_op jit(solution)/shard_map/dot_general | solution.py:13
  168.1 4.5 %fusion.45 = bf16[128,3584]{1,0:T(8,128)(2,1)S(1)} fusion(f32[128,3584]{1,0:T(8,128)S(1)} %copy-done.4, bf16[1024,3584]{1,0:T(8,128)(2,1)} %collective-permute-done.4, pred[]{:T(512)S(6)} %eq.4, bf16[128,2048]{1,0:T(8,128)(2,1)S(1)} %copy-done.8), kind=kOutput, calls=%fused_computation.31 | convolution fusion | flops 940572672 | bytes 10616833 | tf_op jit(solution)/shard_map/dot_general | solution.py:13
  173.4 1.4 collective-permute-start.18
  174.8 1.9 fusion.60
  176.7 10.9 %collective-permute-done.28 = bf16[128,3584]{1,0:T(8,128)(2,1)S(1)} collective-permute-done((bf16[128,3584]{1,0:T(8,128)(2,1)S(1)}, bf16[128,3584]{1,0:T(8,128)(2,1)S(1)}, u32[]{:S(2)}, u32[]{:S(2)}) %collective-permute-start.28) | collective-permute-done | bytes 917536 | tf_op jit(solution)/shard_map/ppermute | solution.py:27
  187.5 1.4 collective-permute-start.14
  188.9 2.2 fusion.59
  191.3 15.9 %collective-permute-done.26 = bf16[128,3584]{1,0:T(8,128)(2,1)S(1)} collective-permute-done((bf16[128,3584]{1,0:T(8,128)(2,1)S(1)}, bf16[128,3584]{1,0:T(8,128)(2,1)S(1)}, u32[]{:S(2)}, u32[]{:S(2)}) %collective-permute-start.26) | collective-permute-done | bytes 917536 | tf_op jit(solution)/shard_map/ppermute | solution.py:27
  207.2 1.9 fusion.58
  209.3 17.6 %collective-permute-done.22 = bf16[128,3584]{1,0:T(8,128)(2,1)S(1)} collective-permute-done((bf16[128,3584]{1,0:T(8,128)(2,1)S(1)}, bf16[128,3584]{1,0:T(8,128)(2,1)S(1)}, u32[]{:S(2)}, u32[]{:S(2)}) %collective-permute-start.22) | collective-permute-done | bytes 917536 | tf_op jit(solution)/shard_map/ppermute | solution.py:27
  226.9 1.9 fusion.65
  229.4 17.2 %collective-permute-done.18 = bf16[128,3584]{1,0:T(8,128)(2,1)} collective-permute-done((bf16[128,3584]{1,0:T(8,128)(2,1)S(1)}, bf16[128,3584]{1,0:T(8,128)(2,1)}, u32[]{:S(2)}, u32[]{:S(2)}) %collective-permute-start.18) | collective-permute-done | bytes 917536 | tf_op jit(solution)/shard_map/ppermute | solution.py:27
  246.6 2.7 fusion.63
  249.6 15.8 %collective-permute-done.14 = bf16[128,3584]{1,0:T(8,128)(2,1)} collective-permute-done((bf16[128,3584]{1,0:T(8,128)(2,1)S(1)}, bf16[128,3584]{1,0:T(8,128)(2,1)}, u32[]{:S(2)}, u32[]{:S(2)}) %collective-permute-start.14) | collective-permute-done | bytes 917536 | tf_op jit(solution)/shard_map/ppermute | solution.py:27
  265.4 2.7 fusion.61
  268.5 3.4 %fusion.48 = f32[12,2048]{1,0:T(8,128)S(1)} fusion(bf16[1,2048,1024]{2,1,0:T(8,128)(2,1)} %all-gather.7.cloned.1.call-done, bf16[6,1024]{1,0:T(8,128)(2,1)S(1)} %get-tuple-element.11, bf16[6,1024]{1,0:T(8,128)(2,1)S(1)} %get-tuple-element.12), kind=kOutput, calls=%fused_computation.34 | convolution fusion | flops 50380800 | bytes 4317184 | tf_op jit(solution)/shard_map/dot_general | solution.py:13
  272.0 1.2 collective-permute-done.31
  273.3 1.4 collective-permute-start.32
  274.7 2.4 collective-permute-done.32
  277.1 1.6 collective-permute-start.33
  278.8 2.6 collective-permute-start.34
  281.3 1.4 collective-permute-start.35
  283.3 1.7 collective-permute-done.35
  (121 shorter events, 11.0 us)
Async XLA Ops:
  6.5 168.2 %copy-start = (bf16[32,7168]{1,0:T(8,128)(2,1)S(1)}, bf16[32,7168]{1,0:T(8,128)(2,1)}, u32[]{:S(2)}) copy-start(bf16[32,7168]{1,0:T(8,128)(2,1)} %param.10) | copy-start | bytes 1376260
  6.5 96.7 %all-gather.5.cloned.1.call-start = ((), (), s32[]{:S(2)}) async-start(), calls=%async_computation | async-start | bytes 2621440 | tf_op jit(solution)/shard_map/all_gather | solution.py:102
  6.5 7.2 %copy-start.1 = (bf16[1,384,2048]{2,1,0:T(8,128)(2,1)S(1)}, bf16[1,384,2048]{2,1,0:T(8,128)(2,1)}, u32[]{:S(2)}) copy-start(bf16[1,384,2048]{2,1,0:T(8,128)(2,1)} %param.6) | copy-start | bytes 4718596
  13.2 90.7 %collective-permute-start.4 = (bf16[1024,3584]{1,0:T(8,128)(2,1)}, bf16[1024,3584]{1,0:T(8,128)(2,1)}, u32[]{:S(2)}, u32[]{:S(2)}) collective-permute-start(bf16[1024,3584]{1,0:T(8,128)(2,1)} %dynamic-slice_bitcast_fusion), channel_id=1, source_target_pairs={{0,1},{1,0},{2,3},{3,2},{4,5},{5,4},{6,7},{7,6},{8,9},{9,8},{10,11... | collective-permute-start | bytes 22020104 | tf_op jit(solution)/shard_map/ppermute | solution.py:24
  14.7 25.6 %collective-permute-start.1 = (bf16[128,1024]{1,0:T(8,128)(2,1)}, bf16[128,1024]{1,0:T(8,128)(2,1)S(1)}, u32[]{:S(2)}, u32[]{:S(2)}) collective-permute-start(bf16[128,1024]{1,0:T(8,128)(2,1)} %get-tuple-element.24), channel_id=1, source_target_pairs={{0,16},{1,17},{18,2},{19,3},{4,20},{5,21},{22,6},{23,7},{8,24},{9,... | collective-permute-start | bytes 786440 | tf_op jit(solution)/shard_map/ppermute | solution.py:58
  19.1 23.8 %collective-permute-start.2 = (bf16[128,1024]{1,0:T(8,128)(2,1)}, bf16[128,1024]{1,0:T(8,128)(2,1)S(1)}, u32[]{:S(2)}, u32[]{:S(2)}) collective-permute-start(bf16[128,1024]{1,0:T(8,128)(2,1)} %get-tuple-element.23), channel_id=1, source_target_pairs={{0,16},{1,17},{2,18},{3,19},{16,0},{17,1},{18,2},{19,3},{4,20},{5,... | collective-permute-start | bytes 786440 | tf_op jit(solution)/shard_map/ppermute | solution.py:49
  20.0 26.6 %collective-permute-start.5 = (bf16[128,1024]{1,0:T(8,128)(2,1)}, bf16[128,1024]{1,0:T(8,128)(2,1)S(1)}, u32[]{:S(2)}, u32[]{:S(2)}) collective-permute-start(bf16[128,1024]{1,0:T(8,128)(2,1)} %get-tuple-element.21), channel_id=1, source_target_pairs={{0,16},{1,17},{18,2},{19,3},{4,20},{5,21},{22,6},{23,7},{8,24},{9,... | collective-permute-start | bytes 786440 | tf_op jit(solution)/shard_map/ppermute | solution.py:58
  25.4 12.4 %collective-permute-start = (f32[384,32]{0,1:T(8,128)S(1)}, f32[384,32]{0,1:T(8,128)S(1)}, u32[]{:S(2)}, u32[]{:S(2)}) collective-permute-start(f32[384,32]{0,1:T(8,128)S(1)} %fusion.55), channel_id=1, source_target_pairs={{0,16},{16,0},{1,17},{17,1},{2,18},{18,2},{3,19},{19,3},{4,20},{20... | collective-permute-start | bytes 147464 | tf_op jit(solution)/shard_map/ppermute | solution.py:108
  25.5 242.9 %all-gather.7.cloned.1.call-start = ((), (), s32[]{:S(2)}) async-start(), calls=%async_computation.1 | async-start | bytes 6291456 | tf_op jit(solution)/shard_map/all_gather | solution.py:103
  37.9 10.4 %collective-permute-start.6 = (bf16[128,1024]{1,0:T(8,128)(2,1)}, bf16[128,1024]{1,0:T(8,128)(2,1)}, u32[]{:S(2)}, u32[]{:S(2)}) collective-permute-start(bf16[128,1024]{1,0:T(8,128)(2,1)} %get-tuple-element.22), channel_id=1, source_target_pairs={{0,16},{1,17},{2,18},{3,19},{16,0},{17,1},{18,2},{19,3},{4,20},{5,... | collective-permute-start | bytes 786440 | tf_op jit(solution)/shard_map/ppermute | solution.py:49
  40.3 21.5 %collective-permute-start.8 = (bf16[128,1024]{1,0:T(8,128)(2,1)}, bf16[128,1024]{1,0:T(8,128)(2,1)}, u32[]{:S(2)}, u32[]{:S(2)}) collective-permute-start(bf16[128,1024]{1,0:T(8,128)(2,1)} %get-tuple-element.19), channel_id=1, source_target_pairs={{0,16},{1,17},{18,2},{19,3},{4,20},{5,21},{22,6},{23,7},{8,24},{9,... | collective-permute-start | bytes 786440 | tf_op jit(solution)/shard_map/ppermute | solution.py:58
  42.9 14.5 %collective-permute-start.9 = (bf16[128,1024]{1,0:T(8,128)(2,1)}, bf16[128,1024]{1,0:T(8,128)(2,1)}, u32[]{:S(2)}, u32[]{:S(2)}) collective-permute-start(bf16[128,1024]{1,0:T(8,128)(2,1)} %get-tuple-element.20), channel_id=1, source_target_pairs={{0,16},{1,17},{2,18},{3,19},{16,0},{17,1},{18,2},{19,3},{4,20},{5,... | collective-permute-start | bytes 786440 | tf_op jit(solution)/shard_map/ppermute | solution.py:49
  43.0 57.9 %slice-start = ((s8[14680064]{0:T(1024)(128)(4,1)}), s8[2097152]{0:T(1024)(128)(4,1)S(1)}, s32[]{:S(2)}) async-start(s8[14680064]{0:T(1024)(128)(4,1)} %bitcast.114), calls=%async_computation.2 | async-start | bytes 4194304
  46.7 54.2 %slice-start.1 = ((s8[14680064]{0:T(1024)(128)(4,1)}), s8[4194304]{0:T(1024)(128)(4,1)S(1)}, s32[]{:S(2)}) async-start(s8[14680064]{0:T(1024)(128)(4,1)} %bitcast.114), calls=%async_computation.3 | async-start | bytes 8388608
  46.7 19.5 %collective-permute-start.19 = (bf16[128,1024]{1,0:T(8,128)(2,1)}, bf16[128,1024]{1,0:T(8,128)(2,1)S(1)}, u32[]{:S(2)}, u32[]{:S(2)}) collective-permute-start(bf16[128,1024]{1,0:T(8,128)(2,1)} %get-tuple-element.19), channel_id=1, source_target_pairs={{2,0},{3,1},{16,18},{17,19},{6,4},{7,5},{20,22},{21,23},{10,8},{11... | collective-permute-start | bytes 786440 | tf_op jit(solution)/shard_map/ppermute | solution.py:48
  48.3 25.1 %collective-permute-start.15 = (bf16[128,1024]{1,0:T(8,128)(2,1)}, bf16[128,1024]{1,0:T(8,128)(2,1)S(1)}, u32[]{:S(2)}, u32[]{:S(2)}) collective-permute-start(bf16[128,1024]{1,0:T(8,128)(2,1)} %get-tuple-element.21), channel_id=1, source_target_pairs={{2,0},{3,1},{16,18},{17,19},{6,4},{7,5},{20,22},{21,23},{10,8},{11... | collective-permute-start | bytes 786440 | tf_op jit(solution)/shard_map/ppermute | solution.py:48
  57.5 11.4 %collective-permute-start.20 = (bf16[128,1024]{1,0:T(8,128)(2,1)}, bf16[128,1024]{1,0:T(8,128)(2,1)S(1)}, u32[]{:S(2)}, u32[]{:S(2)}) collective-permute-start(bf16[128,1024]{1,0:T(8,128)(2,1)} %collective-permute-done.9), channel_id=1, source_target_pairs={{0,2},{1,3},{18,16},{19,17},{4,6},{5,7},{22,20},{23,21},{8,10},{9,... | collective-permute-start | bytes 786440 | tf_op jit(solution)/shard_map/ppermute | solution.py:50
  61.8 12.3 %collective-permute-start.16 = (bf16[128,1024]{1,0:T(8,128)(2,1)}, bf16[128,1024]{1,0:T(8,128)(2,1)S(1)}, u32[]{:S(2)}, u32[]{:S(2)}) collective-permute-start(bf16[128,1024]{1,0:T(8,128)(2,1)} %collective-permute-done.6), channel_id=1, source_target_pairs={{0,2},{1,3},{18,16},{19,17},{4,6},{5,7},{22,20},{23,21},{8,10},{9,... | collective-permute-start | bytes 786440 | tf_op jit(solution)/shard_map/ppermute | solution.py:50
  66.2 10.3 %collective-permute-start.11 = (bf16[128,1024]{1,0:T(8,128)(2,1)}, bf16[128,1024]{1,0:T(8,128)(2,1)S(1)}, u32[]{:S(2)}, u32[]{:S(2)}) collective-permute-start(bf16[128,1024]{1,0:T(8,128)(2,1)} %get-tuple-element.24), channel_id=1, source_target_pairs={{2,0},{3,1},{16,18},{17,19},{6,4},{7,5},{20,22},{21,23},{10,8},{11... | collective-permute-start | bytes 786440 | tf_op jit(solution)/shard_map/ppermute | solution.py:48
  68.9 9.1 %collective-permute-start.12 = (bf16[128,1024]{1,0:T(8,128)(2,1)S(1)}, bf16[128,1024]{1,0:T(8,128)(2,1)S(1)}, u32[]{:S(2)}, u32[]{:S(2)}) collective-permute-start(bf16[128,1024]{1,0:T(8,128)(2,1)S(1)} %collective-permute-done.2), channel_id=1, source_target_pairs={{0,2},{1,3},{18,16},{19,17},{4,6},{5,7},{22,20},{23,21},{8,10},{9,... | collective-permute-start | bytes 786440 | tf_op jit(solution)/shard_map/ppermute | solution.py:50
  73.4 99.2 %collective-permute-start.24 = (bf16[384,3584]{1,0:T(8,128)(2,1)}, bf16[384,3584]{1,0:T(8,128)(2,1)}, u32[]{:S(2)}, u32[]{:S(2)}) collective-permute-start(bf16[384,3584]{1,0:T(8,128)(2,1)} %dynamic-slice_bitcast_fusion.1), channel_id=1, source_target_pairs={{0,1},{1,0},{2,3},{3,2},{4,5},{5,4},{6,7},{7,6},{8,9},{9,8},{10,11... | collective-permute-start | bytes 8257544 | tf_op jit(solution)/shard_map/ppermute | solution.py:24
  74.1 9.6 %collective-permute-start.21 = (bf16[128,1024]{1,0:T(8,128)(2,1)S(1)}, bf16[128,1024]{1,0:T(8,128)(2,1)S(1)}, u32[]{:S(2)}, u32[]{:S(2)}) collective-permute-start(bf16[128,1024]{1,0:T(8,128)(2,1)S(1)} %broadcast_select_fusion), channel_id=1, source_target_pairs={{0,16},{1,17},{2,18},{3,19},{16,0},{17,1},{18,2},{19,3},{4,20},{5,... | collective-permute-start | bytes 786440 | tf_op jit(solution)/shard_map/ppermute | solution.py:52
  76.6 114.5 %collective-permute-start.23 = (f32[384,32]{0,1:T(8,128)S(1)}, f32[384,32]{0,1:T(8,128)S(1)}, u32[]{:S(2)}, u32[]{:S(2)}) collective-permute-start(f32[384,32]{0,1:T(8,128)S(1)} %add.131), channel_id=1, source_target_pairs={{0,1},{1,0},{2,3},{3,2},{4,5},{5,4},{6,7},{7,6},{8,9},{9,8},{10,11... | collective-permute-start | bytes 147464 | tf_op jit(solution)/shard_map/ppermute | solution.py:24
  78.0 9.9 %collective-permute-start.17 = (bf16[128,1024]{1,0:T(8,128)(2,1)S(1)}, bf16[128,1024]{1,0:T(8,128)(2,1)S(1)}, u32[]{:S(2)}, u32[]{:S(2)}) collective-permute-start(bf16[128,1024]{1,0:T(8,128)(2,1)S(1)} %broadcast_select_fusion.1), channel_id=1, source_target_pairs={{0,16},{1,17},{2,18},{3,19},{16,0},{17,1},{18,2},{19,3},{4,20},{5,... | collective-permute-start | bytes 786440 | tf_op jit(solution)/shard_map/ppermute | solution.py:52
  83.7 19.6 %collective-permute-start.10 = (bf16[128,2048]{1,0:T(8,128)(2,1)}, bf16[128,2048]{1,0:T(8,128)(2,1)}, u32[]{:S(2)}, u32[]{:S(2)}) collective-permute-start(bf16[128,2048]{1,0:T(8,128)(2,1)} %get-tuple-element.13), channel_id=1, source_target_pairs={{0,1},{1,0},{2,3},{3,2},{4,5},{5,4},{6,7},{7,6},{8,9},{9,8},{10,11... | collective-permute-start | bytes 1572872 | tf_op jit(solution)/shard_map/ppermute | solution.py:24
  87.8 12.1 %collective-permute-start.13 = (bf16[128,1024]{1,0:T(8,128)(2,1)S(1)}, bf16[128,1024]{1,0:T(8,128)(2,1)S(1)}, u32[]{:S(2)}, u32[]{:S(2)}) collective-permute-start(bf16[128,1024]{1,0:T(8,128)(2,1)S(1)} %broadcast_select_fusion.2), channel_id=1, source_target_pairs={{0,16},{1,17},{2,18},{3,19},{16,0},{17,1},{18,2},{19,3},{4,20},{5,... | collective-permute-start | bytes 786440 | tf_op jit(solution)/shard_map/ppermute | solution.py:52
  88.6 5.7 %copy-start.5 = (bf16[128,2048]{1,0:T(8,128)(2,1)}, bf16[128,2048]{1,0:T(8,128)(2,1)S(1)}, u32[]{:S(2)}) copy-start(bf16[128,2048]{1,0:T(8,128)(2,1)S(1)} %maximum_select_fusion.4) | copy-start | bytes 1572868
  88.6 12.2 %slice-start.2 = ((s8[14680064]{0:T(1024)(128)(4,1)}), s8[4194304]{0:T(1024)(128)(4,1)S(1)}, s32[]{:S(2)}) async-start(s8[14680064]{0:T(1024)(128)(4,1)} %bitcast.114), calls=%async_computation.4 | async-start | bytes 8388608
  94.3 6.6 %slice-start.3 = ((s8[14680064]{0:T(1024)(128)(4,1)}), s8[4194304]{0:T(1024)(128)(4,1)S(1)}, s32[]{:S(2)}) async-start(s8[14680064]{0:T(1024)(128)(4,1)} %bitcast.114), calls=%async_computation.5 | async-start | bytes 8388608
  99.9 18.2 %collective-permute-start.7 = (bf16[128,2048]{1,0:T(8,128)(2,1)}, bf16[128,2048]{1,0:T(8,128)(2,1)}, u32[]{:S(2)}, u32[]{:S(2)}) collective-permute-start(bf16[128,2048]{1,0:T(8,128)(2,1)} %get-tuple-element.14), channel_id=1, source_target_pairs={{0,1},{1,0},{2,3},{3,2},{4,5},{5,4},{6,7},{7,6},{8,9},{9,8},{10,11... | collective-permute-start | bytes 1572872 | tf_op jit(solution)/shard_map/ppermute | solution.py:24
  100.1 0.8 copy-start.7
  103.3 25.1 %collective-permute-start.3 = (bf16[128,2048]{1,0:T(8,128)(2,1)}, bf16[128,2048]{1,0:T(8,128)(2,1)S(1)}, u32[]{:S(2)}, u32[]{:S(2)}) collective-permute-start(bf16[128,2048]{1,0:T(8,128)(2,1)} %get-tuple-element.15), channel_id=1, source_target_pairs={{0,1},{1,0},{2,3},{3,2},{4,5},{5,4},{6,7},{7,6},{8,9},{9,8},{10,11... | collective-permute-start | bytes 1572872 | tf_op jit(solution)/shard_map/ppermute | solution.py:24
  103.9 35.2 %collective-permute-start.29 = (bf16[128,2048]{1,0:T(8,128)(2,1)S(1)}, bf16[128,2048]{1,0:T(8,128)(2,1)S(1)}, u32[]{:S(2)}, u32[]{:S(2)}) collective-permute-start(bf16[128,2048]{1,0:T(8,128)(2,1)S(1)} %maximum_select_fusion.5), channel_id=1, source_target_pairs={{0,1},{1,0},{2,3},{3,2},{4,5},{5,4},{6,7},{7,6},{8,9},{9,8},{10,11... | collective-permute-start | bytes 1572872 | tf_op jit(solution)/shard_map/ppermute | solution.py:24
  109.5 8.6 %copy-start.6 = (bf16[128,2048]{1,0:T(8,128)(2,1)S(1)}, bf16[128,2048]{1,0:T(8,128)(2,1)}, u32[]{:S(2)}) copy-start(bf16[128,2048]{1,0:T(8,128)(2,1)} %copy-done.5) | copy-start | bytes 1572868
  109.5 15.3 %slice-start.4 = ((s8[14680064]{0:T(1024)(128)(4,1)}), s8[4194304]{0:T(1024)(128)(4,1)S(1)}, s32[]{:S(2)}) async-start(s8[14680064]{0:T(1024)(128)(4,1)} %bitcast.116), calls=%async_computation.6 | async-start | bytes 8388608
  109.5 15.3 %slice-start.5 = ((s8[14680064]{0:T(1024)(128)(4,1)}), s8[4194304]{0:T(1024)(128)(4,1)S(1)}, s32[]{:S(2)}) async-start(s8[14680064]{0:T(1024)(128)(4,1)} %bitcast.116), calls=%async_computation.7 | async-start | bytes 8388608
  109.5 15.3 %slice-start.6 = ((s8[14680064]{0:T(1024)(128)(4,1)}), s8[4194304]{0:T(1024)(128)(4,1)S(1)}, s32[]{:S(2)}) async-start(s8[14680064]{0:T(1024)(128)(4,1)} %bitcast.116), calls=%async_computation.8 | async-start | bytes 8388608
  118.1 6.7 %slice-start.7 = ((s8[14680064]{0:T(1024)(128)(4,1)}), s8[2097152]{0:T(1024)(128)(4,1)S(1)}, s32[]{:S(2)}) async-start(s8[14680064]{0:T(1024)(128)(4,1)} %bitcast.116), calls=%async_computation.9 | async-start | bytes 4194304
  118.1 27.9 %collective-permute-start.27 = (bf16[128,2048]{1,0:T(8,128)(2,1)S(1)}, bf16[128,2048]{1,0:T(8,128)(2,1)S(1)}, u32[]{:S(2)}, u32[]{:S(2)}) collective-permute-start(bf16[128,2048]{1,0:T(8,128)(2,1)S(1)} %copy-done.6), channel_id=1, source_target_pairs={{0,1},{1,0},{2,3},{3,2},{4,5},{5,4},{6,7},{7,6},{8,9},{9,8},{10,11... | collective-permute-start | bytes 1572872 | tf_op jit(solution)/shard_map/ppermute | solution.py:24
  124.9 3.5 %copy-start.8 = (bf16[128,2048]{1,0:T(8,128)(2,1)S(1)}, bf16[128,2048]{1,0:T(8,128)(2,1)}, u32[]{:S(2)}) copy-start(bf16[128,2048]{1,0:T(8,128)(2,1)} %copy-done.7) | copy-start | bytes 1572868
  124.9 3.7 %copy-start.9 = (bf16[128,2048]{1,0:T(8,128)(2,1)S(1)}, bf16[128,2048]{1,0:T(8,128)(2,1)}, u32[]{:S(2)}) copy-start(bf16[128,2048]{1,0:T(8,128)(2,1)} %get-tuple-element.15) | copy-start | bytes 1572868
  128.3 60.6 %copy-start.10 = (f32[256,3584]{1,0:T(8,128)}, f32[256,3584]{1,0:T(8,128)S(1)}, u32[]{:S(2)}) copy-start(f32[256,3584]{1,0:T(8,128)S(1)} %fusion.21) | copy-start | bytes 11010052
  128.4 23.9 %collective-permute-start.25 = (bf16[128,2048]{1,0:T(8,128)(2,1)S(1)}, bf16[128,2048]{1,0:T(8,128)(2,1)S(1)}, u32[]{:S(2)}, u32[]{:S(2)}) collective-permute-start(bf16[128,2048]{1,0:T(8,128)(2,1)S(1)} %copy-done.8), channel_id=1, source_target_pairs={{0,1},{1,0},{2,3},{3,2},{4,5},{5,4},{6,7},{7,6},{8,9},{9,8},{10,11... | collective-permute-start | bytes 1572872 | tf_op jit(solution)/shard_map/ppermute | solution.py:24
  144.6 28.8 %collective-permute-start.30 = (bf16[128,3584]{1,0:T(8,128)(2,1)S(1)}, bf16[128,3584]{1,0:T(8,128)(2,1)S(1)}, u32[]{:S(2)}, u32[]{:S(2)}) collective-permute-start(bf16[128,3584]{1,0:T(8,128)(2,1)S(1)} %fusion.36), channel_id=1, source_target_pairs={{0,2},{1,3},{2,0},{3,1},{4,6},{5,7},{6,4},{7,5},{8,10},{9,11},{10,... | collective-permute-start | bytes 2752520 | tf_op jit(solution)/shard_map/ppermute | solution.py:27
  151.6 35.9 %collective-permute-start.28 = (bf16[128,3584]{1,0:T(8,128)(2,1)S(1)}, bf16[128,3584]{1,0:T(8,128)(2,1)S(1)}, u32[]{:S(2)}, u32[]{:S(2)}) collective-permute-start(bf16[128,3584]{1,0:T(8,128)(2,1)S(1)} %fusion.39), channel_id=1, source_target_pairs={{0,2},{1,3},{2,0},{3,1},{4,6},{5,7},{6,4},{7,5},{8,10},{9,11},{10,... | collective-permute-start | bytes 2752520 | tf_op jit(solution)/shard_map/ppermute | solution.py:27
  156.5 2.8 copy-start.3
  157.8 5.8 %copy-start.2 = (f32[128,3584]{1,0:T(8,128)S(1)}, f32[128,3584]{1,0:T(8,128)}, u32[]{:S(2)}) copy-start(f32[128,3584]{1,0:T(8,128)} %fusion.8) | copy-start | bytes 5505028
  157.8 49.4 %collective-permute-start.26 = (bf16[128,3584]{1,0:T(8,128)(2,1)S(1)}, bf16[128,3584]{1,0:T(8,128)(2,1)S(1)}, u32[]{:S(2)}, u32[]{:S(2)}) collective-permute-start(bf16[128,3584]{1,0:T(8,128)(2,1)S(1)} %fusion.42), channel_id=1, source_target_pairs={{0,2},{1,3},{2,0},{3,1},{4,6},{5,7},{6,4},{7,5},{8,10},{9,11},{10,... | collective-permute-start | bytes 2752520 | tf_op jit(solution)/shard_map/ppermute | solution.py:27
  163.6 4.5 %copy-start.4 = (f32[128,3584]{1,0:T(8,128)S(1)}, f32[128,3584]{1,0:T(8,128)}, u32[]{:S(2)}) copy-start(f32[128,3584]{1,0:T(8,128)} %fusion.10) | copy-start | bytes 5505028
  168.1 6.6 %copy-start.11 = (f32[256,3584]{1,0:T(8,128)S(1)}, f32[256,3584]{1,0:T(8,128)}, u32[]{:S(2)}) copy-start(f32[256,3584]{1,0:T(8,128)} %fusion.24) | copy-start | bytes 11010052
  172.7 54.2 %collective-permute-start.22 = (bf16[128,3584]{1,0:T(8,128)(2,1)S(1)}, bf16[128,3584]{1,0:T(8,128)(2,1)S(1)}, u32[]{:S(2)}, u32[]{:S(2)}) collective-permute-start(bf16[128,3584]{1,0:T(8,128)(2,1)S(1)} %fusion.47), channel_id=1, source_target_pairs={{0,2},{1,3},{2,0},{3,1},{4,6},{5,7},{6,4},{7,5},{8,10},{9,11},{10,... | collective-permute-start | bytes 2752520 | tf_op jit(solution)/shard_map/ppermute | solution.py:27
  173.4 73.3 %collective-permute-start.18 = (bf16[128,3584]{1,0:T(8,128)(2,1)S(1)}, bf16[128,3584]{1,0:T(8,128)(2,1)}, u32[]{:S(2)}, u32[]{:S(2)}) collective-permute-start(bf16[128,3584]{1,0:T(8,128)(2,1)S(1)} %fusion.46), channel_id=1, source_target_pairs={{0,2},{1,3},{2,0},{3,1},{4,6},{5,7},{6,4},{7,5},{8,10},{9,11},{10,... | collective-permute-start | bytes 2752520 | tf_op jit(solution)/shard_map/ppermute | solution.py:27
  176.7 30.5 %copy-start.12 = (f32[256,3584]{1,0:T(8,128)S(1)}, f32[256,3584]{1,0:T(8,128)}, u32[]{:S(2)}) copy-start(f32[256,3584]{1,0:T(8,128)} %fusion.18) | copy-start | bytes 11010052
  187.5 77.9 %collective-permute-start.14 = (bf16[128,3584]{1,0:T(8,128)(2,1)S(1)}, bf16[128,3584]{1,0:T(8,128)(2,1)}, u32[]{:S(2)}, u32[]{:S(2)}) collective-permute-start(bf16[128,3584]{1,0:T(8,128)(2,1)S(1)} %fusion.45), channel_id=1, source_target_pairs={{0,2},{1,3},{2,0},{3,1},{4,6},{5,7},{6,4},{7,5},{8,10},{9,11},{10,... | collective-permute-start | bytes 2752520 | tf_op jit(solution)/shard_map/ppermute | solution.py:27
  271.9 1.3 collective-permute-start.31
  273.3 3.8 %collective-permute-start.32 = (f32[3,1024]{1,0:T(4,128)S(1)}, f32[3,1024]{1,0:T(4,128)S(1)}, u32[]{:S(2)}, u32[]{:S(2)}) collective-permute-start(f32[3,1024]{1,0:T(4,128)S(1)} %bitcast.120), channel_id=1, source_target_pairs={{0,16},{16,0},{1,17},{17,1},{2,18},{18,2},{3,19},{19,3},{4,20},{20... | collective-permute-start | bytes 36872 | tf_op jit(solution)/shard_map/ppermute | solution.py:76
  277.1 5.6 %collective-permute-start.33 = (f32[3,256]{1,0:T(4,128)S(1)}, f32[3,256]{1,0:T(4,128)S(1)}, u32[]{:S(2)}, u32[]{:S(2)}) collective-permute-start(f32[3,256]{1,0:T(4,128)S(1)} %get-tuple-element.27), channel_id=1, source_target_pairs={{0,4},{4,8},{8,12},{12,0},{1,5},{5,9},{9,13},{13,1},{2,6},{6,10},{... | collective-permute-start | bytes 9224 | tf_op jit(solution)/shard_map/ppermute | solution.py:76
  278.8 4.5 %collective-permute-start.34 = (f32[3,256]{1,0:T(4,128)S(1)}, f32[3,256]{1,0:T(4,128)S(1)}, u32[]{:S(2)}, u32[]{:S(2)}) collective-permute-start(f32[3,256]{1,0:T(4,128)S(1)} %get-tuple-element.29), channel_id=1, source_target_pairs={{0,8},{4,12},{8,0},{12,4},{1,9},{5,13},{9,1},{13,5},{2,10},{6,14},... | collective-permute-start | bytes 9224 | tf_op jit(solution)/shard_map/ppermute | solution.py:76
  281.3 3.6 %collective-permute-start.35 = (f32[3,256]{1,0:T(4,128)S(1)}, f32[3,256]{1,0:T(4,128)S(1)}, u32[]{:S(2)}, u32[]{:S(2)}) collective-permute-start(f32[3,256]{1,0:T(4,128)S(1)} %get-tuple-element.28), channel_id=1, source_target_pairs={{0,12},{4,0},{8,4},{12,8},{1,13},{5,1},{9,5},{13,9},{2,14},{6,2},{... | collective-permute-start | bytes 9224 | tf_op jit(solution)/shard_map/ppermute | solution.py:76
Sparse Core Ops, SparseCore 0:
  25.7 23.3 all-gather.4
  103.4 57.1 all-gather.6

commit v2 on v0

v2 whole, which is shorter than its diff:
```python
import jax
import jax.numpy as jnp
from jax import lax
from jax.sharding import PartitionSpec as P

KA = 32
KB = 32
SEQ = 128
F32 = jnp.float32
BF16 = jnp.bfloat16


def dot(a, b, dims):
    return lax.dot_general(a, b, (dims, ((), ())), preferred_element_type=F32)


def after(value, *earlier):
    return lax.optimization_barrier((value, *earlier))[0]


def make_per_device(n_fsdp, n_ckpt, n_dp):
    n_x = n_dp // 2
    core_pairs = [(i, i ^ 1) for i in range(n_dp)]

    def swap_core(value):
        return lax.ppermute(value, "dp", core_pairs)

    def shift_x(value, shift):
        shift = shift % n_x
        return lax.ppermute(value, "dp", [(i, (i + 2 * shift) % n_dp) for i in range(n_dp)])

    square = n_x == 2 and n_fsdp == 2
    both = ("fsdp", "dp")
    off_x, off_y, on_x, on_y = [], [], [], []
    if square:
        for f in range(2):
            for d in range(n_dp):
                here = f * n_dp + d
                by_x, by_y = (here, f * n_dp + (d + 2) % n_dp), (here, (1 - f) * n_dp + d)
                (on_x if d // 2 == f else off_x).append(by_x)
                (on_y if d // 2 == f else off_y).append(by_y)

    def spread(rows, x_index, aligned, width, cuts, marks):
        if square:
            first = cuts[0]
            stages = [lax.ppermute(rows[first[0] : first[1]], both, off_x + on_y)]
            started = start_landmarks(after(marks, stages[0]))
            for index, (lo, hi) in enumerate(cuts[1:], start=1):
                operand = jnp.where(aligned, stages[-1], after(rows, stages[-1])[lo:hi])
                if index == 2:
                    operand = after(operand, *started)
                stages.append(lax.ppermute(operand, both, off_x + on_y))

            def other(shift, cut, earlier):
                if cut + 2 == len(stages) and len(stages) == len(cuts):
                    stages.append(lax.ppermute(after(stages[-1], earlier), both, on_y))
                here, there = stages[cut], stages[cut + 1]
                if earlier is not None:
                    here, there = after((here, there), earlier)
                return jnp.where(aligned, here, there)

            def own(earlier, later):
                rest = lax.ppermute(after(rows, stages[-1], earlier)[first[1] :], both, on_y)
                begin, rest, _ = lax.optimization_barrier((stages[0], rest, later))
                return jnp.where(aligned, rows, jnp.concatenate([begin, rest], axis=0))

            return own, other, started
        full = lax.all_gather(rows, "fsdp", axis=1, tiled=True)

        def own(earlier, later):
            return lax.dynamic_slice_in_dim(after(full, later), x_index * width, width, 1)

        parts = []
        for shift in range(1, n_x):
            part = lax.dynamic_slice_in_dim(full, lax.rem(x_index + shift, n_x) * width, width, 1)
            parts.append(shift_x(part, shift))

        def other(shift, cut, earlier):
            lo, hi = cuts[cut]
            block = parts[shift - 1][lo:hi]
            return block if earlier is None else after(block, earlier)

        return own, other, []

    def start_landmarks(marks):
        return [lax.ppermute(marks, both, off_y), lax.ppermute(marks, both, on_x)]

    def cross_landmarks(started):
        return [lax.ppermute(started[0], both, on_x)] if square else []

    def gather_landmarks(marks, started, crossed, x_index, core, aligned):
        if not square:
            marks = lax.all_gather(marks, "dp", axis=0, tiled=True)
            marks = lax.all_gather(marks, "fsdp", axis=1, tiled=True)
            return lambda earlier: marks

        def assemble(earlier):
            blocks = after((marks, started[0], started[1], crossed[0]), earlier)
            mine = jnp.where(aligned, jnp.stack(blocks[:2]), jnp.stack(blocks[2:]))
            beside = lax.ppermute(mine, both, on_y + off_y)
            own = jnp.where(aligned, mine, beside)
            far = jnp.where(aligned, beside, mine)
            chips = jnp.where(x_index == 0, jnp.stack([own, far]), jnp.stack([far, own]))
            sibling = lax.ppermute(chips, "dp", core_pairs)
            cores = lax.optimization_barrier(
                [jnp.where(core == 0, chips, sibling), jnp.where(core == 0, sibling, chips)]
            )
            rows = []
            for x in range(2):
                for one in cores:
                    rows.append(jnp.concatenate([one[x, x], one[x, 1 - x]], axis=1))
            return jnp.concatenate(lax.optimization_barrier(rows), axis=0)

        return assemble

    def scatter_sum(value, axis_name, size):
        index = lax.axis_index(axis_name)
        total = lax.dynamic_index_in_dim(value, index, 1, keepdims=False)
        for shift in range(1, size):
            block = lax.dynamic_index_in_dim(value, lax.rem(index + shift, size), 1, keepdims=False)
            total = total + lax.ppermute(
                block, axis_name, [(i, (i + shift) % size) for i in range(size)]
            )
        return total

    def per_device(activations, gate_weight, cotangent, sketch_left, sketch_right, landmarks):
        f_index = lax.axis_index("fsdp")
        d_index = lax.axis_index("dp")
        x_index, core = d_index // 2, lax.rem(d_index, 2)
        aligned = x_index == f_index
        rows, weight, cot = activations[0], gate_weight[0], cotangent[0]
        tokens, part = rows.shape
        depth = weight.shape[0]
        examples = tokens // SEQ

        weight_sibling = swap_core(weight)
        cuts = [(e * SEQ, (e + 1) * SEQ) for e in range(examples)]
        own, other, started = spread(
            rows, x_index, aligned, 2 * depth, cuts, landmarks[0]
        )
        crossed = cross_landmarks(started)
        assemble = gather_landmarks(landmarks[0], started, crossed, x_index, core, aligned)

        def split(block):
            low, high = block[:, :depth], block[:, depth:]
            return jnp.where(core == 0, low, high), jnp.where(core == 0, high, low)

        def product(block, h0=0, h1=weight.shape[1]):
            mine, theirs = split(block)
            return dot(mine, weight[:, h0:h1], ((1,), (0,))) + dot(
                theirs, weight_sibling[:, h0:h1], ((1,), (0,))
            )

        def partials(cut, lo, hi, earlier, h0=0, h1=weight.shape[1]):
            return [
                product(other(shift, cut, earlier)[lo:hi], h0, h1).astype(BF16)
                for shift in range(1, n_x)
            ]

        def send(values, earlier=None):
            if earlier is not None:
                values = [after(value, *earlier) for value in values]
            return [shift_x(value, -shift) for shift, value in enumerate(values, start=1)]

        half, hidden = SEQ // 2, weight.shape[1]
        part_a = partials(0, 0, SEQ, None, 0, hidden // 2)
        got_a = send(part_a)
        part_b = partials(0, 0, SEQ, part_a, hidden // 2, hidden)
        got_b = send(part_b)
        part_c = partials(1, 0, SEQ, part_b + crossed)
        got_c = send(part_c, got_a + got_b)
        part_d = partials(2, 0, half, got_b)
        got_d = send(part_d, got_c)
        part_e = partials(2, half, SEQ, part_d)
        got_e = send(part_e, got_c)
        marks = assemble(got_b[0])
        left = dot(
            after(rows, got_b[0]),
            lax.dynamic_slice_in_dim(sketch_left, f_index * part, part, 1),
            ((1,), (1,)),
        )
        if n_fsdp == 2:
            left = left + lax.ppermute(left, "fsdp", [(0, 1), (1, 0)])
        else:
            left = lax.psum(left, "fsdp")

        mine, theirs = split(own(part_c[0], part_e[0]))
        own_part = dot(mine, weight, ((1,), (0,)))
        theirs = after(theirs, own_part, *got_c)
        own_part = own_part + dot(theirs, weight_sibling, ((1,), (0,)))
        own_part, marks, left = lax.optimization_barrier((own_part, marks, left))

        def right_part(got, lo, hi, h0=0, h1=hidden):
            preact = own_part[lo:hi, h0:h1]
            for piece in got:
                preact = preact + piece.astype(F32)
            grad_up = (cot[lo:hi, h0:h1].astype(F32) * jax.nn.silu(preact)).astype(BF16)
            return dot(grad_up, sketch_right[:, h0:h1], ((1,), (1,)))

        rights = [
            right_part(got_a, 0, SEQ, 0, hidden // 2) + right_part(got_b, 0, SEQ, hidden // 2),
            right_part(got_c, SEQ, 2 * SEQ),
            right_part(got_d, 2 * SEQ, 2 * SEQ + half),
            right_part(got_e, 2 * SEQ + half, 3 * SEQ),
        ]
        right = jnp.concatenate(rights, axis=0).reshape(examples, SEQ, KB)
        features = jnp.einsum(
            "esa,esb->eab",
            left.reshape(examples, SEQ, KA),
            right,
            precision=lax.Precision.HIGHEST,
        ).reshape(examples, KA * KB)
        high = lax.reduce_precision(features, 8, 7)
        pair = jnp.concatenate([high, features - high], axis=0).astype(BF16)
        panels = dot(pair, marks, ((1,), (1,)))
        scores = panels[:examples] + panels[examples:]

        here = scores.shape[1] // (n_fsdp * n_ckpt)
        scores = scatter_sum(scores.reshape(examples, n_fsdp, n_ckpt * here), "fsdp", n_fsdp)
        return scatter_sum(scores.reshape(examples, n_ckpt, here), "ckpt", n_ckpt)

    return per_device


def solution(mesh):
    in_specs = (
        P("ckpt", "dp", "fsdp"),
        P("ckpt", "dp", "fsdp"),
        P("ckpt", "dp", "fsdp"),
        P(),
        P(None, "fsdp"),
        P("ckpt", "dp", "fsdp"),
    )
    out_specs = P("dp", ("fsdp", "ckpt"))
    per_device = make_per_device(mesh.shape["fsdp"], mesh.shape["ckpt"], mesh.shape["dp"])
    return jax.shard_map(
        per_device, mesh=mesh, in_specs=in_specs, out_specs=out_specs, check_vma=False
    )
```

time: 523 us -> 211 us (0.40)
  waiting for transfers between devices: 457 us -> 76.2 us
  matrix products: 42.2 us -> 80.9 us
  starting transfers between devices: 0.12 us -> 37.2 us
  other arithmetic: 0 us -> 14.2 us
  between operations: 13.2 us -> 0.53 us
  blocking collectives: 8.6 us -> 0 us
    all_gather x3 -> x0, waiting for transfers between devices: 392 us -> none  [the longest x1 345 us: per_device(): lax.all_gather(weight, 'dp', axis=0, tiled=True)]
    ppermute x0 -> x21, waiting for transfers between devices: none -> 76.2 us  [the longest x5 34.8 us: shift_x(): lax.ppermute(value, 'dp', [(i, (i + 2 * shift) % n_dp) for i in range(n_d...]
    unnamed x5 -> x0, waiting for transfers between devices: 64.8 us -> none
    dot_general x4 -> x20, matrix products: 39 us -> 80.9 us  [the longest x19 80.7 us: dot(): return lax.dot_general(a, b, (dims, ((), ())), preferred_element_type=F32)]
    ppermute x0 -> x21, starting transfers between devices: none -> 37.2 us  [the longest x5 7.64 us: shift_x(): lax.ppermute(value, 'dp', [(i, (i + 2 * shift) % n_dp) for i in range(n_d...]
    select_n x0 -> x11, other arithmetic: none -> 9.08 us  [the longest x1 2.06 us: spread(): operand = jnp.where(aligned, stages[-1], after(rows, stages[-1])[lo:hi])]
    psum x1 -> x0, blocking collectives: 8.6 us -> none  [per_device(): right_sketch = lax.psum(right_part, 'fsdp')]
  transfers between devices with their start and end apart: 4 -> 21, of which waited for: 3 -> 13; matrix products, arithmetic and copies ran while one was open for 7% -> 42% of each run, Pallas kernels for 0% -> 0%
where the time goes in v2:
time: 211 us
  matrix products  80.9 us (38%)
  waiting for transfers between devices  76.2 us (36%)
  starting transfers between devices  37.2 us (18%)
  other arithmetic  14.2 us (7%)
    dot_general x19, matrix products, dot(): return lax.dot_general(a, b, (dims, ((), ())), preferred_element_type=F32)  80.7 us
    ppermute x5, waiting for transfers between devices, shift_x(): lax.ppermute(value, 'dp', [(i, (i + 2 * shift) % n_dp) for i in range(n_d...  34.8 us
    ppermute x1, waiting for transfers between devices, spread(): stages = [lax.ppermute(rows[first[0]:first[1]], both, off_x + on_y)]  12.5 us
    ppermute x1, waiting for transfers between devices, per_device(): left = left + lax.ppermute(left, 'fsdp', [(0, 1), (1, 0)])  12.2 us
    ppermute x4, waiting for transfers between devices, scatter_sum(): lax.ppermute(block, axis_name, [(i, (i + shift) % size) for i in range(si...  7.8 us
    ppermute x5, starting transfers between devices, shift_x(): lax.ppermute(value, 'dp', [(i, (i + 2 * shift) % n_dp) for i in range(n_d...  7.64 us
    ppermute x2, starting transfers between devices, start_landmarks(): return [lax.ppermute(marks, both, off_y), lax.ppermute(marks, both, on_x)]  7.46 us
    ppermute x4, starting transfers between devices, scatter_sum(): lax.ppermute(block, axis_name, [(i, (i + shift) % size) for i in range(si...  5.07 us
  transfers between devices with their start and end apart: 21, of which 13 were waited for; matrix products, arithmetic and copies ran while one was open for 42% of the time, Pallas kernels for 0%

profile of v2, /device:TPU:0, one launch (start us, length us, event | category | flops | bytes accessed | tf_op | source)
XLA Modules:
  0.0 210.7 jit_solution(13990283668495544930)
XLA Ops:
  0.0 0.5 collective-permute-start.5
  0.5 1.1 slice_bitcast_fusion.8
  1.5 2.6 %collective-permute-start = (bf16[128,2048]{1,0:T(8,128)(2,1)S(1)}, bf16[128,2048]{1,0:T(8,128)(2,1)S(1)}, u32[]{:S(2)}, u32[]{:S(2)}) collective-permute-start(bf16[128,2048]{1,0:T(8,128)(2,1)S(1)} %slice_bitcast_fusion.8), channel_id=1, source_target_pairs={{2,0},{3,1},{16,18},{17,19},{0,16},{1,17},{18,2},{19,3},{6,4},{7,5... | collective-permute-start | bytes 1572872 | tf_op jit(solution)/shard_map/ppermute | solution.py:46
  4.2 12.5 %collective-permute-done = bf16[128,2048]{1,0:T(8,128)(2,1)S(1)} collective-permute-done((bf16[128,2048]{1,0:T(8,128)(2,1)S(1)}, bf16[128,2048]{1,0:T(8,128)(2,1)S(1)}, u32[]{:S(2)}, u32[]{:S(2)}) %collective-permute-start) | collective-permute-done | bytes 524320 | tf_op jit(solution)/shard_map/ppermute | solution.py:46
  16.7 2.1 slice_select_fusion.1
  18.7 1.8 collective-permute-start.1
  20.5 1.3 collective-permute-start.2
  21.8 6.2 %collective-permute-start.3 = (bf16[512,512]{1,0:T(8,128)(2,1)}, bf16[512,512]{1,0:T(8,128)(2,1)}, u32[]{:S(2)}, u32[]{:S(2)}) collective-permute-start(bf16[512,512]{1,0:T(8,128)(2,1)} %bitcast.103), channel_id=1, source_target_pairs={{0,2},{1,3},{18,16},{19,17},{4,6},{5,7},{22,20},{23,21},{8,10},{9,... | collective-permute-start | bytes 1572872 | tf_op jit(solution)/shard_map/ppermute | solution.py:86
  28.0 4.7 %collective-permute-done.1 = bf16[128,2048]{1,0:T(8,128)(2,1)S(1)} collective-permute-done((bf16[128,2048]{1,0:T(8,128)(2,1)}, bf16[128,2048]{1,0:T(8,128)(2,1)S(1)}, u32[]{:S(2)}, u32[]{:S(2)}) %collective-permute-start.1) | collective-permute-done | bytes 524320 | tf_op jit(solution)/shard_map/ppermute | solution.py:52
  32.7 1.1 broadcast_select_fusion.7
  33.8 2.1 %collective-permute-done.2 = bf16[512,512]{1,0:T(8,128)(2,1)} collective-permute-done((bf16[512,512]{1,0:T(8,128)(2,1)}, bf16[512,512]{1,0:T(8,128)(2,1)}, u32[]{:S(2)}, u32[]{:S(2)}) %collective-permute-start.2) | collective-permute-done | bytes 524320 | tf_op jit(solution)/shard_map/ppermute | solution.py:86
  35.9 2.0 collective-permute-done.3
  37.9 2.5 %collective-permute-start.4 = (bf16[128,2048]{1,0:T(8,128)(2,1)S(1)}, bf16[128,2048]{1,0:T(8,128)(2,1)S(1)}, u32[]{:S(2)}, u32[]{:S(2)}) collective-permute-start(bf16[128,2048]{1,0:T(8,128)(2,1)S(1)} %get-tuple-element.42), channel_id=1, source_target_pairs={{2,0},{3,1},{16,18},{17,19},{0,16},{1,17},{18,2},{19,3},{6,4},{7,5... | collective-permute-start | bytes 1572872 | tf_op jit(solution)/shard_map/ppermute | solution.py:52
  40.4 1.9 collective-permute-start.6
  42.4 4.4 %fusion.7 = f32[128,3584]{1,0:T(8,128)S(1)} fusion(bf16[1024,7168]{1,0:T(8,128)(2,1)} %collective-permute-done.5, pred[]{:T(512)S(6)} %eq.6, bf16[128,2048]{1,0:T(8,128)(2,1)S(1)} %get-tuple-element.85), kind=kOutput, calls=%fused_computation.11 | convolution fusion | flops 939655168 | bytes 9699329 | tf_op jit(solution)/shard_map/dot_general | solution.py:14
  46.8 4.5 %fusion.20 = bf16[128,3584]{1,0:T(8,128)(2,1)S(1)} fusion(f32[128,3584]{1,0:T(8,128)S(1)} %fusion.7, bf16[1024,7168]{1,0:T(8,128)(2,1)} %bitcast.94, pred[]{:T(512)S(6)} %eq.6, bf16[128,2048]{1,0:T(8,128)(2,1)S(1)} %get-tuple-element.85), kind=kOutput, calls=%fused_computation.18 | convolution fusion | flops 940572672 | bytes 10616833 | tf_op jit(solution)/shard_map/dot_general | solution.py:14
  51.5 1.1 fusion.5
  52.6 4.4 %fusion.17 = bf16[128,3584]{1,0:T(8,128)(2,1)S(1)} fusion(f32[128,3584]{1,0:T(8,128)S(1)} %fusion.5, bf16[1024,7168]{1,0:T(8,128)(2,1)} %collective-permute-done.5, pred[]{:T(512)S(6)} %eq.6, bf16[128,2048]{1,0:T(8,128)(2,1)S(1)} %broadcast_select_fusion.6), kind=kOutput, calls=%fused_computation.17 | convolution fusion | flops 940572672 | bytes 10616833 | tf_op jit(solution)/shard_map/dot_general | solution.py:14
  57.0 2.1 collective-permute-start.9
  59.0 2.0 collective-permute-start.7
  61.1 2.1 fusion.39
  63.2 7.7 %fusion = bf16[128,7168]{1,0:T(8,128)(2,1)S(1)} fusion(f32[128,7168]{1,0:T(8,128)S(1)} %fusion.39, bf16[1024,7168]{1,0:T(8,128)(2,1)} %collective-permute-done.5, pred[]{:T(512)S(6)} %eq.6, bf16[128,2048]{1,0:T(8,128)(2,1)S(1)} %broadcast_select_fusion.5), kind=kOutput, calls=%fused_computation.2 | convolution fusion | flops 1881014272 | bytes 20709376 | tf_op jit(solution)/shard_map/dot_general | solution.py:14
  71.1 3.7 %collective-permute-start.8 = (bf16[256,2048]{1,0:T(8,128)(2,1)S(1)}, bf16[256,2048]{1,0:T(8,128)(2,1)S(1)}, u32[]{:S(2)}, u32[]{:S(2)}) collective-permute-start(bf16[256,2048]{1,0:T(8,128)(2,1)S(1)} %slice.152), channel_id=1, source_target_pairs={{0,16},{1,17},{18,2},{19,3},{4,20},{5,21},{22,6},{23,7},{8,24},{9,... | collective-permute-start | bytes 3145736 | tf_op jit(solution)/shard_map/ppermute | solution.py:63
  74.7 16.6 %collective-permute-done.9 = bf16[128,3584]{1,0:T(8,128)(2,1)S(1)} collective-permute-done((bf16[128,3584]{1,0:T(8,128)(2,1)S(1)}, bf16[128,3584]{1,0:T(8,128)(2,1)S(1)}, u32[]{:S(2)}, u32[]{:S(2)}) %collective-permute-start.9) | collective-permute-done | bytes 917536 | tf_op jit(solution)/shard_map/ppermute | solution.py:30
  91.4 2.7 %fusion.71 = f32[64,7168]{1,0:T(8,128)S(1)} fusion(pred[]{:T(512)S(6)} %eq.6, bf16[128,2048]{1,0:T(8,128)(2,1)S(1)} %broadcast_select_fusion.4, bf16[1,1024,7168]{2,1,0:T(8,128)(2,1)S(1)} %bitcast.96), kind=kOutput, calls=%fused_computation.99 | convolution fusion | flops 939589632 | bytes 16777216 | tf_op jit(solution)/shard_map/dot_general | solution.py:14
  94.1 8.8 %fusion.1 = bf16[64,7168]{1,0:T(8,128)(2,1)} fusion(f32[64,7168]{1,0:T(8,128)S(1)} %fusion.71, bf16[1024,7168]{1,0:T(8,128)(2,1)} %collective-permute-done.5, pred[]{:T(512)S(6)} %eq.6, bf16[128,2048]{1,0:T(8,128)(2,1)S(1)} %broadcast_select_fusion.4), kind=kOutput, calls=%fused_computation.5 | convolution fusion | flops 940507136 | bytes 17694720 | tf_op jit(solution)/shard_map/dot_general | solution.py:14
  103.0 2.7 %fusion.68 = f32[64,7168]{1,0:T(8,128)S(1)} fusion(pred[]{:T(512)S(6)} %eq.6, bf16[128,2048]{1,0:T(8,128)(2,1)S(1)} %broadcast_select_fusion.3, bf16[1,1024,7168]{2,1,0:T(8,128)(2,1)S(1)} %bitcast.96), kind=kOutput, calls=%fused_computation.96 | convolution fusion | flops 939589632 | bytes 16777216 | tf_op jit(solution)/shard_map/dot_general | solution.py:14
  105.7 2.5 %collective-permute-start.11 = (bf16[128,7168]{1,0:T(8,128)(2,1)S(1)}, bf16[128,7168]{1,0:T(8,128)(2,1)S(1)}, u32[]{:S(2)}, u32[]{:S(2)}) collective-permute-start(bf16[128,7168]{1,0:T(8,128)(2,1)S(1)} %fusion), channel_id=1, source_target_pairs={{0,2},{1,3},{2,0},{3,1},{4,6},{5,7},{6,4},{7,5},{8,10},{9,11},{10,... | collective-permute-start | bytes 5505032 | tf_op jit(solution)/shard_map/ppermute | solution.py:30
  108.2 1.4 maximum_select_fusion.2
  109.7 0.6 fusion.65
  110.3 2.0 collective-permute-start.14
  112.3 8.8 %fusion.2 = bf16[64,7168]{1,0:T(8,128)(2,1)} fusion(f32[64,7168]{1,0:T(8,128)S(1)} %fusion.68, bf16[1024,7168]{1,0:T(8,128)(2,1)} %collective-permute-done.5, pred[]{:T(512)S(6)} %eq.6, bf16[128,2048]{1,0:T(8,128)(2,1)S(1)} %broadcast_select_fusion.3), kind=kOutput, calls=%fused_computation.6 | convolution fusion | flops 940507136 | bytes 17694720 | tf_op jit(solution)/shard_map/dot_general | solution.py:14
  121.1 12.2 %collective-permute-done.14 = f32[384,32]{0,1:T(8,128)S(1)} collective-permute-done((f32[384,32]{0,1:T(8,128)S(1)}, f32[384,32]{0,1:T(8,128)S(1)}, u32[]{:S(2)}, u32[]{:S(2)}) %collective-permute-start.14) | collective-permute-done | bytes 49184 | tf_op jit(solution)/shard_map/ppermute | solution.py:183
  133.3 0.6 maximum_select_fusion.1
  133.9 1.5 select_bitcast_fusion.1
  135.5 1.8 maximum_select_fusion
  137.2 8.7 %fusion.33 = f32[384,7168]{1,0:T(8,128)} fusion(pred[]{:T(512)S(6)} %eq.6, bf16[384,2048]{1,0:T(8,128)(2,1)S(1)} %maximum_select_fusion.1, bf16[1,1024,7168]{2,1,0:T(8,128)(2,1)S(1)} %bitcast.96), kind=kOutput, calls=%fused_computation.44 | convolution fusion | flops 5637537792 | bytes 27262976 | tf_op jit(solution)/shard_map/dot_general | solution.py:14
  146.1 0.1 collective-permute-done.11
  146.2 1.7 collective-permute-start.16
  148.0 1.2 collective-permute-start.15
  149.2 13.0 %convolution_add_fusion = f32[384,7168]{1,0:T(8,128)S(1)} fusion(f32[384,7168]{1,0:T(8,128)} %fusion.33, bf16[384,1024]{1,0:T(8,128)(2,1)S(1)} %broadcast_select_fusion.2, bf16[1024,7168]{1,0:T(8,128)(2,1)} %collective-permute-done.5), kind=kOutput, calls=%fused_computation | convolution fusion | flops 5639897088 | bytes 37486592 | tf_op jit(solution)/shard_map/dot_general | solution.py:14
  162.2 1.8 broadcast_select_fusion
  164.0 0.3 slice_bitcast_fusion.1
  164.3 0.1 pad_maximum_fusion.1
  164.5 0.1 pad_maximum_fusion.2
  164.6 0.1 pad_maximum_fusion.3
  164.9 2.4 %pad_maximum_fusion = bf16[2048,1024]{1,0:T(8,128)(2,1)} fusion(bf16[512,1024]{1,0:T(8,128)(2,1)S(1)} %pad_maximum_fusion.4, bf16[512,1024]{1,0:T(8,128)(2,1)S(1)} %pad_maximum_fusion.3, bf16[512,1024]{1,0:T(8,128)(2,1)S(1)} %pad_maximum_fusion.2, bf16[512,1024]{1,0:T(8,128)(2,1)S(1)} %pad_maximum_fusion.1), kind=kLoop, calls=%fused_computation.19 | loop fusion | flops 16777216 | bytes 8388608 | tf_op jit(solution)/shard_map/concatenate | solution.py:112
  167.3 2.4 %collective-permute-done.16 = bf16[64,7168]{1,0:T(8,128)(2,1)} collective-permute-done((bf16[64,7168]{1,0:T(8,128)(2,1)}, bf16[64,7168]{1,0:T(8,128)(2,1)}, u32[]{:S(2)}, u32[]{:S(2)}) %collective-permute-start.16) | collective-permute-done | bytes 917536 | tf_op jit(solution)/shard_map/ppermute | solution.py:30
  169.7 1.9 fusion.30
  171.7 1.3 fusion.26
  173.0 15.7 %collective-permute-done.15 = bf16[64,7168]{1,0:T(8,128)(2,1)} collective-permute-done((bf16[64,7168]{1,0:T(8,128)(2,1)}, bf16[64,7168]{1,0:T(8,128)(2,1)}, u32[]{:S(2)}, u32[]{:S(2)}) %collective-permute-start.15) | collective-permute-done | bytes 917536 | tf_op jit(solution)/shard_map/ppermute | solution.py:30
  188.7 1.9 fusion.28
  190.6 0.7 fusion.32
  191.3 2.0 convolution_add_fusion.4
  193.3 0.3 fusion.85
  193.7 3.4 %fusion.91 = f32[6,2048]{1,0:T(8,128)S(1)} fusion(bf16[2048,1024]{1,0:T(8,128)(2,1)} %pad_maximum_fusion, bf16[3,1024]{1,0:T(4,128)(2,1)S(1)} %get-tuple-element.93, bf16[3,1024]{1,0:T(4,128)(2,1)S(1)} %get-tuple-element.92), kind=kOutput, calls=%fused_computation.123 | convolution fusion | flops 25190400 | bytes 4255744 | tf_op jit(solution)/shard_map/dot_general | solution.py:14
  197.2 0.4 collective-permute-start.17
  197.6 3.4 %collective-permute-done.17 = f32[3,1024]{1,0:T(4,128)S(1)} collective-permute-done((f32[3,1024]{1,0:T(4,128)S(1)}, f32[3,1024]{1,0:T(4,128)S(1)}, u32[]{:S(2)}, u32[]{:S(2)}) %collective-permute-start.17) | collective-permute-done | bytes 12320 | tf_op jit(solution)/shard_map/ppermute | solution.py:121
  201.0 3.7 %collective-permute-start.20 = (f32[3,256]{1,0:T(4,128)S(1)}, f32[3,256]{1,0:T(4,128)S(1)}, u32[]{:S(2)}, u32[]{:S(2)}) collective-permute-start(f32[3,256]{1,0:T(4,128)S(1)} %get-tuple-element.90), channel_id=1, source_target_pairs={{0,12},{4,0},{8,4},{12,8},{1,13},{5,1},{9,5},{13,9},{2,14},{6,2},{... | collective-permute-start | bytes 9224 | tf_op jit(solution)/shard_map/ppermute | solution.py:121
  204.7 1.0 collective-permute-start.18
  205.7 0.3 collective-permute-done.20
  206.0 3.2 %collective-permute-done.19 = f32[3,256]{1,0:T(4,128)S(1)} collective-permute-done((f32[3,256]{1,0:T(4,128)S(1)}, f32[3,256]{1,0:T(4,128)S(1)}, u32[]{:S(2)}, u32[]{:S(2)}) %collective-permute-start.19) | collective-permute-done | bytes 3104 | tf_op jit(solution)/shard_map/ppermute | solution.py:121
  209.2 0.9 collective-permute-done.18
  210.1 0.6 fusion.96
  (64 shorter events, 1.1 us)
Async XLA Ops:
  0.0 109.7 %copy-start = (bf16[32,4096]{1,0:T(8,128)(2,1)S(1)}, bf16[32,4096]{1,0:T(8,128)(2,1)}, u32[]{:S(2)}) copy-start(bf16[32,4096]{1,0:T(8,128)(2,1)} %param.9) | copy-start | bytes 786436
  0.0 42.3 %collective-permute-start.5 = (bf16[1024,7168]{1,0:T(8,128)(2,1)}, bf16[1024,7168]{1,0:T(8,128)(2,1)}, u32[]{:S(2)}, u32[]{:S(2)}) collective-permute-start(bf16[1024,7168]{1,0:T(8,128)(2,1)} %bitcast.93), channel_id=1, source_target_pairs={{0,1},{1,0},{2,3},{3,2},{4,5},{5,4},{6,7},{7,6},{8,9},{9,8},{10,11... | collective-permute-start | bytes 44040200 | tf_op jit(solution)/shard_map/ppermute | solution.py:26
  1.5 15.1 %collective-permute-start = (bf16[128,2048]{1,0:T(8,128)(2,1)S(1)}, bf16[128,2048]{1,0:T(8,128)(2,1)S(1)}, u32[]{:S(2)}, u32[]{:S(2)}) collective-permute-start(bf16[128,2048]{1,0:T(8,128)(2,1)S(1)} %slice_bitcast_fusion.8), channel_id=1, source_target_pairs={{2,0},{3,1},{16,18},{17,19},{0,16},{1,17},{18,2},{19,3},{6,4},{7,5... | collective-permute-start | bytes 1572872 | tf_op jit(solution)/shard_map/ppermute | solution.py:46
  16.7 34.7 %slice-start = ((s8[14680064]{0:T(1024)(128)(4,1)}), s8[2097152]{0:T(1024)(128)(4,1)S(1)}, s32[]{:S(2)}) async-start(s8[14680064]{0:T(1024)(128)(4,1)} %bitcast.95), calls=%async_computation | async-start | bytes 4194304
  18.7 13.9 %collective-permute-start.1 = (bf16[128,2048]{1,0:T(8,128)(2,1)}, bf16[128,2048]{1,0:T(8,128)(2,1)S(1)}, u32[]{:S(2)}, u32[]{:S(2)}) collective-permute-start(bf16[128,2048]{1,0:T(8,128)(2,1)} %slice_select_fusion.1), channel_id=1, source_target_pairs={{2,0},{3,1},{16,18},{17,19},{0,16},{1,17},{18,2},{19,3},{6,4},{7,5... | collective-permute-start | bytes 1572872 | tf_op jit(solution)/shard_map/ppermute | solution.py:52
  20.5 15.4 %collective-permute-start.2 = (bf16[512,512]{1,0:T(8,128)(2,1)}, bf16[512,512]{1,0:T(8,128)(2,1)}, u32[]{:S(2)}, u32[]{:S(2)}) collective-permute-start(bf16[512,512]{1,0:T(8,128)(2,1)} %bitcast.102), channel_id=1, source_target_pairs={{2,18},{3,19},{16,0},{17,1},{6,22},{7,23},{20,4},{21,5},{10,26},{1... | collective-permute-start | bytes 1572872 | tf_op jit(solution)/shard_map/ppermute | solution.py:86
  21.8 16.1 %collective-permute-start.3 = (bf16[512,512]{1,0:T(8,128)(2,1)}, bf16[512,512]{1,0:T(8,128)(2,1)}, u32[]{:S(2)}, u32[]{:S(2)}) collective-permute-start(bf16[512,512]{1,0:T(8,128)(2,1)} %bitcast.103), channel_id=1, source_target_pairs={{0,2},{1,3},{18,16},{19,17},{4,6},{5,7},{22,20},{23,21},{8,10},{9,... | collective-permute-start | bytes 1572872 | tf_op jit(solution)/shard_map/ppermute | solution.py:86
  37.9 21.1 %collective-permute-start.4 = (bf16[128,2048]{1,0:T(8,128)(2,1)S(1)}, bf16[128,2048]{1,0:T(8,128)(2,1)S(1)}, u32[]{:S(2)}, u32[]{:S(2)}) collective-permute-start(bf16[128,2048]{1,0:T(8,128)(2,1)S(1)} %get-tuple-element.42), channel_id=1, source_target_pairs={{2,0},{3,1},{16,18},{17,19},{0,16},{1,17},{18,2},{19,3},{6,4},{7,5... | collective-permute-start | bytes 1572872 | tf_op jit(solution)/shard_map/ppermute | solution.py:52
  40.4 18.6 %collective-permute-start.6 = (bf16[512,512]{1,0:T(8,128)(2,1)}, bf16[512,512]{1,0:T(8,128)(2,1)S(1)}, u32[]{:S(2)}, u32[]{:S(2)}) collective-permute-start(bf16[512,512]{1,0:T(8,128)(2,1)} %collective-permute-done.2), channel_id=1, source_target_pairs={{0,2},{1,3},{18,16},{19,17},{4,6},{5,7},{22,20},{23,21},{8,10},{9,... | collective-permute-start | bytes 1572872 | tf_op jit(solution)/shard_map/ppermute | solution.py:89
  42.3 9.1 %slice-start.1 = ((s8[14680064]{0:T(1024)(128)(4,1)}), s8[4194304]{0:T(1024)(128)(4,1)S(1)}, s32[]{:S(2)}) async-start(s8[14680064]{0:T(1024)(128)(4,1)} %bitcast.95), calls=%async_computation.1 | async-start | bytes 8388608
  42.3 9.1 %slice-start.2 = ((s8[14680064]{0:T(1024)(128)(4,1)}), s8[4194304]{0:T(1024)(128)(4,1)S(1)}, s32[]{:S(2)}) async-start(s8[14680064]{0:T(1024)(128)(4,1)} %bitcast.95), calls=%async_computation.2 | async-start | bytes 8388608
  46.7 4.7 %slice-start.3 = ((s8[14680064]{0:T(1024)(128)(4,1)}), s8[4194304]{0:T(1024)(128)(4,1)S(1)}, s32[]{:S(2)}) async-start(s8[14680064]{0:T(1024)(128)(4,1)} %bitcast.95), calls=%async_computation.3 | async-start | bytes 8388608
  51.3 54.4 %collective-permute-start.10 = (bf16[128,3584]{1,0:T(8,128)(2,1)S(1)}, bf16[128,3584]{1,0:T(8,128)(2,1)}, u32[]{:S(2)}, u32[]{:S(2)}) collective-permute-start(bf16[128,3584]{1,0:T(8,128)(2,1)S(1)} %fusion.20), channel_id=1, source_target_pairs={{0,2},{1,3},{2,0},{3,1},{4,6},{5,7},{6,4},{7,5},{8,10},{9,11},{10,... | collective-permute-start | bytes 2752520 | tf_op jit(solution)/shard_map/ppermute | solution.py:30
  57.0 34.4 %collective-permute-start.9 = (bf16[128,3584]{1,0:T(8,128)(2,1)S(1)}, bf16[128,3584]{1,0:T(8,128)(2,1)S(1)}, u32[]{:S(2)}, u32[]{:S(2)}) collective-permute-start(bf16[128,3584]{1,0:T(8,128)(2,1)S(1)} %fusion.17), channel_id=1, source_target_pairs={{0,2},{1,3},{2,0},{3,1},{4,6},{5,7},{6,4},{7,5},{8,10},{9,11},{10,... | collective-permute-start | bytes 2752520 | tf_op jit(solution)/shard_map/ppermute | solution.py:30
  59.0 11.9 %collective-permute-start.7 = (bf16[128,2048]{1,0:T(8,128)(2,1)S(1)}, bf16[128,2048]{1,0:T(8,128)(2,1)S(1)}, u32[]{:S(2)}, u32[]{:S(2)}) collective-permute-start(bf16[128,2048]{1,0:T(8,128)(2,1)S(1)} %collective-permute-done.4), channel_id=1, source_target_pairs={{0,16},{1,17},{18,2},{19,3},{4,20},{5,21},{22,6},{23,7},{8,24},{9,... | collective-permute-start | bytes 1572872 | tf_op jit(solution)/shard_map/ppermute | solution.py:56
  63.2 7.7 %copy-start.2 = (bf16[1,384,2048]{2,1,0:T(8,128)(2,1)S(1)}, bf16[1,384,2048]{2,1,0:T(8,128)(2,1)}, u32[]{:S(2)}) copy-start(bf16[1,384,2048]{2,1,0:T(8,128)(2,1)} %param.6) | copy-start | bytes 4718596
  71.1 62.3 %collective-permute-start.8 = (bf16[256,2048]{1,0:T(8,128)(2,1)S(1)}, bf16[256,2048]{1,0:T(8,128)(2,1)S(1)}, u32[]{:S(2)}, u32[]{:S(2)}) collective-permute-start(bf16[256,2048]{1,0:T(8,128)(2,1)S(1)} %slice.152), channel_id=1, source_target_pairs={{0,16},{1,17},{18,2},{19,3},{4,20},{5,21},{22,6},{23,7},{8,24},{9,... | collective-permute-start | bytes 3145736 | tf_op jit(solution)/shard_map/ppermute | solution.py:63
  91.3 2.7 %copy-start.8 = (bf16[128,3584]{1,0:T(8,128)(2,1)}, bf16[128,3584]{1,0:T(8,128)(2,1)S(1)}, u32[]{:S(2)}) copy-start(bf16[128,3584]{1,0:T(8,128)(2,1)S(1)} %collective-permute-done.9) | copy-start | bytes 2752516
  103.0 5.2 %copy-start.5 = (bf16[1,512,512]{2,1,0:T(8,128)(2,1)S(1)}, bf16[1,512,512]{2,1,0:T(8,128)(2,1)}, u32[]{:S(2)}) copy-start(bf16[1,512,512]{2,1,0:T(8,128)(2,1)} %param.11) | copy-start | bytes 1572868
  105.7 40.5 %collective-permute-start.11 = (bf16[128,7168]{1,0:T(8,128)(2,1)S(1)}, bf16[128,7168]{1,0:T(8,128)(2,1)S(1)}, u32[]{:S(2)}, u32[]{:S(2)}) collective-permute-start(bf16[128,7168]{1,0:T(8,128)(2,1)S(1)} %fusion), channel_id=1, source_target_pairs={{0,2},{1,3},{2,0},{3,1},{4,6},{5,7},{6,4},{7,5},{8,10},{9,11},{10,... | collective-permute-start | bytes 5505032 | tf_op jit(solution)/shard_map/ppermute | solution.py:30
  109.6 24.3 %collective-permute-start.12 = (bf16[2,512,512]{2,1,0:T(8,128)(2,1)S(1)}, bf16[2,512,512]{2,1,0:T(8,128)(2,1)S(1)}, u32[]{:S(2)}, u32[]{:S(2)}) collective-permute-start(bf16[2,512,512]{2,1,0:T(8,128)(2,1)S(1)} %maximum_select_fusion.2), channel_id=1, source_target_pairs={{0,16},{1,17},{18,2},{19,3},{2,18},{3,19},{16,0},{17,1},{4,20},{5,... | collective-permute-start | bytes 3145736 | tf_op jit(solution)/shard_map/ppermute | solution.py:100
  110.3 23.0 %collective-permute-start.14 = (f32[384,32]{0,1:T(8,128)S(1)}, f32[384,32]{0,1:T(8,128)S(1)}, u32[]{:S(2)}, u32[]{:S(2)}) collective-permute-start(f32[384,32]{0,1:T(8,128)S(1)} %fusion.65), channel_id=1, source_target_pairs={{0,16},{16,0},{1,17},{17,1},{2,18},{18,2},{3,19},{19,3},{4,20},{20... | collective-permute-start | bytes 147464 | tf_op jit(solution)/shard_map/ppermute | solution.py:183
  135.4 1.8 copy-start.3
  137.2 24.9 %collective-permute-start.13 = (bf16[2,2,512,512]{3,2,1,0:T(8,128)(2,1)}, bf16[2,2,512,512]{3,2,1,0:T(8,128)(2,1)}, u32[]{:S(2)}, u32[]{:S(2)}) collective-permute-start(bf16[2,2,512,512]{3,2,1,0:T(8,128)(2,1)} %maximum_select_fusion), channel_id=1, source_target_pairs={{0,1},{1,0},{2,3},{3,2},{4,5},{5,4},{6,7},{7,6},{8,9},{9,8},{10,11... | collective-permute-start | bytes 6291464 | tf_op jit(solution)/shard_map/ppermute | solution.py:104
  146.1 16.1 %copy-start.4 = (bf16[1,2,512,512]{3,2,1,0:T(8,128)(2,1)S(1)}, bf16[1,2,512,512]{3,2,1,0:T(8,128)(2,1)}, u32[]{:S(2)}) copy-start(bf16[1,2,512,512]{3,2,1,0:T(8,128)(2,1)} %copy-done.3) | copy-start | bytes 3145732
  146.2 1.7 copy-start.6
  146.2 23.5 %collective-permute-start.16 = (bf16[64,7168]{1,0:T(8,128)(2,1)}, bf16[64,7168]{1,0:T(8,128)(2,1)}, u32[]{:S(2)}, u32[]{:S(2)}) collective-permute-start(bf16[64,7168]{1,0:T(8,128)(2,1)} %fusion.2), channel_id=1, source_target_pairs={{0,2},{1,3},{2,0},{3,1},{4,6},{5,7},{6,4},{7,5},{8,10},{9,11},{10,... | collective-permute-start | bytes 2752520 | tf_op jit(solution)/shard_map/ppermute | solution.py:30
  148.0 40.7 %collective-permute-start.15 = (bf16[64,7168]{1,0:T(8,128)(2,1)}, bf16[64,7168]{1,0:T(8,128)(2,1)}, u32[]{:S(2)}, u32[]{:S(2)}) collective-permute-start(bf16[64,7168]{1,0:T(8,128)(2,1)} %fusion.1), channel_id=1, source_target_pairs={{0,2},{1,3},{2,0},{3,1},{4,6},{5,7},{6,4},{7,5},{8,10},{9,11},{10,... | collective-permute-start | bytes 2752520 | tf_op jit(solution)/shard_map/ppermute | solution.py:30
  164.6 5.1 %slice-start.4 = ((s8[5505024]{0:T(1024)(128)(4,1)}), s8[4194304]{0:T(1024)(128)(4,1)S(1)}, s32[]{:S(2)}) async-start(s8[5505024]{0:T(1024)(128)(4,1)} %bitcast.109), calls=%async_computation.4 | async-start | bytes 8388608
  164.9 4.8 %slice-start.5 = ((s8[5505024]{0:T(1024)(128)(4,1)}), s8[1310720]{0:T(1024)(128)(4,1)S(1)}, s32[]{:S(2)}) async-start(s8[5505024]{0:T(1024)(128)(4,1)} %bitcast.109), calls=%async_computation.5 | async-start | bytes 2621440
  164.9 4.8 %copy-start.10 = (bf16[32,7168]{1,0:T(8,128)(2,1)S(1)}, bf16[32,7168]{1,0:T(8,128)(2,1)}, u32[]{:S(2)}) copy-start(bf16[32,7168]{1,0:T(8,128)(2,1)} %param.10) | copy-start | bytes 1376260
  167.3 4.3 %copy-start.7 = (bf16[128,7168]{1,0:T(8,128)(2,1)S(1)}, bf16[128,7168]{1,0:T(8,128)(2,1)}, u32[]{:S(2)}) copy-start(bf16[128,7168]{1,0:T(8,128)(2,1)} %copy-done.6) | copy-start | bytes 5505028
  173.0 17.6 %copy-start.9 = (bf16[128,3584]{1,0:T(8,128)(2,1)S(1)}, bf16[128,3584]{1,0:T(8,128)(2,1)}, u32[]{:S(2)}) copy-start(bf16[128,3584]{1,0:T(8,128)(2,1)} %copy-done.8) | copy-start | bytes 2752516
  193.7 17.0 %copy-start.1 = (bf16[32,4096]{1,0:T(8,128)(2,1)S(1)}, bf16[32,4096]{1,0:T(8,128)(2,1)}, u32[]{:S(2)}) copy-start(bf16[32,4096]{1,0:T(8,128)(2,1)} %param.9) | copy-start | bytes 786436
  197.2 3.8 %collective-permute-start.17 = (f32[3,1024]{1,0:T(4,128)S(1)}, f32[3,1024]{1,0:T(4,128)S(1)}, u32[]{:S(2)}, u32[]{:S(2)}) collective-permute-start(f32[3,1024]{1,0:T(4,128)S(1)} %bitcast.108), channel_id=1, source_target_pairs={{0,16},{16,0},{1,17},{17,1},{2,18},{18,2},{3,19},{19,3},{4,20},{20... | collective-permute-start | bytes 36872 | tf_op jit(solution)/shard_map/ppermute | solution.py:121
  201.0 5.0 %collective-permute-start.20 = (f32[3,256]{1,0:T(4,128)S(1)}, f32[3,256]{1,0:T(4,128)S(1)}, u32[]{:S(2)}, u32[]{:S(2)}) collective-permute-start(f32[3,256]{1,0:T(4,128)S(1)} %get-tuple-element.90), channel_id=1, source_target_pairs={{0,12},{4,0},{8,4},{12,8},{1,13},{5,1},{9,5},{13,9},{2,14},{6,2},{... | collective-permute-start | bytes 9224 | tf_op jit(solution)/shard_map/ppermute | solution.py:121
  204.7 4.5 %collective-permute-start.19 = (f32[3,256]{1,0:T(4,128)S(1)}, f32[3,256]{1,0:T(4,128)S(1)}, u32[]{:S(2)}, u32[]{:S(2)}) collective-permute-start(f32[3,256]{1,0:T(4,128)S(1)} %get-tuple-element.91), channel_id=1, source_target_pairs={{0,8},{4,12},{8,0},{12,4},{1,9},{5,13},{9,1},{13,5},{2,10},{6,14},... | collective-permute-start | bytes 9224 | tf_op jit(solution)/shard_map/ppermute | solution.py:121
  204.7 5.4 %collective-permute-start.18 = (f32[3,256]{1,0:T(4,128)S(1)}, f32[3,256]{1,0:T(4,128)S(1)}, u32[]{:S(2)}, u32[]{:S(2)}) collective-permute-start(f32[3,256]{1,0:T(4,128)S(1)} %get-tuple-element.89), channel_id=1, source_target_pairs={{0,4},{4,8},{8,12},{12,0},{1,5},{5,9},{9,13},{13,1},{2,6},{6,10},{... | collective-permute-start | bytes 9224 | tf_op jit(solution)/shard_map/ppermute | solution.py:121

commit v3 on v2

--- a/solution.py
+++ b/solution.py
@@ -45,10 +45,8 @@
             first = cuts[0]
             stages = [lax.ppermute(rows[first[0] : first[1]], both, off_x + on_y)]
             started = start_landmarks(after(marks, stages[0]))
-            for index, (lo, hi) in enumerate(cuts[1:], start=1):
+            for lo, hi in cuts[1:]:
                 operand = jnp.where(aligned, stages[-1], after(rows, stages[-1])[lo:hi])
-                if index == 2:
-                    operand = after(operand, *started)
                 stages.append(lax.ppermute(operand, both, off_x + on_y))
 
             def other(shift, cut, earlier):
@@ -92,7 +90,7 @@
         if not square:
             marks = lax.all_gather(marks, "dp", axis=0, tiled=True)
             marks = lax.all_gather(marks, "fsdp", axis=1, tiled=True)
-            return lambda earlier: marks
+            return lambda earlier: [marks]
 
         def assemble(earlier):
             blocks = after((marks, started[0], started[1], crossed[0]), earlier)
@@ -109,7 +107,7 @@
             for x in range(2):
                 for one in cores:
                     rows.append(jnp.concatenate([one[x, x], one[x, 1 - x]], axis=1))
-            return jnp.concatenate(lax.optimization_barrier(rows), axis=0)
+            return lax.optimization_barrier(rows)
 
         return assemble
 
@@ -162,20 +160,23 @@
                 values = [after(value, *earlier) for value in values]
             return [shift_x(value, -shift) for shift, value in enumerate(values, start=1)]
 
-        half, hidden = SEQ // 2, weight.shape[1]
-        part_a = partials(0, 0, SEQ, None, 0, hidden // 2)
+        most, hidden = 3 * SEQ // 4, weight.shape[1]
+        part_a = partials(0, 0, SEQ, started[:1] or None, 0, hidden // 2)
         got_a = send(part_a)
-        part_b = partials(0, 0, SEQ, part_a, hidden // 2, hidden)
+        part_b = partials(0, 0, SEQ, part_a + started, hidden // 2, hidden)
         got_b = send(part_b)
         part_c = partials(1, 0, SEQ, part_b + crossed)
-        got_c = send(part_c, got_a + got_b)
-        part_d = partials(2, 0, half, got_b)
+        part_de = partials(2, 0, SEQ, part_c)
+        part_d = [value[:most] for value in part_de]
+        part_e = [value[most:] for value in part_de]
+        got_c = send(part_c, got_a + got_b + part_d + part_e)
         got_d = send(part_d, got_c)
-        part_e = partials(2, half, SEQ, part_d)
         got_e = send(part_e, got_c)
-        marks = assemble(got_b[0])
+        mark_rows = assemble(got_b[0])
+        mine, theirs = split(own(part_c[0], got_b[0]))
+        own_part = dot(mine, weight, ((1,), (0,)))
         left = dot(
-            after(rows, got_b[0]),
+            after(rows, own_part),
             lax.dynamic_slice_in_dim(sketch_left, f_index * part, part, 1),
             ((1,), (1,)),
         )
@@ -183,12 +184,9 @@
             left = left + lax.ppermute(left, "fsdp", [(0, 1), (1, 0)])
         else:
             left = lax.psum(left, "fsdp")
-
-        mine, theirs = split(own(part_c[0], part_e[0]))
-        own_part = dot(mine, weight, ((1,), (0,)))
         theirs = after(theirs, own_part, *got_c)
         own_part = own_part + dot(theirs, weight_sibling, ((1,), (0,)))
-        own_part, marks, left = lax.optimization_barrier((own_part, marks, left))
+        own_part, left = lax.optimization_barrier((own_part, left))
 
         def right_part(got, lo, hi, h0=0, h1=hidden):
             preact = own_part[lo:hi, h0:h1]
@@ -198,11 +196,15 @@
             return dot(grad_up, sketch_right[:, h0:h1], ((1,), (1,)))
 
         rights = [
-            right_part(got_a, 0, SEQ, 0, hidden // 2) + right_part(got_b, 0, SEQ, hidden // 2),
-            right_part(got_c, SEQ, 2 * SEQ),
-            right_part(got_d, 2 * SEQ, 2 * SEQ + half),
-            right_part(got_e, 2 * SEQ + half, 3 * SEQ),
+            right_part(got_a, 0, SEQ, 0, hidden // 2) + right_part(got_b, 0, SEQ, hidden // 2)
         ]
+        for got, lo, hi in (
+            (got_c, SEQ, 2 * SEQ),
+            (got_d, 2 * SEQ, 2 * SEQ + most),
+            (got_e, 2 * SEQ + most, 3 * SEQ),
+        ):
+            rights.append(right_part([after(value, rights[-1], *mark_rows) for value in got], lo, hi))
+        marks = jnp.concatenate(mark_rows, axis=0)
         right = jnp.concatenate(rights, axis=0).reshape(examples, SEQ, KB)
         features = jnp.einsum(
             "esa,esb->eab",

time: 211 us -> 190 us (0.900)
  matrix products: 80.9 us -> 72.1 us
  other arithmetic: 14.2 us -> 7.67 us
  waiting for transfers between devices: 76.2 us -> 70.2 us
  local copies, waits for them, and re-layouts: 1.71 us -> 5.01 us
  starting transfers between devices: 37.2 us -> 34 us
    dot_general x19 -> x17, matrix products: 80.7 us -> 71.8 us  [dot(): return lax.dot_general(a, b, (dims, ((), ())), preferred_element_type=F32)]
    ppermute x5, starting transfers between devices: 7.64 us -> 4.1 us  [shift_x(): lax.ppermute(value, 'dp', [(i, (i + 2 * shift) % n_dp) for i in range(n_d...]
    ppermute x1, waiting for transfers between devices: 12.2 us -> 8.82 us  [per_device(): left = left + lax.ppermute(left, 'fsdp', [(0, 1), (1, 0)])]
    ppermute x5, waiting for transfers between devices: 34.8 us -> 31.6 us  [shift_x(): lax.ppermute(value, 'dp', [(i, (i + 2 * shift) % n_dp) for i in range(n_d...]
    ppermute x1, waiting for transfers between devices: 0.01 us -> 3.13 us  [own(): rest = lax.ppermute(after(rows, stages[-1], earlier)[first[1]:], both, on_y)]
    ppermute x2, waiting for transfers between devices: 4.11 us -> 1.49 us  [start_landmarks(): return [lax.ppermute(marks, both, off_y), lax.ppermute(marks, both, on_x)]]
    concatenate x1 -> x0, other arithmetic: 2.41 us -> none  [assemble(): return jnp.concatenate(lax.optimization_barrier(rows), axis=0)]
    ppermute x1, starting transfers between devices: 0.12 us -> 2.52 us  [assemble(): beside = lax.ppermute(mine, both, on_y + off_y)]
  transfers between devices with their start and end apart: 21 -> 21, of which waited for: 13 -> 11; matrix products, arithmetic and copies ran while one was open for 42% -> 41% of each run, Pallas kernels for 0% -> 0%
where the time goes in v3:
time: 190 us; the launch traced here: 189 us
  matrix products  72.1 us (38%)
  waiting for transfers between devices  70.2 us (37%)
  starting transfers between devices  34 us (18%)
  other arithmetic  7.67 us (4%)
  local copies, waits for them, and re-layouts  5.01 us (3%)
    dot_general x17, matrix products, dot(): return lax.dot_general(a, b, (dims, ((), ())), preferred_element_type=F32)  71.8 us
    ppermute x5, waiting for transfers between devices, shift_x(): lax.ppermute(value, 'dp', [(i, (i + 2 * shift) % n_dp) for i in range(n_d...  31.6 us
    ppermute x1, waiting for transfers between devices, spread(): stages = [lax.ppermute(rows[first[0]:first[1]], both, off_x + on_y)]  12.4 us
    ppermute x1, waiting for transfers between devices, per_device(): left = left + lax.ppermute(left, 'fsdp', [(0, 1), (1, 0)])  8.82 us
    ppermute x4, waiting for transfers between devices, scatter_sum(): lax.ppermute(block, axis_name, [(i, (i + shift) % size) for i in range(si...  6.58 us
    ppermute x2, waiting for transfers between devices, spread(): stages.append(lax.ppermute(operand, both, off_x + on_y))  6.16 us
    ppermute x2, starting transfers between devices, start_landmarks(): return [lax.ppermute(marks, both, off_y), lax.ppermute(marks, both, on_x)]  5.86 us
    ppermute x4, starting transfers between devices, scatter_sum(): lax.ppermute(block, axis_name, [(i, (i + shift) % size) for i in range(si...  5.61 us
  transfers between devices with their start and end apart: 21, of which 11 were waited for; matrix products, arithmetic and copies ran while one was open for 41% of the time, Pallas kernels for 0%

profile of v3, /device:TPU:0, one launch (start us, length us, event | category | flops | bytes accessed | tf_op | source)
XLA Modules:
  0.0 189.4 jit_solution(9859526335929696509)
XLA Ops:
  0.0 0.5 collective-permute-start.4
  0.5 1.1 slice_bitcast_fusion.8
  1.6 2.7 %collective-permute-start = (bf16[128,2048]{1,0:T(8,128)(2,1)S(1)}, bf16[128,2048]{1,0:T(8,128)(2,1)S(1)}, u32[]{:S(2)}, u32[]{:S(2)}) collective-permute-start(bf16[128,2048]{1,0:T(8,128)(2,1)S(1)} %slice_bitcast_fusion.8), channel_id=1, source_target_pairs={{2,0},{3,1},{16,18},{17,19},{0,16},{1,17},{18,2},{19,3},{6,4},{7,5... | collective-permute-start | bytes 1572872 | tf_op jit(solution)/shard_map/ppermute | solution.py:46
  4.3 12.4 %collective-permute-done = bf16[128,2048]{1,0:T(8,128)(2,1)S(1)} collective-permute-done((bf16[128,2048]{1,0:T(8,128)(2,1)S(1)}, bf16[128,2048]{1,0:T(8,128)(2,1)S(1)}, u32[]{:S(2)}, u32[]{:S(2)}) %collective-permute-start) | collective-permute-done | bytes 524320 | tf_op jit(solution)/shard_map/ppermute | solution.py:46
  16.7 1.9 %slice_select_fusion.1 = bf16[128,2048]{1,0:T(8,128)(2,1)} fusion(bf16[128,2048]{1,0:T(8,128)(2,1)S(1)} %collective-permute-done, bf16[384,2048]{1,0:T(8,128)(2,1)} %bitcast.94, pred[]{:T(512)S(6)} %eq.7), kind=kLoop, calls=%fused_computation.63 | loop fusion | flops 262144 | bytes 1572865 | tf_op jit(solution)/shard_map/jit(_where)/select_n | solution.py:49
  18.6 1.8 collective-permute-start.1
  20.4 1.3 collective-permute-start.3
  21.7 4.6 %collective-permute-start.5 = (bf16[512,512]{1,0:T(8,128)(2,1)}, bf16[512,512]{1,0:T(8,128)(2,1)S(1)}, u32[]{:S(2)}, u32[]{:S(2)}) collective-permute-start(bf16[512,512]{1,0:T(8,128)(2,1)} %bitcast.99), channel_id=1, source_target_pairs={{0,2},{1,3},{18,16},{19,17},{4,6},{5,7},{22,20},{23,21},{8,10},{9,... | collective-permute-start | bytes 1572872 | tf_op jit(solution)/shard_map/ppermute | solution.py:84
  26.3 6.2 %collective-permute-done.1 = bf16[128,2048]{1,0:T(8,128)(2,1)S(1)} collective-permute-done((bf16[128,2048]{1,0:T(8,128)(2,1)}, bf16[128,2048]{1,0:T(8,128)(2,1)S(1)}, u32[]{:S(2)}, u32[]{:S(2)}) %collective-permute-start.1) | collective-permute-done | bytes 524320 | tf_op jit(solution)/shard_map/ppermute | solution.py:50
  32.5 1.6 collective-permute-start.2
  34.1 1.5 collective-permute-done.3
  35.6 1.7 collective-permute-start.6
  37.3 4.4 %fusion.8 = f32[128,3584]{1,0:T(8,128)S(1)} fusion(bf16[1024,7168]{1,0:T(8,128)(2,1)} %bitcast.90, pred[]{:T(512)S(6)} %eq.6, bf16[128,2048]{1,0:T(8,128)(2,1)S(1)} %broadcast_select_fusion.6), kind=kOutput, calls=%fused_computation.11 | convolution fusion | flops 939655168 | bytes 9699329 | tf_op jit(solution)/shard_map/dot_general | solution.py:14
  41.7 5.4 %fusion.19 = bf16[128,3584]{1,0:T(8,128)(2,1)} fusion(f32[128,3584]{1,0:T(8,128)S(1)} %fusion.8, bf16[1024,7168]{1,0:T(8,128)(2,1)} %collective-permute-done.4, pred[]{:T(512)S(6)} %eq.6, bf16[128,2048]{1,0:T(8,128)(2,1)S(1)} %broadcast_select_fusion.6), kind=kOutput, calls=%fused_computation.16 | convolution fusion | flops 940572672 | bytes 10616833 | tf_op jit(solution)/shard_map/dot_general | solution.py:14
  47.3 1.1 fusion.4
  48.4 5.3 %fusion.16 = bf16[128,3584]{1,0:T(8,128)(2,1)} fusion(f32[128,3584]{1,0:T(8,128)S(1)} %fusion.4, bf16[1024,7168]{1,0:T(8,128)(2,1)} %collective-permute-done.4, pred[]{:T(512)S(6)} %eq.6, bf16[128,2048]{1,0:T(8,128)(2,1)S(1)} %broadcast_select_fusion.5), kind=kOutput, calls=%fused_computation.15 | convolution fusion | flops 940572672 | bytes 10616833 | tf_op jit(solution)/shard_map/dot_general | solution.py:14
  53.7 2.0 %collective-permute-start.9 = (bf16[128,3584]{1,0:T(8,128)(2,1)}, bf16[128,3584]{1,0:T(8,128)(2,1)}, u32[]{:S(2)}, u32[]{:S(2)}) collective-permute-start(bf16[128,3584]{1,0:T(8,128)(2,1)} %fusion.16), channel_id=1, source_target_pairs={{0,2},{1,3},{2,0},{3,1},{4,6},{5,7},{6,4},{7,5},{8,10},{9,11},{10,... | collective-permute-start | bytes 2752520 | tf_op jit(solution)/shard_map/ppermute | solution.py:30
  55.8 2.2 %collective-permute-start.7 = (bf16[128,2048]{1,0:T(8,128)(2,1)S(1)}, bf16[128,2048]{1,0:T(8,128)(2,1)S(1)}, u32[]{:S(2)}, u32[]{:S(2)}) collective-permute-start(bf16[128,2048]{1,0:T(8,128)(2,1)S(1)} %collective-permute-done.2), channel_id=1, source_target_pairs={{0,16},{1,17},{18,2},{19,3},{4,20},{5,21},{22,6},{23,7},{8,24},{9,... | collective-permute-start | bytes 1572872 | tf_op jit(solution)/shard_map/ppermute | solution.py:54
  58.1 2.1 %fusion.49 = f32[128,7168]{1,0:T(8,128)S(1)} fusion(pred[]{:T(512)S(6)} %eq.6, bf16[128,2048]{1,0:T(8,128)(2,1)S(1)} %broadcast_select_fusion.4, bf16[1,1024,7168]{2,1,0:T(8,128)(2,1)S(1)} %bitcast.92), kind=kOutput, calls=%fused_computation.74 | convolution fusion | flops 1879179264 | bytes 18874368 | tf_op jit(solution)/shard_map/dot_general | solution.py:14
  60.1 8.5 %fusion = bf16[128,7168]{1,0:T(8,128)(2,1)} fusion(f32[128,7168]{1,0:T(8,128)S(1)} %fusion.49, bf16[1024,7168]{1,0:T(8,128)(2,1)} %collective-permute-done.4, pred[]{:T(512)S(6)} %eq.6, bf16[128,2048]{1,0:T(8,128)(2,1)S(1)} %broadcast_select_fusion.4), kind=kOutput, calls=%fused_computation.3 | convolution fusion | flops 1881014272 | bytes 20709376 | tf_op jit(solution)/shard_map/dot_general | solution.py:14
  68.8 3.0 %collective-permute-start.8 = (bf16[256,2048]{1,0:T(8,128)(2,1)S(1)}, bf16[256,2048]{1,0:T(8,128)(2,1)S(1)}, u32[]{:S(2)}, u32[]{:S(2)}) collective-permute-start(bf16[256,2048]{1,0:T(8,128)(2,1)S(1)} %slice.146), channel_id=1, source_target_pairs={{0,16},{1,17},{18,2},{19,3},{4,20},{5,21},{22,6},{23,7},{8,24},{9,... | collective-permute-start | bytes 3145736 | tf_op jit(solution)/shard_map/ppermute | solution.py:61
  71.8 2.1 %fusion.46 = f32[128,7168]{1,0:T(8,128)S(1)} fusion(pred[]{:T(512)S(6)} %eq.6, bf16[128,2048]{1,0:T(8,128)(2,1)S(1)} %broadcast_select_fusion.3, bf16[1,1024,7168]{2,1,0:T(8,128)(2,1)S(1)} %bitcast.92), kind=kOutput, calls=%fused_computation.71 | convolution fusion | flops 1879179264 | bytes 18874368 | tf_op jit(solution)/shard_map/dot_general | solution.py:14
  73.9 7.3 %fusion.1 = bf16[128,7168]{1,0:T(8,128)(2,1)S(1)} fusion(f32[128,7168]{1,0:T(8,128)S(1)} %fusion.46, bf16[1024,7168]{1,0:T(8,128)(2,1)} %collective-permute-done.4, pred[]{:T(512)S(6)} %eq.6, bf16[128,2048]{1,0:T(8,128)(2,1)S(1)} %broadcast_select_fusion.3), kind=kOutput, calls=%fused_computation.4 | convolution fusion | flops 1881014272 | bytes 20709376 | tf_op jit(solution)/shard_map/dot_general | solution.py:14
  81.2 0.8 slice.190
  82.0 1.2 slice.189
  83.2 4.2 %collective-permute-done.9 = bf16[128,3584]{1,0:T(8,128)(2,1)} collective-permute-done((bf16[128,3584]{1,0:T(8,128)(2,1)}, bf16[128,3584]{1,0:T(8,128)(2,1)}, u32[]{:S(2)}, u32[]{:S(2)}) %collective-permute-start.9) | collective-permute-done | bytes 917536 | tf_op jit(solution)/shard_map/ppermute | solution.py:30
  87.5 0.2 maximum_select_fusion.2
  87.7 2.5 %collective-permute-start.13 = (bf16[2,512,512]{2,1,0:T(8,128)(2,1)S(1)}, bf16[2,512,512]{2,1,0:T(8,128)(2,1)S(1)}, u32[]{:S(2)}, u32[]{:S(2)}) collective-permute-start(bf16[2,512,512]{2,1,0:T(8,128)(2,1)S(1)} %maximum_select_fusion.2), channel_id=1, source_target_pairs={{0,16},{1,17},{18,2},{19,3},{2,18},{3,19},{16,0},{17,1},{4,20},{5,... | collective-permute-start | bytes 3145736 | tf_op jit(solution)/shard_map/ppermute | solution.py:98
  90.3 3.1 %collective-permute-done.8 = bf16[256,2048]{1,0:T(8,128)(2,1)S(1)} collective-permute-done((bf16[256,2048]{1,0:T(8,128)(2,1)S(1)}, bf16[256,2048]{1,0:T(8,128)(2,1)S(1)}, u32[]{:S(2)}, u32[]{:S(2)}) %collective-permute-start.8) | collective-permute-done | bytes 1048608 | tf_op jit(solution)/shard_map/ppermute | solution.py:61
  93.4 0.6 maximum_select_fusion.1
  94.0 8.6 %fusion.38 = f32[384,7168]{1,0:T(8,128)} fusion(pred[]{:T(512)S(6)} %eq.6, bf16[384,2048]{1,0:T(8,128)(2,1)S(1)} %maximum_select_fusion.1, bf16[1,1024,7168]{2,1,0:T(8,128)(2,1)S(1)} %bitcast.92), kind=kOutput, calls=%fused_computation.48 | convolution fusion | flops 5637537792 | bytes 27262976 | tf_op jit(solution)/shard_map/dot_general | solution.py:14
  102.6 0.6 fusion.81
  103.1 2.5 %collective-permute-start.12 = (f32[384,32]{0,1:T(8,128)S(1)}, f32[384,32]{0,1:T(8,128)S(1)}, u32[]{:S(2)}, u32[]{:S(2)}) collective-permute-start(f32[384,32]{0,1:T(8,128)S(1)} %fusion.81), channel_id=1, source_target_pairs={{0,16},{16,0},{1,17},{17,1},{2,18},{18,2},{3,19},{19,3},{4,20},{20... | collective-permute-start | bytes 147464 | tf_op jit(solution)/shard_map/ppermute | solution.py:184
  105.7 8.8 %collective-permute-done.12 = f32[384,32]{0,1:T(8,128)S(1)} collective-permute-done((f32[384,32]{0,1:T(8,128)S(1)}, f32[384,32]{0,1:T(8,128)S(1)}, u32[]{:S(2)}, u32[]{:S(2)}) %collective-permute-start.12) | collective-permute-done | bytes 49184 | tf_op jit(solution)/shard_map/ppermute | solution.py:184
  114.6 0.3 select_bitcast_fusion.1
  114.9 1.6 maximum_select_fusion
  116.6 13.9 %collective-permute-done.11 = bf16[128,7168]{1,0:T(8,128)(2,1)} collective-permute-done((bf16[128,7168]{1,0:T(8,128)(2,1)}, bf16[128,7168]{1,0:T(8,128)(2,1)}, u32[]{:S(2)}, u32[]{:S(2)}) %collective-permute-start.11) | collective-permute-done | bytes 1835040 | tf_op jit(solution)/shard_map/ppermute | solution.py:30
  130.5 0.6 collective-permute-start.16
  131.0 1.5 collective-permute-start.15
  132.5 13.0 %convolution_add_fusion = f32[384,7168]{1,0:T(8,128)S(1)} fusion(f32[384,7168]{1,0:T(8,128)} %fusion.38, bf16[384,1024]{1,0:T(8,128)(2,1)S(1)} %broadcast_select_fusion.2, bf16[1024,7168]{1,0:T(8,128)(2,1)} %collective-permute-done.4), kind=kOutput, calls=%fused_computation | convolution fusion | flops 5639897088 | bytes 37486592 | tf_op jit(solution)/shard_map/dot_general | solution.py:14
  145.5 2.2 %fusion.37 = f32[128,32]{0,1:T(8,128)S(1)} fusion(bf16[128,3584]{1,0:T(8,128)(2,1)} %collective-permute-done.9, f32[384,7168]{1,0:T(8,128)S(1)} %convolution_add_fusion, bf16[384,7168]{1,0:T(8,128)(2,1)} %bitcast.109, bf16[32,7168]{1,0:T(8,128)(2,1)S(1)} %copy-done.8), kind=kOutput, calls=%fused_computation.47 | convolution fusion | flops 33488896 | bytes 3915776 | tf_op jit(solution)/shard_map/dot_general | solution.py:14
  147.7 2.2 %convolution_add_fusion.3 = f32[128,32]{0,1:T(8,128)S(1)} fusion(f32[128,32]{0,1:T(8,128)S(1)} %fusion.37, bf16[128,3584]{1,0:T(8,128)(2,1)} %collective-permute-done.10, f32[384,7168]{1,0:T(8,128)S(1)} %convolution_add_fusion, bf16[384,7168]{1,0:T(8,128)(2,1)} %bitcast.110, bf16[32,7168]{1,0:T(8,128)(2,1)S(1)} %copy-done.8), kind=kOutput, calls=%fused_computation.37 | convolution fusion | flops 33492992 | bytes 3932160 | tf_op jit(solution)/shard_map/dot_general | solution.py:14
  149.9 0.5 broadcast_select_fusion
  150.4 0.3 slice_bitcast_fusion.1
  150.7 0.1 pad_maximum_fusion.3
  151.0 0.1 pad_maximum_fusion
  151.1 1.1 pad_maximum_fusion.2
  152.3 0.7 slice-done.4
  153.0 0.5 slice-done.5
  153.5 0.1 copy-done.9
  153.6 2.8 %fusion.32 = f32[128,32]{0,1:T(8,128)S(1)} fusion(bf16[32,7168]{1,0:T(8,128)(2,1)S(1)} %copy-done.9, bf16[128,7168]{1,0:T(8,128)(2,1)} %collective-permute-done.11, f32[384,7168]{1,0:T(8,128)S(1)} %convolution_add_fusion, bf16[1,384,7168]{2,1,0:T(8,128)(2,1)S(1)} %bitcast.112), kind=kOutput, calls=%fused_computation.34 | convolution fusion | flops 66977792 | bytes 7815168 | tf_op jit(solution)/shard_map/dot_general | solution.py:14
  156.4 13.4 %collective-permute-done.15 = bf16[96,7168]{1,0:T(8,128)(2,1)} collective-permute-done((bf16[96,7168]{1,0:T(8,128)(2,1)}, bf16[96,7168]{1,0:T(8,128)(2,1)}, u32[]{:S(2)}, u32[]{:S(2)}) %collective-permute-start.15) | collective-permute-done | bytes 1376288 | tf_op jit(solution)/shard_map/ppermute | solution.py:30
  169.8 2.4 %fusion.34 = f32[96,32]{0,1:T(8,128)S(1)} fusion(bf16[32,7168]{1,0:T(8,128)(2,1)S(1)} %copy-done.9, bf16[96,7168]{1,0:T(8,128)(2,1)} %collective-permute-done.15, f32[384,7168]{1,0:T(8,128)S(1)} %convolution_add_fusion, bf16[1,384,7168]{2,1,0:T(8,128)(2,1)S(1)} %bitcast.112), kind=kOutput, calls=%fused_computation.36 | convolution fusion | flops 50233344 | bytes 5976064 | tf_op jit(solution)/shard_map/dot_general | solution.py:14
  172.2 1.5 fusion.43
  173.7 0.3 fusion.83
  174.1 2.4 %fusion.22 = f32[6,2048]{1,0:T(8,128)S(1)} fusion(bf16[512,1024]{1,0:T(8,128)(2,1)S(1)} %pad_maximum_fusion.3, bf16[512,1024]{1,0:T(8,128)(2,1)} %pad_maximum_fusion.2, bf16[512,1024]{1,0:T(8,128)(2,1)S(1)} %pad_maximum_fusion.1, bf16[512,1024]{1,0:T(8,128)(2,1)S(1)} %pad_maximum_fusion, bf16[3,1024]{1,0:T(4,128)(2,1)S(1)} %get-tuple-element.93, ...), kind=kOutput, calls=%fused_computation.17 | convolution fusion | flops 41967616 | bytes 4255744 | tf_op jit(solution)/shard_map/dot_general | solution.py:14
  176.6 0.9 collective-permute-start.17
  177.5 2.9 %collective-permute-done.17 = f32[3,1024]{1,0:T(4,128)S(1)} collective-permute-done((f32[3,1024]{1,0:T(4,128)S(1)}, f32[3,1024]{1,0:T(4,128)S(1)}, u32[]{:S(2)}, u32[]{:S(2)}) %collective-permute-start.17) | collective-permute-done | bytes 12320 | tf_op jit(solution)/shard_map/ppermute | solution.py:119
  180.4 1.6 collective-permute-start.18
  182.0 2.2 %collective-permute-start.20 = (f32[3,256]{1,0:T(4,128)S(1)}, f32[3,256]{1,0:T(4,128)S(1)}, u32[]{:S(2)}, u32[]{:S(2)}) collective-permute-start(f32[3,256]{1,0:T(4,128)S(1)} %get-tuple-element.90), channel_id=1, source_target_pairs={{0,12},{4,0},{8,4},{12,8},{1,13},{5,1},{9,5},{13,9},{2,14},{6,2},{... | collective-permute-start | bytes 9224 | tf_op jit(solution)/shard_map/ppermute | solution.py:119
  184.3 0.8 collective-permute-start.19
  185.1 0.8 collective-permute-done.18
  185.9 2.9 %collective-permute-done.19 = f32[3,256]{1,0:T(4,128)S(1)} collective-permute-done((f32[3,256]{1,0:T(4,128)S(1)}, f32[3,256]{1,0:T(4,128)S(1)}, u32[]{:S(2)}, u32[]{:S(2)}) %collective-permute-start.19) | collective-permute-done | bytes 3104 | tf_op jit(solution)/shard_map/ppermute | solution.py:119
  188.8 0.6 fusion.93
  (61 shorter events, 1.0 us)
Async XLA Ops:
  0.0 102.6 %copy-start = (bf16[32,4096]{1,0:T(8,128)(2,1)S(1)}, bf16[32,4096]{1,0:T(8,128)(2,1)}, u32[]{:S(2)}) copy-start(bf16[32,4096]{1,0:T(8,128)(2,1)} %param.9) | copy-start | bytes 786436
  0.0 32.4 %copy-start.2 = (bf16[1,384,2048]{2,1,0:T(8,128)(2,1)S(1)}, bf16[1,384,2048]{2,1,0:T(8,128)(2,1)}, u32[]{:S(2)}) copy-start(bf16[1,384,2048]{2,1,0:T(8,128)(2,1)} %param.6) | copy-start | bytes 4718596
  0.0 41.7 %collective-permute-start.4 = (bf16[1024,7168]{1,0:T(8,128)(2,1)}, bf16[1024,7168]{1,0:T(8,128)(2,1)}, u32[]{:S(2)}, u32[]{:S(2)}) collective-permute-start(bf16[1024,7168]{1,0:T(8,128)(2,1)} %bitcast.89), channel_id=1, source_target_pairs={{0,1},{1,0},{2,3},{3,2},{4,5},{5,4},{6,7},{7,6},{8,9},{9,8},{10,11... | collective-permute-start | bytes 44040200 | tf_op jit(solution)/shard_map/ppermute | solution.py:26
  1.6 15.1 %collective-permute-start = (bf16[128,2048]{1,0:T(8,128)(2,1)S(1)}, bf16[128,2048]{1,0:T(8,128)(2,1)S(1)}, u32[]{:S(2)}, u32[]{:S(2)}) collective-permute-start(bf16[128,2048]{1,0:T(8,128)(2,1)S(1)} %slice_bitcast_fusion.8), channel_id=1, source_target_pairs={{2,0},{3,1},{16,18},{17,19},{0,16},{1,17},{18,2},{19,3},{6,4},{7,5... | collective-permute-start | bytes 1572872 | tf_op jit(solution)/shard_map/ppermute | solution.py:46
  18.6 13.8 %collective-permute-start.1 = (bf16[128,2048]{1,0:T(8,128)(2,1)}, bf16[128,2048]{1,0:T(8,128)(2,1)S(1)}, u32[]{:S(2)}, u32[]{:S(2)}) collective-permute-start(bf16[128,2048]{1,0:T(8,128)(2,1)} %slice_select_fusion.1), channel_id=1, source_target_pairs={{2,0},{3,1},{16,18},{17,19},{0,16},{1,17},{18,2},{19,3},{6,4},{7,5... | collective-permute-start | bytes 1572872 | tf_op jit(solution)/shard_map/ppermute | solution.py:50
  20.4 15.2 %collective-permute-start.3 = (bf16[512,512]{1,0:T(8,128)(2,1)}, bf16[512,512]{1,0:T(8,128)(2,1)S(1)}, u32[]{:S(2)}, u32[]{:S(2)}) collective-permute-start(bf16[512,512]{1,0:T(8,128)(2,1)} %bitcast.98), channel_id=1, source_target_pairs={{2,18},{3,19},{16,0},{17,1},{6,22},{7,23},{20,4},{21,5},{10,26},{1... | collective-permute-start | bytes 1572872 | tf_op jit(solution)/shard_map/ppermute | solution.py:84
  21.7 25.5 %collective-permute-start.5 = (bf16[512,512]{1,0:T(8,128)(2,1)}, bf16[512,512]{1,0:T(8,128)(2,1)S(1)}, u32[]{:S(2)}, u32[]{:S(2)}) collective-permute-start(bf16[512,512]{1,0:T(8,128)(2,1)} %bitcast.99), channel_id=1, source_target_pairs={{0,2},{1,3},{18,16},{19,17},{4,6},{5,7},{22,20},{23,21},{8,10},{9,... | collective-permute-start | bytes 1572872 | tf_op jit(solution)/shard_map/ppermute | solution.py:84
  32.4 14.8 %slice-start = ((s8[14680064]{0:T(1024)(128)(4,1)}), s8[4194304]{0:T(1024)(128)(4,1)S(1)}, s32[]{:S(2)}) async-start(s8[14680064]{0:T(1024)(128)(4,1)} %bitcast.91), calls=%async_computation | async-start | bytes 8388608
  32.5 23.3 %collective-permute-start.2 = (bf16[128,2048]{1,0:T(8,128)(2,1)S(1)}, bf16[128,2048]{1,0:T(8,128)(2,1)S(1)}, u32[]{:S(2)}, u32[]{:S(2)}) collective-permute-start(bf16[128,2048]{1,0:T(8,128)(2,1)S(1)} %slice_select_fusion), channel_id=1, source_target_pairs={{2,0},{3,1},{16,18},{17,19},{0,16},{1,17},{18,2},{19,3},{6,4},{7,5... | collective-permute-start | bytes 1572872 | tf_op jit(solution)/shard_map/ppermute | solution.py:50
  35.6 20.2 %collective-permute-start.6 = (bf16[512,512]{1,0:T(8,128)(2,1)S(1)}, bf16[512,512]{1,0:T(8,128)(2,1)S(1)}, u32[]{:S(2)}, u32[]{:S(2)}) collective-permute-start(bf16[512,512]{1,0:T(8,128)(2,1)S(1)} %collective-permute-done.3), channel_id=1, source_target_pairs={{0,2},{1,3},{18,16},{19,17},{4,6},{5,7},{22,20},{23,21},{8,10},{9,... | collective-permute-start | bytes 1572872 | tf_op jit(solution)/shard_map/ppermute | solution.py:87
  37.3 9.9 %slice-start.1 = ((s8[14680064]{0:T(1024)(128)(4,1)}), s8[4194304]{0:T(1024)(128)(4,1)S(1)}, s32[]{:S(2)}) async-start(s8[14680064]{0:T(1024)(128)(4,1)} %bitcast.91), calls=%async_computation.1 | async-start | bytes 8388608
  37.3 9.9 %slice-start.2 = ((s8[14680064]{0:T(1024)(128)(4,1)}), s8[4194304]{0:T(1024)(128)(4,1)S(1)}, s32[]{:S(2)}) async-start(s8[14680064]{0:T(1024)(128)(4,1)} %bitcast.91), calls=%async_computation.2 | async-start | bytes 8388608
  41.7 5.6 %slice-start.3 = ((s8[14680064]{0:T(1024)(128)(4,1)}), s8[2097152]{0:T(1024)(128)(4,1)S(1)}, s32[]{:S(2)}) async-start(s8[14680064]{0:T(1024)(128)(4,1)} %bitcast.91), calls=%async_computation.3 | async-start | bytes 4194304
  47.2 43.0 %collective-permute-start.10 = (bf16[128,3584]{1,0:T(8,128)(2,1)}, bf16[128,3584]{1,0:T(8,128)(2,1)}, u32[]{:S(2)}, u32[]{:S(2)}) collective-permute-start(bf16[128,3584]{1,0:T(8,128)(2,1)} %fusion.19), channel_id=1, source_target_pairs={{0,2},{1,3},{2,0},{3,1},{4,6},{5,7},{6,4},{7,5},{8,10},{9,11},{10,... | collective-permute-start | bytes 2752520 | tf_op jit(solution)/shard_map/ppermute | solution.py:30
  47.2 40.3 %copy-start.4 = (bf16[512,512]{1,0:T(8,128)(2,1)}, bf16[512,512]{1,0:T(8,128)(2,1)S(1)}, u32[]{:S(2)}) copy-start(bf16[512,512]{1,0:T(8,128)(2,1)S(1)} %collective-permute-done.5) | copy-start | bytes 1572868
  53.7 33.7 %collective-permute-start.9 = (bf16[128,3584]{1,0:T(8,128)(2,1)}, bf16[128,3584]{1,0:T(8,128)(2,1)}, u32[]{:S(2)}, u32[]{:S(2)}) collective-permute-start(bf16[128,3584]{1,0:T(8,128)(2,1)} %fusion.16), channel_id=1, source_target_pairs={{0,2},{1,3},{2,0},{3,1},{4,6},{5,7},{6,4},{7,5},{8,10},{9,11},{10,... | collective-permute-start | bytes 2752520 | tf_op jit(solution)/shard_map/ppermute | solution.py:30
  55.7 31.7 %copy-start.6 = (bf16[512,512]{1,0:T(8,128)(2,1)}, bf16[512,512]{1,0:T(8,128)(2,1)S(1)}, u32[]{:S(2)}) copy-start(bf16[512,512]{1,0:T(8,128)(2,1)S(1)} %collective-permute-done.6) | copy-start | bytes 1572868
  55.8 12.9 %collective-permute-start.7 = (bf16[128,2048]{1,0:T(8,128)(2,1)S(1)}, bf16[128,2048]{1,0:T(8,128)(2,1)S(1)}, u32[]{:S(2)}, u32[]{:S(2)}) collective-permute-start(bf16[128,2048]{1,0:T(8,128)(2,1)S(1)} %collective-permute-done.2), channel_id=1, source_target_pairs={{0,16},{1,17},{18,2},{19,3},{4,20},{5,21},{22,6},{23,7},{8,24},{9,... | collective-permute-start | bytes 1572872 | tf_op jit(solution)/shard_map/ppermute | solution.py:54
  68.8 24.6 %collective-permute-start.8 = (bf16[256,2048]{1,0:T(8,128)(2,1)S(1)}, bf16[256,2048]{1,0:T(8,128)(2,1)S(1)}, u32[]{:S(2)}, u32[]{:S(2)}) collective-permute-start(bf16[256,2048]{1,0:T(8,128)(2,1)S(1)} %slice.146), channel_id=1, source_target_pairs={{0,16},{1,17},{18,2},{19,3},{4,20},{5,21},{22,6},{23,7},{8,24},{9,... | collective-permute-start | bytes 3145736 | tf_op jit(solution)/shard_map/ppermute | solution.py:61
  81.2 6.3 %copy-start.3 = (bf16[1,512,512]{2,1,0:T(8,128)(2,1)S(1)}, bf16[1,512,512]{2,1,0:T(8,128)(2,1)}, u32[]{:S(2)}) copy-start(bf16[1,512,512]{2,1,0:T(8,128)(2,1)} %param.11) | copy-start | bytes 1572868
  87.7 26.9 %collective-permute-start.13 = (bf16[2,512,512]{2,1,0:T(8,128)(2,1)S(1)}, bf16[2,512,512]{2,1,0:T(8,128)(2,1)S(1)}, u32[]{:S(2)}, u32[]{:S(2)}) collective-permute-start(bf16[2,512,512]{2,1,0:T(8,128)(2,1)S(1)} %maximum_select_fusion.2), channel_id=1, source_target_pairs={{0,16},{1,17},{18,2},{19,3},{2,18},{3,19},{16,0},{17,1},{4,20},{5,... | collective-permute-start | bytes 3145736 | tf_op jit(solution)/shard_map/ppermute | solution.py:98
  90.2 40.3 %collective-permute-start.11 = (bf16[128,7168]{1,0:T(8,128)(2,1)}, bf16[128,7168]{1,0:T(8,128)(2,1)}, u32[]{:S(2)}, u32[]{:S(2)}) collective-permute-start(bf16[128,7168]{1,0:T(8,128)(2,1)} %fusion), channel_id=1, source_target_pairs={{0,2},{1,3},{2,0},{3,1},{4,6},{5,7},{6,4},{7,5},{8,10},{9,11},{10,... | collective-permute-start | bytes 5505032 | tf_op jit(solution)/shard_map/ppermute | solution.py:30
  102.6 12.0 %copy-start.5 = (bf16[512,512]{1,0:T(8,128)(2,1)S(1)}, bf16[512,512]{1,0:T(8,128)(2,1)}, u32[]{:S(2)}) copy-start(bf16[512,512]{1,0:T(8,128)(2,1)} %copy-done.4) | copy-start | bytes 1572868
  102.6 12.0 %copy-start.7 = (bf16[512,512]{1,0:T(8,128)(2,1)S(1)}, bf16[512,512]{1,0:T(8,128)(2,1)}, u32[]{:S(2)}) copy-start(bf16[512,512]{1,0:T(8,128)(2,1)} %copy-done.6) | copy-start | bytes 1572868
  103.1 11.4 %collective-permute-start.12 = (f32[384,32]{0,1:T(8,128)S(1)}, f32[384,32]{0,1:T(8,128)S(1)}, u32[]{:S(2)}, u32[]{:S(2)}) collective-permute-start(f32[384,32]{0,1:T(8,128)S(1)} %fusion.81), channel_id=1, source_target_pairs={{0,16},{16,0},{1,17},{17,1},{2,18},{18,2},{3,19},{19,3},{4,20},{20... | collective-permute-start | bytes 147464 | tf_op jit(solution)/shard_map/ppermute | solution.py:184
  116.6 28.9 %copy-start.8 = (bf16[32,7168]{1,0:T(8,128)(2,1)S(1)}, bf16[32,7168]{1,0:T(8,128)(2,1)}, u32[]{:S(2)}) copy-start(bf16[32,7168]{1,0:T(8,128)(2,1)} %param.10) | copy-start | bytes 1376260
  116.6 33.4 %collective-permute-start.14 = (bf16[2,2,512,512]{3,2,1,0:T(8,128)(2,1)}, bf16[2,2,512,512]{3,2,1,0:T(8,128)(2,1)S(1)}, u32[]{:S(2)}, u32[]{:S(2)}) collective-permute-start(bf16[2,2,512,512]{3,2,1,0:T(8,128)(2,1)} %maximum_select_fusion), channel_id=1, source_target_pairs={{0,1},{1,0},{2,3},{3,2},{4,5},{5,4},{6,7},{7,6},{8,9},{9,8},{10,11... | collective-permute-start | bytes 6291464 | tf_op jit(solution)/shard_map/ppermute | solution.py:102
  130.5 41.7 %collective-permute-start.16 = (bf16[32,7168]{1,0:T(8,128)(2,1)}, bf16[32,7168]{1,0:T(8,128)(2,1)}, u32[]{:S(2)}, u32[]{:S(2)}) collective-permute-start(bf16[32,7168]{1,0:T(8,128)(2,1)} %slice.190), channel_id=1, source_target_pairs={{0,2},{1,3},{2,0},{3,1},{4,6},{5,7},{6,4},{7,5},{8,10},{9,11},{10,... | collective-permute-start | bytes 1376264 | tf_op jit(solution)/shard_map/ppermute | solution.py:30
  131.0 38.8 %collective-permute-start.15 = (bf16[96,7168]{1,0:T(8,128)(2,1)}, bf16[96,7168]{1,0:T(8,128)(2,1)}, u32[]{:S(2)}, u32[]{:S(2)}) collective-permute-start(bf16[96,7168]{1,0:T(8,128)(2,1)} %slice.189), channel_id=1, source_target_pairs={{0,2},{1,3},{2,0},{3,1},{4,6},{5,7},{6,4},{7,5},{8,10},{9,11},{10,... | collective-permute-start | bytes 4128776 | tf_op jit(solution)/shard_map/ppermute | solution.py:30
  150.4 2.6 %slice-start.4 = ((s8[5505024]{0:T(1024)(128)(4,1)}), s8[4194304]{0:T(1024)(128)(4,1)S(1)}, s32[]{:S(2)}) async-start(s8[5505024]{0:T(1024)(128)(4,1)} %bitcast.111), calls=%async_computation.4 | async-start | bytes 8388608
  150.7 2.7 %slice-start.5 = ((s8[5505024]{0:T(1024)(128)(4,1)}), s8[1310720]{0:T(1024)(128)(4,1)S(1)}, s32[]{:S(2)}) async-start(s8[5505024]{0:T(1024)(128)(4,1)} %bitcast.111), calls=%async_computation.5 | async-start | bytes 2621440
  150.9 2.7 %copy-start.9 = (bf16[32,7168]{1,0:T(8,128)(2,1)S(1)}, bf16[32,7168]{1,0:T(8,128)(2,1)}, u32[]{:S(2)}) copy-start(bf16[32,7168]{1,0:T(8,128)(2,1)} %param.10) | copy-start | bytes 1376260
  174.1 15.3 %copy-start.1 = (bf16[32,4096]{1,0:T(8,128)(2,1)S(1)}, bf16[32,4096]{1,0:T(8,128)(2,1)}, u32[]{:S(2)}) copy-start(bf16[32,4096]{1,0:T(8,128)(2,1)} %param.9) | copy-start | bytes 786436
  176.6 3.8 %collective-permute-start.17 = (f32[3,1024]{1,0:T(4,128)S(1)}, f32[3,1024]{1,0:T(4,128)S(1)}, u32[]{:S(2)}, u32[]{:S(2)}) collective-permute-start(f32[3,1024]{1,0:T(4,128)S(1)} %bitcast.108), channel_id=1, source_target_pairs={{0,16},{16,0},{1,17},{17,1},{2,18},{18,2},{3,19},{19,3},{4,20},{20... | collective-permute-start | bytes 36872 | tf_op jit(solution)/shard_map/ppermute | solution.py:119
  180.4 5.5 %collective-permute-start.18 = (f32[3,256]{1,0:T(4,128)S(1)}, f32[3,256]{1,0:T(4,128)S(1)}, u32[]{:S(2)}, u32[]{:S(2)}) collective-permute-start(f32[3,256]{1,0:T(4,128)S(1)} %get-tuple-element.89), channel_id=1, source_target_pairs={{0,4},{4,8},{8,12},{12,0},{1,5},{5,9},{9,13},{13,1},{2,6},{6,10},{... | collective-permute-start | bytes 9224 | tf_op jit(solution)/shard_map/ppermute | solution.py:119
  182.0 3.8 %collective-permute-start.20 = (f32[3,256]{1,0:T(4,128)S(1)}, f32[3,256]{1,0:T(4,128)S(1)}, u32[]{:S(2)}, u32[]{:S(2)}) collective-permute-start(f32[3,256]{1,0:T(4,128)S(1)} %get-tuple-element.90), channel_id=1, source_target_pairs={{0,12},{4,0},{8,4},{12,8},{1,13},{5,1},{9,5},{13,9},{2,14},{6,2},{... | collective-permute-start | bytes 9224 | tf_op jit(solution)/shard_map/ppermute | solution.py:119
  184.3 4.5 %collective-permute-start.19 = (f32[3,256]{1,0:T(4,128)S(1)}, f32[3,256]{1,0:T(4,128)S(1)}, u32[]{:S(2)}, u32[]{:S(2)}) collective-permute-start(f32[3,256]{1,0:T(4,128)S(1)} %get-tuple-element.91), channel_id=1, source_target_pairs={{0,8},{4,12},{8,0},{12,4},{1,9},{5,13},{9,1},{13,5},{2,10},{6,14},... | collective-permute-start | bytes 9224 | tf_op jit(solution)/shard_map/ppermute | solution.py:119

commit v4 on v3

--- a/solution.py
+++ b/solution.py
@@ -171,7 +171,6 @@
         part_e = [value[most:] for value in part_de]
         got_c = send(part_c, got_a + got_b + part_d + part_e)
         got_d = send(part_d, got_c)
-        got_e = send(part_e, got_c)
         mark_rows = assemble(got_b[0])
         mine, theirs = split(own(part_c[0], got_b[0]))
         own_part = dot(mine, weight, ((1,), (0,)))
@@ -187,6 +186,7 @@
         theirs = after(theirs, own_part, *got_c)
         own_part = own_part + dot(theirs, weight_sibling, ((1,), (0,)))
         own_part, left = lax.optimization_barrier((own_part, left))
+        got_e = send(part_e, got_c + [own_part])
 
         def right_part(got, lo, hi, h0=0, h1=hidden):
             preact = own_part[lo:hi, h0:h1]

time: 190 us -> 186 us (0.979)
  waiting for transfers between devices: 70.2 us -> 67.6 us
    ppermute x5, waiting for transfers between devices: 31.6 us -> 29 us  [shift_x(): lax.ppermute(value, 'dp', [(i, (i + 2 * shift) % n_dp) for i in range(n_d...]
  transfers between devices with their start and end apart: 21 -> 21, of which waited for: 11 -> 12; matrix products, arithmetic and copies ran while one was open for 41% -> 42% of each run, Pallas kernels for 0% -> 0%
where the time goes in v4:
time: 186 us
  matrix products  71.1 us (38%)
  waiting for transfers between devices  67.6 us (36%)
  starting transfers between devices  34 us (18%)
  other arithmetic  7.67 us (4%)
  local copies, waits for them, and re-layouts  5.01 us (3%)
    dot_general x17, matrix products, dot(): return lax.dot_general(a, b, (dims, ((), ())), preferred_element_type=F32)  70.8 us
    ppermute x5, waiting for transfers between devices, shift_x(): lax.ppermute(value, 'dp', [(i, (i + 2 * shift) % n_dp) for i in range(n_d...  29 us
    ppermute x1, waiting for transfers between devices, spread(): stages = [lax.ppermute(rows[first[0]:first[1]], both, off_x + on_y)]  12.4 us
    ppermute x1, waiting for transfers between devices, per_device(): left = left + lax.ppermute(left, 'fsdp', [(0, 1), (1, 0)])  8.82 us
    ppermute x4, waiting for transfers between devices, scatter_sum(): lax.ppermute(block, axis_name, [(i, (i + shift) % size) for i in range(si...  6.58 us
    ppermute x2, waiting for transfers between devices, spread(): stages.append(lax.ppermute(operand, both, off_x + on_y))  6.16 us
    ppermute x2, starting transfers between devices, start_landmarks(): return [lax.ppermute(marks, both, off_y), lax.ppermute(marks, both, on_x)]  5.86 us
    ppermute x4, starting transfers between devices, scatter_sum(): lax.ppermute(block, axis_name, [(i, (i + shift) % size) for i in range(si...  5.61 us
  transfers between devices with their start and end apart: 21, of which 12 were waited for; matrix products, arithmetic and copies ran while one was open for 42% of the time, Pallas kernels for 0%

profile of v4, /device:TPU:0, one launch (start us, length us, event | category | flops | bytes accessed | tf_op | source)
XLA Modules:
  0.0 185.9 jit_solution(9106222139260384432)
XLA Ops:
  0.0 0.5 collective-permute-start.4
  0.5 1.1 slice_bitcast_fusion.8
  1.6 2.7 %collective-permute-start = (bf16[128,2048]{1,0:T(8,128)(2,1)S(1)}, bf16[128,2048]{1,0:T(8,128)(2,1)S(1)}, u32[]{:S(2)}, u32[]{:S(2)}) collective-permute-start(bf16[128,2048]{1,0:T(8,128)(2,1)S(1)} %slice_bitcast_fusion.8), channel_id=1, source_target_pairs={{2,0},{3,1},{16,18},{17,19},{0,16},{1,17},{18,2},{19,3},{6,4},{7,5... | collective-permute-start | bytes 1572872 | tf_op jit(solution)/shard_map/ppermute | solution.py:46
  4.3 12.4 %collective-permute-done = bf16[128,2048]{1,0:T(8,128)(2,1)S(1)} collective-permute-done((bf16[128,2048]{1,0:T(8,128)(2,1)S(1)}, bf16[128,2048]{1,0:T(8,128)(2,1)S(1)}, u32[]{:S(2)}, u32[]{:S(2)}) %collective-permute-start) | collective-permute-done | bytes 524320 | tf_op jit(solution)/shard_map/ppermute | solution.py:46
  16.7 1.9 %slice_select_fusion.1 = bf16[128,2048]{1,0:T(8,128)(2,1)} fusion(bf16[128,2048]{1,0:T(8,128)(2,1)S(1)} %collective-permute-done, bf16[384,2048]{1,0:T(8,128)(2,1)} %bitcast.94, pred[]{:T(512)S(6)} %eq.7), kind=kLoop, calls=%fused_computation.63 | loop fusion | flops 262144 | bytes 1572865 | tf_op jit(solution)/shard_map/jit(_where)/select_n | solution.py:49
  18.6 1.8 collective-permute-start.1
  20.4 1.3 collective-permute-start.3
  21.7 4.6 %collective-permute-start.5 = (bf16[512,512]{1,0:T(8,128)(2,1)}, bf16[512,512]{1,0:T(8,128)(2,1)S(1)}, u32[]{:S(2)}, u32[]{:S(2)}) collective-permute-start(bf16[512,512]{1,0:T(8,128)(2,1)} %bitcast.99), channel_id=1, source_target_pairs={{0,2},{1,3},{18,16},{19,17},{4,6},{5,7},{22,20},{23,21},{8,10},{9,... | collective-permute-start | bytes 1572872 | tf_op jit(solution)/shard_map/ppermute | solution.py:84
  26.3 6.2 %collective-permute-done.1 = bf16[128,2048]{1,0:T(8,128)(2,1)S(1)} collective-permute-done((bf16[128,2048]{1,0:T(8,128)(2,1)}, bf16[128,2048]{1,0:T(8,128)(2,1)S(1)}, u32[]{:S(2)}, u32[]{:S(2)}) %collective-permute-start.1) | collective-permute-done | bytes 524320 | tf_op jit(solution)/shard_map/ppermute | solution.py:50
  32.5 1.6 collective-permute-start.2
  34.1 1.5 collective-permute-done.3
  35.6 1.7 collective-permute-start.6
  37.3 4.4 %fusion.8 = f32[128,3584]{1,0:T(8,128)S(1)} fusion(bf16[1024,7168]{1,0:T(8,128)(2,1)} %bitcast.90, pred[]{:T(512)S(6)} %eq.6, bf16[128,2048]{1,0:T(8,128)(2,1)S(1)} %broadcast_select_fusion.6), kind=kOutput, calls=%fused_computation.11 | convolution fusion | flops 939655168 | bytes 9699329 | tf_op jit(solution)/shard_map/dot_general | solution.py:14
  41.7 5.4 %fusion.19 = bf16[128,3584]{1,0:T(8,128)(2,1)} fusion(f32[128,3584]{1,0:T(8,128)S(1)} %fusion.8, bf16[1024,7168]{1,0:T(8,128)(2,1)} %collective-permute-done.4, pred[]{:T(512)S(6)} %eq.6, bf16[128,2048]{1,0:T(8,128)(2,1)S(1)} %broadcast_select_fusion.6), kind=kOutput, calls=%fused_computation.16 | convolution fusion | flops 940572672 | bytes 10616833 | tf_op jit(solution)/shard_map/dot_general | solution.py:14
  47.3 1.1 fusion.4
  48.4 5.3 %fusion.16 = bf16[128,3584]{1,0:T(8,128)(2,1)} fusion(f32[128,3584]{1,0:T(8,128)S(1)} %fusion.4, bf16[1024,7168]{1,0:T(8,128)(2,1)} %collective-permute-done.4, pred[]{:T(512)S(6)} %eq.6, bf16[128,2048]{1,0:T(8,128)(2,1)S(1)} %broadcast_select_fusion.5), kind=kOutput, calls=%fused_computation.15 | convolution fusion | flops 940572672 | bytes 10616833 | tf_op jit(solution)/shard_map/dot_general | solution.py:14
  53.7 2.0 %collective-permute-start.9 = (bf16[128,3584]{1,0:T(8,128)(2,1)}, bf16[128,3584]{1,0:T(8,128)(2,1)}, u32[]{:S(2)}, u32[]{:S(2)}) collective-permute-start(bf16[128,3584]{1,0:T(8,128)(2,1)} %fusion.16), channel_id=1, source_target_pairs={{0,2},{1,3},{2,0},{3,1},{4,6},{5,7},{6,4},{7,5},{8,10},{9,11},{10,... | collective-permute-start | bytes 2752520 | tf_op jit(solution)/shard_map/ppermute | solution.py:30
  55.8 2.2 %collective-permute-start.7 = (bf16[128,2048]{1,0:T(8,128)(2,1)S(1)}, bf16[128,2048]{1,0:T(8,128)(2,1)S(1)}, u32[]{:S(2)}, u32[]{:S(2)}) collective-permute-start(bf16[128,2048]{1,0:T(8,128)(2,1)S(1)} %collective-permute-done.2), channel_id=1, source_target_pairs={{0,16},{1,17},{18,2},{19,3},{4,20},{5,21},{22,6},{23,7},{8,24},{9,... | collective-permute-start | bytes 1572872 | tf_op jit(solution)/shard_map/ppermute | solution.py:54
  58.1 2.1 %fusion.49 = f32[128,7168]{1,0:T(8,128)S(1)} fusion(pred[]{:T(512)S(6)} %eq.6, bf16[128,2048]{1,0:T(8,128)(2,1)S(1)} %broadcast_select_fusion.4, bf16[1,1024,7168]{2,1,0:T(8,128)(2,1)S(1)} %bitcast.92), kind=kOutput, calls=%fused_computation.74 | convolution fusion | flops 1879179264 | bytes 18874368 | tf_op jit(solution)/shard_map/dot_general | solution.py:14
  60.1 8.5 %fusion = bf16[128,7168]{1,0:T(8,128)(2,1)} fusion(f32[128,7168]{1,0:T(8,128)S(1)} %fusion.49, bf16[1024,7168]{1,0:T(8,128)(2,1)} %collective-permute-done.4, pred[]{:T(512)S(6)} %eq.6, bf16[128,2048]{1,0:T(8,128)(2,1)S(1)} %broadcast_select_fusion.4), kind=kOutput, calls=%fused_computation.3 | convolution fusion | flops 1881014272 | bytes 20709376 | tf_op jit(solution)/shard_map/dot_general | solution.py:14
  68.8 3.0 %collective-permute-start.8 = (bf16[256,2048]{1,0:T(8,128)(2,1)S(1)}, bf16[256,2048]{1,0:T(8,128)(2,1)S(1)}, u32[]{:S(2)}, u32[]{:S(2)}) collective-permute-start(bf16[256,2048]{1,0:T(8,128)(2,1)S(1)} %slice.146), channel_id=1, source_target_pairs={{0,16},{1,17},{18,2},{19,3},{4,20},{5,21},{22,6},{23,7},{8,24},{9,... | collective-permute-start | bytes 3145736 | tf_op jit(solution)/shard_map/ppermute | solution.py:61
  71.8 2.1 %fusion.46 = f32[128,7168]{1,0:T(8,128)S(1)} fusion(pred[]{:T(512)S(6)} %eq.6, bf16[128,2048]{1,0:T(8,128)(2,1)S(1)} %broadcast_select_fusion.3, bf16[1,1024,7168]{2,1,0:T(8,128)(2,1)S(1)} %bitcast.92), kind=kOutput, calls=%fused_computation.71 | convolution fusion | flops 1879179264 | bytes 18874368 | tf_op jit(solution)/shard_map/dot_general | solution.py:14
  73.9 7.3 %fusion.1 = bf16[128,7168]{1,0:T(8,128)(2,1)S(1)} fusion(f32[128,7168]{1,0:T(8,128)S(1)} %fusion.46, bf16[1024,7168]{1,0:T(8,128)(2,1)} %collective-permute-done.4, pred[]{:T(512)S(6)} %eq.6, bf16[128,2048]{1,0:T(8,128)(2,1)S(1)} %broadcast_select_fusion.3), kind=kOutput, calls=%fused_computation.4 | convolution fusion | flops 1881014272 | bytes 20709376 | tf_op jit(solution)/shard_map/dot_general | solution.py:14
  81.2 0.8 slice.190
  82.0 1.2 slice.189
  83.2 4.2 %collective-permute-done.9 = bf16[128,3584]{1,0:T(8,128)(2,1)} collective-permute-done((bf16[128,3584]{1,0:T(8,128)(2,1)}, bf16[128,3584]{1,0:T(8,128)(2,1)}, u32[]{:S(2)}, u32[]{:S(2)}) %collective-permute-start.9) | collective-permute-done | bytes 917536 | tf_op jit(solution)/shard_map/ppermute | solution.py:30
  87.5 0.2 maximum_select_fusion.2
  87.7 2.5 %collective-permute-start.13 = (bf16[2,512,512]{2,1,0:T(8,128)(2,1)S(1)}, bf16[2,512,512]{2,1,0:T(8,128)(2,1)S(1)}, u32[]{:S(2)}, u32[]{:S(2)}) collective-permute-start(bf16[2,512,512]{2,1,0:T(8,128)(2,1)S(1)} %maximum_select_fusion.2), channel_id=1, source_target_pairs={{0,16},{1,17},{18,2},{19,3},{2,18},{3,19},{16,0},{17,1},{4,20},{5,... | collective-permute-start | bytes 3145736 | tf_op jit(solution)/shard_map/ppermute | solution.py:98
  90.3 3.1 %collective-permute-done.8 = bf16[256,2048]{1,0:T(8,128)(2,1)S(1)} collective-permute-done((bf16[256,2048]{1,0:T(8,128)(2,1)S(1)}, bf16[256,2048]{1,0:T(8,128)(2,1)S(1)}, u32[]{:S(2)}, u32[]{:S(2)}) %collective-permute-start.8) | collective-permute-done | bytes 1048608 | tf_op jit(solution)/shard_map/ppermute | solution.py:61
  93.4 0.6 maximum_select_fusion.1
  94.0 8.6 %fusion.38 = f32[384,7168]{1,0:T(8,128)} fusion(pred[]{:T(512)S(6)} %eq.6, bf16[384,2048]{1,0:T(8,128)(2,1)S(1)} %maximum_select_fusion.1, bf16[1,1024,7168]{2,1,0:T(8,128)(2,1)S(1)} %bitcast.92), kind=kOutput, calls=%fused_computation.48 | convolution fusion | flops 5637537792 | bytes 27262976 | tf_op jit(solution)/shard_map/dot_general | solution.py:14
  102.6 0.6 fusion.81
  103.1 2.5 %collective-permute-start.12 = (f32[384,32]{0,1:T(8,128)S(1)}, f32[384,32]{0,1:T(8,128)S(1)}, u32[]{:S(2)}, u32[]{:S(2)}) collective-permute-start(f32[384,32]{0,1:T(8,128)S(1)} %fusion.81), channel_id=1, source_target_pairs={{0,16},{16,0},{1,17},{17,1},{2,18},{18,2},{3,19},{19,3},{4,20},{20... | collective-permute-start | bytes 147464 | tf_op jit(solution)/shard_map/ppermute | solution.py:183
  105.7 8.8 %collective-permute-done.12 = f32[384,32]{0,1:T(8,128)S(1)} collective-permute-done((f32[384,32]{0,1:T(8,128)S(1)}, f32[384,32]{0,1:T(8,128)S(1)}, u32[]{:S(2)}, u32[]{:S(2)}) %collective-permute-start.12) | collective-permute-done | bytes 49184 | tf_op jit(solution)/shard_map/ppermute | solution.py:183
  114.6 0.3 select_bitcast_fusion.1
  114.9 1.6 maximum_select_fusion
  116.6 13.9 %collective-permute-done.11 = bf16[128,7168]{1,0:T(8,128)(2,1)} collective-permute-done((bf16[128,7168]{1,0:T(8,128)(2,1)}, bf16[128,7168]{1,0:T(8,128)(2,1)}, u32[]{:S(2)}, u32[]{:S(2)}) %collective-permute-start.11) | collective-permute-done | bytes 1835040 | tf_op jit(solution)/shard_map/ppermute | solution.py:30
  130.5 0.6 collective-permute-start.15
  131.0 13.0 %convolution_add_fusion = f32[384,7168]{1,0:T(8,128)S(1)} fusion(f32[384,7168]{1,0:T(8,128)} %fusion.38, bf16[384,1024]{1,0:T(8,128)(2,1)S(1)} %broadcast_select_fusion.2, bf16[1024,7168]{1,0:T(8,128)(2,1)} %collective-permute-done.4), kind=kOutput, calls=%fused_computation | convolution fusion | flops 5639897088 | bytes 37486592 | tf_op jit(solution)/shard_map/dot_general | solution.py:14
  144.0 1.5 collective-permute-start.16
  145.5 2.2 %fusion.37 = f32[128,32]{0,1:T(8,128)S(1)} fusion(bf16[128,3584]{1,0:T(8,128)(2,1)} %collective-permute-done.9, f32[384,7168]{1,0:T(8,128)S(1)} %convolution_add_fusion, bf16[384,7168]{1,0:T(8,128)(2,1)} %bitcast.109, bf16[32,7168]{1,0:T(8,128)(2,1)S(1)} %copy-done.8), kind=kOutput, calls=%fused_computation.47 | convolution fusion | flops 33488896 | bytes 3915776 | tf_op jit(solution)/shard_map/dot_general | solution.py:14
  147.7 2.2 %convolution_add_fusion.3 = f32[128,32]{0,1:T(8,128)S(1)} fusion(f32[128,32]{0,1:T(8,128)S(1)} %fusion.37, bf16[128,3584]{1,0:T(8,128)(2,1)} %collective-permute-done.10, f32[384,7168]{1,0:T(8,128)S(1)} %convolution_add_fusion, bf16[384,7168]{1,0:T(8,128)(2,1)} %bitcast.110, bf16[32,7168]{1,0:T(8,128)(2,1)S(1)} %copy-done.8), kind=kOutput, calls=%fused_computation.37 | convolution fusion | flops 33492992 | bytes 3932160 | tf_op jit(solution)/shard_map/dot_general | solution.py:14
  150.0 0.5 broadcast_select_fusion
  150.5 0.3 slice_bitcast_fusion.1
  150.8 0.1 pad_maximum_fusion.3
  151.1 0.1 pad_maximum_fusion
  151.2 1.1 pad_maximum_fusion.2
  152.3 0.7 slice-done.4
  153.0 0.5 slice-done.5
  153.6 2.8 %fusion.32 = f32[128,32]{0,1:T(8,128)S(1)} fusion(bf16[32,7168]{1,0:T(8,128)(2,1)S(1)} %copy-done.9, bf16[128,7168]{1,0:T(8,128)(2,1)} %collective-permute-done.11, f32[384,7168]{1,0:T(8,128)S(1)} %convolution_add_fusion, bf16[1,384,7168]{2,1,0:T(8,128)(2,1)S(1)} %bitcast.112), kind=kOutput, calls=%fused_computation.34 | convolution fusion | flops 66977792 | bytes 7815168 | tf_op jit(solution)/shard_map/dot_general | solution.py:14
  156.4 7.5 %collective-permute-done.15 = bf16[96,7168]{1,0:T(8,128)(2,1)} collective-permute-done((bf16[96,7168]{1,0:T(8,128)(2,1)}, bf16[96,7168]{1,0:T(8,128)(2,1)}, u32[]{:S(2)}, u32[]{:S(2)}) %collective-permute-start.15) | collective-permute-done | bytes 1376288 | tf_op jit(solution)/shard_map/ppermute | solution.py:30
  163.9 2.4 %fusion.34 = f32[96,32]{0,1:T(8,128)S(1)} fusion(bf16[32,7168]{1,0:T(8,128)(2,1)S(1)} %copy-done.9, bf16[96,7168]{1,0:T(8,128)(2,1)} %collective-permute-done.15, f32[384,7168]{1,0:T(8,128)S(1)} %convolution_add_fusion, bf16[1,384,7168]{2,1,0:T(8,128)(2,1)S(1)} %bitcast.112), kind=kOutput, calls=%fused_computation.36 | convolution fusion | flops 50233344 | bytes 5976064 | tf_op jit(solution)/shard_map/dot_general | solution.py:14
  166.3 3.4 %collective-permute-done.16 = bf16[32,7168]{1,0:T(8,128)(2,1)S(1)} collective-permute-done((bf16[32,7168]{1,0:T(8,128)(2,1)}, bf16[32,7168]{1,0:T(8,128)(2,1)S(1)}, u32[]{:S(2)}, u32[]{:S(2)}) %collective-permute-start.16) | collective-permute-done | bytes 458784 | tf_op jit(solution)/shard_map/ppermute | solution.py:30
  169.7 0.5 fusion.43
  170.1 0.3 fusion.83
  170.6 2.4 %fusion.22 = f32[6,2048]{1,0:T(8,128)S(1)} fusion(bf16[512,1024]{1,0:T(8,128)(2,1)S(1)} %pad_maximum_fusion.3, bf16[512,1024]{1,0:T(8,128)(2,1)} %pad_maximum_fusion.2, bf16[512,1024]{1,0:T(8,128)(2,1)S(1)} %pad_maximum_fusion.1, bf16[512,1024]{1,0:T(8,128)(2,1)S(1)} %pad_maximum_fusion, bf16[3,1024]{1,0:T(4,128)(2,1)S(1)} %get-tuple-element.93, ...), kind=kOutput, calls=%fused_computation.17 | convolution fusion | flops 41967616 | bytes 4255744 | tf_op jit(solution)/shard_map/dot_general | solution.py:14
  173.1 0.9 collective-permute-start.17
  174.0 2.9 %collective-permute-done.17 = f32[3,1024]{1,0:T(4,128)S(1)} collective-permute-done((f32[3,1024]{1,0:T(4,128)S(1)}, f32[3,1024]{1,0:T(4,128)S(1)}, u32[]{:S(2)}, u32[]{:S(2)}) %collective-permute-start.17) | collective-permute-done | bytes 12320 | tf_op jit(solution)/shard_map/ppermute | solution.py:119
  176.9 1.6 collective-permute-start.18
  178.5 2.2 %collective-permute-start.20 = (f32[3,256]{1,0:T(4,128)S(1)}, f32[3,256]{1,0:T(4,128)S(1)}, u32[]{:S(2)}, u32[]{:S(2)}) collective-permute-start(f32[3,256]{1,0:T(4,128)S(1)} %get-tuple-element.90), channel_id=1, source_target_pairs={{0,12},{4,0},{8,4},{12,8},{1,13},{5,1},{9,5},{13,9},{2,14},{6,2},{... | collective-permute-start | bytes 9224 | tf_op jit(solution)/shard_map/ppermute | solution.py:119
  180.8 0.8 collective-permute-start.19
  181.6 0.8 collective-permute-done.18
  182.4 2.9 %collective-permute-done.19 = f32[3,256]{1,0:T(4,128)S(1)} collective-permute-done((f32[3,256]{1,0:T(4,128)S(1)}, f32[3,256]{1,0:T(4,128)S(1)}, u32[]{:S(2)}, u32[]{:S(2)}) %collective-permute-start.19) | collective-permute-done | bytes 3104 | tf_op jit(solution)/shard_map/ppermute | solution.py:119
  185.3 0.6 fusion.93
  (61 shorter events, 1.1 us)
Async XLA Ops:
  0.0 102.6 %copy-start = (bf16[32,4096]{1,0:T(8,128)(2,1)S(1)}, bf16[32,4096]{1,0:T(8,128)(2,1)}, u32[]{:S(2)}) copy-start(bf16[32,4096]{1,0:T(8,128)(2,1)} %param.9) | copy-start | bytes 786436
  0.0 32.4 %copy-start.2 = (bf16[1,384,2048]{2,1,0:T(8,128)(2,1)S(1)}, bf16[1,384,2048]{2,1,0:T(8,128)(2,1)}, u32[]{:S(2)}) copy-start(bf16[1,384,2048]{2,1,0:T(8,128)(2,1)} %param.6) | copy-start | bytes 4718596
  0.0 41.7 %collective-permute-start.4 = (bf16[1024,7168]{1,0:T(8,128)(2,1)}, bf16[1024,7168]{1,0:T(8,128)(2,1)}, u32[]{:S(2)}, u32[]{:S(2)}) collective-permute-start(bf16[1024,7168]{1,0:T(8,128)(2,1)} %bitcast.89), channel_id=1, source_target_pairs={{0,1},{1,0},{2,3},{3,2},{4,5},{5,4},{6,7},{7,6},{8,9},{9,8},{10,11... | collective-permute-start | bytes 44040200 | tf_op jit(solution)/shard_map/ppermute | solution.py:26
  1.6 15.1 %collective-permute-start = (bf16[128,2048]{1,0:T(8,128)(2,1)S(1)}, bf16[128,2048]{1,0:T(8,128)(2,1)S(1)}, u32[]{:S(2)}, u32[]{:S(2)}) collective-permute-start(bf16[128,2048]{1,0:T(8,128)(2,1)S(1)} %slice_bitcast_fusion.8), channel_id=1, source_target_pairs={{2,0},{3,1},{16,18},{17,19},{0,16},{1,17},{18,2},{19,3},{6,4},{7,5... | collective-permute-start | bytes 1572872 | tf_op jit(solution)/shard_map/ppermute | solution.py:46
  18.6 13.8 %collective-permute-start.1 = (bf16[128,2048]{1,0:T(8,128)(2,1)}, bf16[128,2048]{1,0:T(8,128)(2,1)S(1)}, u32[]{:S(2)}, u32[]{:S(2)}) collective-permute-start(bf16[128,2048]{1,0:T(8,128)(2,1)} %slice_select_fusion.1), channel_id=1, source_target_pairs={{2,0},{3,1},{16,18},{17,19},{0,16},{1,17},{18,2},{19,3},{6,4},{7,5... | collective-permute-start | bytes 1572872 | tf_op jit(solution)/shard_map/ppermute | solution.py:50
  20.4 15.2 %collective-permute-start.3 = (bf16[512,512]{1,0:T(8,128)(2,1)}, bf16[512,512]{1,0:T(8,128)(2,1)S(1)}, u32[]{:S(2)}, u32[]{:S(2)}) collective-permute-start(bf16[512,512]{1,0:T(8,128)(2,1)} %bitcast.98), channel_id=1, source_target_pairs={{2,18},{3,19},{16,0},{17,1},{6,22},{7,23},{20,4},{21,5},{10,26},{1... | collective-permute-start | bytes 1572872 | tf_op jit(solution)/shard_map/ppermute | solution.py:84
  21.7 25.5 %collective-permute-start.5 = (bf16[512,512]{1,0:T(8,128)(2,1)}, bf16[512,512]{1,0:T(8,128)(2,1)S(1)}, u32[]{:S(2)}, u32[]{:S(2)}) collective-permute-start(bf16[512,512]{1,0:T(8,128)(2,1)} %bitcast.99), channel_id=1, source_target_pairs={{0,2},{1,3},{18,16},{19,17},{4,6},{5,7},{22,20},{23,21},{8,10},{9,... | collective-permute-start | bytes 1572872 | tf_op jit(solution)/shard_map/ppermute | solution.py:84
  32.4 14.8 %slice-start = ((s8[14680064]{0:T(1024)(128)(4,1)}), s8[4194304]{0:T(1024)(128)(4,1)S(1)}, s32[]{:S(2)}) async-start(s8[14680064]{0:T(1024)(128)(4,1)} %bitcast.91), calls=%async_computation | async-start | bytes 8388608
  32.5 23.3 %collective-permute-start.2 = (bf16[128,2048]{1,0:T(8,128)(2,1)S(1)}, bf16[128,2048]{1,0:T(8,128)(2,1)S(1)}, u32[]{:S(2)}, u32[]{:S(2)}) collective-permute-start(bf16[128,2048]{1,0:T(8,128)(2,1)S(1)} %slice_select_fusion), channel_id=1, source_target_pairs={{2,0},{3,1},{16,18},{17,19},{0,16},{1,17},{18,2},{19,3},{6,4},{7,5... | collective-permute-start | bytes 1572872 | tf_op jit(solution)/shard_map/ppermute | solution.py:50
  35.6 20.2 %collective-permute-start.6 = (bf16[512,512]{1,0:T(8,128)(2,1)S(1)}, bf16[512,512]{1,0:T(8,128)(2,1)S(1)}, u32[]{:S(2)}, u32[]{:S(2)}) collective-permute-start(bf16[512,512]{1,0:T(8,128)(2,1)S(1)} %collective-permute-done.3), channel_id=1, source_target_pairs={{0,2},{1,3},{18,16},{19,17},{4,6},{5,7},{22,20},{23,21},{8,10},{9,... | collective-permute-start | bytes 1572872 | tf_op jit(solution)/shard_map/ppermute | solution.py:87
  37.3 9.9 %slice-start.1 = ((s8[14680064]{0:T(1024)(128)(4,1)}), s8[4194304]{0:T(1024)(128)(4,1)S(1)}, s32[]{:S(2)}) async-start(s8[14680064]{0:T(1024)(128)(4,1)} %bitcast.91), calls=%async_computation.1 | async-start | bytes 8388608
  37.3 9.9 %slice-start.2 = ((s8[14680064]{0:T(1024)(128)(4,1)}), s8[4194304]{0:T(1024)(128)(4,1)S(1)}, s32[]{:S(2)}) async-start(s8[14680064]{0:T(1024)(128)(4,1)} %bitcast.91), calls=%async_computation.2 | async-start | bytes 8388608
  41.7 5.6 %slice-start.3 = ((s8[14680064]{0:T(1024)(128)(4,1)}), s8[2097152]{0:T(1024)(128)(4,1)S(1)}, s32[]{:S(2)}) async-start(s8[14680064]{0:T(1024)(128)(4,1)} %bitcast.91), calls=%async_computation.3 | async-start | bytes 4194304
  47.2 43.0 %collective-permute-start.10 = (bf16[128,3584]{1,0:T(8,128)(2,1)}, bf16[128,3584]{1,0:T(8,128)(2,1)}, u32[]{:S(2)}, u32[]{:S(2)}) collective-permute-start(bf16[128,3584]{1,0:T(8,128)(2,1)} %fusion.19), channel_id=1, source_target_pairs={{0,2},{1,3},{2,0},{3,1},{4,6},{5,7},{6,4},{7,5},{8,10},{9,11},{10,... | collective-permute-start | bytes 2752520 | tf_op jit(solution)/shard_map/ppermute | solution.py:30
  47.2 40.3 %copy-start.4 = (bf16[512,512]{1,0:T(8,128)(2,1)}, bf16[512,512]{1,0:T(8,128)(2,1)S(1)}, u32[]{:S(2)}) copy-start(bf16[512,512]{1,0:T(8,128)(2,1)S(1)} %collective-permute-done.5) | copy-start | bytes 1572868
  53.7 33.7 %collective-permute-start.9 = (bf16[128,3584]{1,0:T(8,128)(2,1)}, bf16[128,3584]{1,0:T(8,128)(2,1)}, u32[]{:S(2)}, u32[]{:S(2)}) collective-permute-start(bf16[128,3584]{1,0:T(8,128)(2,1)} %fusion.16), channel_id=1, source_target_pairs={{0,2},{1,3},{2,0},{3,1},{4,6},{5,7},{6,4},{7,5},{8,10},{9,11},{10,... | collective-permute-start | bytes 2752520 | tf_op jit(solution)/shard_map/ppermute | solution.py:30
  55.7 31.7 %copy-start.6 = (bf16[512,512]{1,0:T(8,128)(2,1)}, bf16[512,512]{1,0:T(8,128)(2,1)S(1)}, u32[]{:S(2)}) copy-start(bf16[512,512]{1,0:T(8,128)(2,1)S(1)} %collective-permute-done.6) | copy-start | bytes 1572868
  55.8 12.9 %collective-permute-start.7 = (bf16[128,2048]{1,0:T(8,128)(2,1)S(1)}, bf16[128,2048]{1,0:T(8,128)(2,1)S(1)}, u32[]{:S(2)}, u32[]{:S(2)}) collective-permute-start(bf16[128,2048]{1,0:T(8,128)(2,1)S(1)} %collective-permute-done.2), channel_id=1, source_target_pairs={{0,16},{1,17},{18,2},{19,3},{4,20},{5,21},{22,6},{23,7},{8,24},{9,... | collective-permute-start | bytes 1572872 | tf_op jit(solution)/shard_map/ppermute | solution.py:54
  68.8 24.6 %collective-permute-start.8 = (bf16[256,2048]{1,0:T(8,128)(2,1)S(1)}, bf16[256,2048]{1,0:T(8,128)(2,1)S(1)}, u32[]{:S(2)}, u32[]{:S(2)}) collective-permute-start(bf16[256,2048]{1,0:T(8,128)(2,1)S(1)} %slice.146), channel_id=1, source_target_pairs={{0,16},{1,17},{18,2},{19,3},{4,20},{5,21},{22,6},{23,7},{8,24},{9,... | collective-permute-start | bytes 3145736 | tf_op jit(solution)/shard_map/ppermute | solution.py:61
  81.2 6.3 %copy-start.3 = (bf16[1,512,512]{2,1,0:T(8,128)(2,1)S(1)}, bf16[1,512,512]{2,1,0:T(8,128)(2,1)}, u32[]{:S(2)}) copy-start(bf16[1,512,512]{2,1,0:T(8,128)(2,1)} %param.11) | copy-start | bytes 1572868
  87.7 26.9 %collective-permute-start.13 = (bf16[2,512,512]{2,1,0:T(8,128)(2,1)S(1)}, bf16[2,512,512]{2,1,0:T(8,128)(2,1)S(1)}, u32[]{:S(2)}, u32[]{:S(2)}) collective-permute-start(bf16[2,512,512]{2,1,0:T(8,128)(2,1)S(1)} %maximum_select_fusion.2), channel_id=1, source_target_pairs={{0,16},{1,17},{18,2},{19,3},{2,18},{3,19},{16,0},{17,1},{4,20},{5,... | collective-permute-start | bytes 3145736 | tf_op jit(solution)/shard_map/ppermute | solution.py:98
  90.2 40.3 %collective-permute-start.11 = (bf16[128,7168]{1,0:T(8,128)(2,1)}, bf16[128,7168]{1,0:T(8,128)(2,1)}, u32[]{:S(2)}, u32[]{:S(2)}) collective-permute-start(bf16[128,7168]{1,0:T(8,128)(2,1)} %fusion), channel_id=1, source_target_pairs={{0,2},{1,3},{2,0},{3,1},{4,6},{5,7},{6,4},{7,5},{8,10},{9,11},{10,... | collective-permute-start | bytes 5505032 | tf_op jit(solution)/shard_map/ppermute | solution.py:30
  102.6 12.0 %copy-start.5 = (bf16[512,512]{1,0:T(8,128)(2,1)S(1)}, bf16[512,512]{1,0:T(8,128)(2,1)}, u32[]{:S(2)}) copy-start(bf16[512,512]{1,0:T(8,128)(2,1)} %copy-done.4) | copy-start | bytes 1572868
  102.6 12.0 %copy-start.7 = (bf16[512,512]{1,0:T(8,128)(2,1)S(1)}, bf16[512,512]{1,0:T(8,128)(2,1)}, u32[]{:S(2)}) copy-start(bf16[512,512]{1,0:T(8,128)(2,1)} %copy-done.6) | copy-start | bytes 1572868
  103.1 11.4 %collective-permute-start.12 = (f32[384,32]{0,1:T(8,128)S(1)}, f32[384,32]{0,1:T(8,128)S(1)}, u32[]{:S(2)}, u32[]{:S(2)}) collective-permute-start(f32[384,32]{0,1:T(8,128)S(1)} %fusion.81), channel_id=1, source_target_pairs={{0,16},{16,0},{1,17},{17,1},{2,18},{18,2},{3,19},{19,3},{4,20},{20... | collective-permute-start | bytes 147464 | tf_op jit(solution)/shard_map/ppermute | solution.py:183
  116.6 29.0 %copy-start.8 = (bf16[32,7168]{1,0:T(8,128)(2,1)S(1)}, bf16[32,7168]{1,0:T(8,128)(2,1)}, u32[]{:S(2)}) copy-start(bf16[32,7168]{1,0:T(8,128)(2,1)} %param.10) | copy-start | bytes 1376260
  116.6 33.4 %collective-permute-start.14 = (bf16[2,2,512,512]{3,2,1,0:T(8,128)(2,1)}, bf16[2,2,512,512]{3,2,1,0:T(8,128)(2,1)S(1)}, u32[]{:S(2)}, u32[]{:S(2)}) collective-permute-start(bf16[2,2,512,512]{3,2,1,0:T(8,128)(2,1)} %maximum_select_fusion), channel_id=1, source_target_pairs={{0,1},{1,0},{2,3},{3,2},{4,5},{5,4},{6,7},{7,6},{8,9},{9,8},{10,11... | collective-permute-start | bytes 6291464 | tf_op jit(solution)/shard_map/ppermute | solution.py:102
  130.5 33.4 %collective-permute-start.15 = (bf16[96,7168]{1,0:T(8,128)(2,1)}, bf16[96,7168]{1,0:T(8,128)(2,1)}, u32[]{:S(2)}, u32[]{:S(2)}) collective-permute-start(bf16[96,7168]{1,0:T(8,128)(2,1)} %slice.189), channel_id=1, source_target_pairs={{0,2},{1,3},{2,0},{3,1},{4,6},{5,7},{6,4},{7,5},{8,10},{9,11},{10,... | collective-permute-start | bytes 4128776 | tf_op jit(solution)/shard_map/ppermute | solution.py:30
  144.0 25.7 %collective-permute-start.16 = (bf16[32,7168]{1,0:T(8,128)(2,1)}, bf16[32,7168]{1,0:T(8,128)(2,1)S(1)}, u32[]{:S(2)}, u32[]{:S(2)}) collective-permute-start(bf16[32,7168]{1,0:T(8,128)(2,1)} %slice.190), channel_id=1, source_target_pairs={{0,2},{1,3},{2,0},{3,1},{4,6},{5,7},{6,4},{7,5},{8,10},{9,11},{10,... | collective-permute-start | bytes 1376264 | tf_op jit(solution)/shard_map/ppermute | solution.py:30
  150.5 2.6 %slice-start.4 = ((s8[5505024]{0:T(1024)(128)(4,1)}), s8[4194304]{0:T(1024)(128)(4,1)S(1)}, s32[]{:S(2)}) async-start(s8[5505024]{0:T(1024)(128)(4,1)} %bitcast.111), calls=%async_computation.4 | async-start | bytes 8388608
  150.8 2.7 %slice-start.5 = ((s8[5505024]{0:T(1024)(128)(4,1)}), s8[1310720]{0:T(1024)(128)(4,1)S(1)}, s32[]{:S(2)}) async-start(s8[5505024]{0:T(1024)(128)(4,1)} %bitcast.111), calls=%async_computation.5 | async-start | bytes 2621440
  150.9 2.7 %copy-start.9 = (bf16[32,7168]{1,0:T(8,128)(2,1)S(1)}, bf16[32,7168]{1,0:T(8,128)(2,1)}, u32[]{:S(2)}) copy-start(bf16[32,7168]{1,0:T(8,128)(2,1)} %param.10) | copy-start | bytes 1376260
  170.5 15.3 %copy-start.1 = (bf16[32,4096]{1,0:T(8,128)(2,1)S(1)}, bf16[32,4096]{1,0:T(8,128)(2,1)}, u32[]{:S(2)}) copy-start(bf16[32,4096]{1,0:T(8,128)(2,1)} %param.9) | copy-start | bytes 786436
  173.1 3.8 %collective-permute-start.17 = (f32[3,1024]{1,0:T(4,128)S(1)}, f32[3,1024]{1,0:T(4,128)S(1)}, u32[]{:S(2)}, u32[]{:S(2)}) collective-permute-start(f32[3,1024]{1,0:T(4,128)S(1)} %bitcast.108), channel_id=1, source_target_pairs={{0,16},{16,0},{1,17},{17,1},{2,18},{18,2},{3,19},{19,3},{4,20},{20... | collective-permute-start | bytes 36872 | tf_op jit(solution)/shard_map/ppermute | solution.py:119
  176.9 5.5 %collective-permute-start.18 = (f32[3,256]{1,0:T(4,128)S(1)}, f32[3,256]{1,0:T(4,128)S(1)}, u32[]{:S(2)}, u32[]{:S(2)}) collective-permute-start(f32[3,256]{1,0:T(4,128)S(1)} %get-tuple-element.89), channel_id=1, source_target_pairs={{0,4},{4,8},{8,12},{12,0},{1,5},{5,9},{9,13},{13,1},{2,6},{6,10},{... | collective-permute-start | bytes 9224 | tf_op jit(solution)/shard_map/ppermute | solution.py:119
  178.5 3.8 %collective-permute-start.20 = (f32[3,256]{1,0:T(4,128)S(1)}, f32[3,256]{1,0:T(4,128)S(1)}, u32[]{:S(2)}, u32[]{:S(2)}) collective-permute-start(f32[3,256]{1,0:T(4,128)S(1)} %get-tuple-element.90), channel_id=1, source_target_pairs={{0,12},{4,0},{8,4},{12,8},{1,13},{5,1},{9,5},{13,9},{2,14},{6,2},{... | collective-permute-start | bytes 9224 | tf_op jit(solution)/shard_map/ppermute | solution.py:119
  180.8 4.5 %collective-permute-start.19 = (f32[3,256]{1,0:T(4,128)S(1)}, f32[3,256]{1,0:T(4,128)S(1)}, u32[]{:S(2)}, u32[]{:S(2)}) collective-permute-start(f32[3,256]{1,0:T(4,128)S(1)} %get-tuple-element.91), channel_id=1, source_target_pairs={{0,8},{4,12},{8,0},{12,4},{1,9},{5,13},{9,1},{13,5},{2,10},{6,14},... | collective-permute-start | bytes 9224 | tf_op jit(solution)/shard_map/ppermute | solution.py:119

commit v5 on v4

--- a/solution.py
+++ b/solution.py
@@ -169,11 +169,11 @@
         part_de = partials(2, 0, SEQ, part_c)
         part_d = [value[:most] for value in part_de]
         part_e = [value[most:] for value in part_de]
-        got_c = send(part_c, got_a + got_b + part_d + part_e)
-        got_d = send(part_d, got_c)
-        mark_rows = assemble(got_b[0])
+        got_c = send(part_c, got_a + part_d + part_e)
+        mark_rows = assemble(part_e[0])
         mine, theirs = split(own(part_c[0], got_b[0]))
         own_part = dot(mine, weight, ((1,), (0,)))
+        got_d = send(part_d, got_b + [own_part])
         left = dot(
             after(rows, own_part),
             lax.dynamic_slice_in_dim(sketch_left, f_index * part, part, 1),

time: 186 us -> 183 us (0.984)
  waiting for transfers between devices: 67.6 us -> 62.3 us
  starting transfers between devices: 34 us -> 36.1 us
    ppermute x1, waiting for transfers between devices: 8.82 us -> 0.01 us  [per_device(): left = left + lax.ppermute(left, 'fsdp', [(0, 1), (1, 0)])]
    ppermute x1, waiting for transfers between devices: 0.01 us -> 6.57 us  [assemble(): beside = lax.ppermute(mine, both, on_y + off_y)]
    ppermute x5, waiting for transfers between devices: 29 us -> 25.5 us  [shift_x(): lax.ppermute(value, 'dp', [(i, (i + 2 * shift) % n_dp) for i in range(n_d...]
    ppermute x5, starting transfers between devices: 4.17 us -> 7.16 us  [shift_x(): lax.ppermute(value, 'dp', [(i, (i + 2 * shift) % n_dp) for i in range(n_d...]
    ppermute x1, starting transfers between devices: 2.52 us -> 0.07 us  [assemble(): beside = lax.ppermute(mine, both, on_y + off_y)]
  transfers between devices with their start and end apart: 21 -> 21, of which waited for: 12 -> 12; matrix products, arithmetic and copies ran while one was open for 42% -> 43% of each run, Pallas kernels for 0% -> 0%
where the time goes in v5:
time: 183 us
  matrix products  71.1 us (39%)
  waiting for transfers between devices  62.3 us (34%)
  starting transfers between devices  36.1 us (20%)
  other arithmetic  7.63 us (4%)
  local copies, waits for them, and re-layouts  5.06 us (3%)
    dot_general x17, matrix products, dot(): return lax.dot_general(a, b, (dims, ((), ())), preferred_element_type=F32)  70.8 us
    ppermute x5, waiting for transfers between devices, shift_x(): lax.ppermute(value, 'dp', [(i, (i + 2 * shift) % n_dp) for i in range(n_d...  25.5 us
    ppermute x1, waiting for transfers between devices, spread(): stages = [lax.ppermute(rows[first[0]:first[1]], both, off_x + on_y)]  12.4 us
    ppermute x5, starting transfers between devices, shift_x(): lax.ppermute(value, 'dp', [(i, (i + 2 * shift) % n_dp) for i in range(n_d...  7.16 us
    ppermute x4, starting transfers between devices, scatter_sum(): lax.ppermute(block, axis_name, [(i, (i + shift) % size) for i in range(si...  7.14 us
    ppermute x1, waiting for transfers between devices, assemble(): beside = lax.ppermute(mine, both, on_y + off_y)  6.57 us
    ppermute x2, waiting for transfers between devices, spread(): stages.append(lax.ppermute(operand, both, off_x + on_y))  6.16 us
    ppermute x2, starting transfers between devices, start_landmarks(): return [lax.ppermute(marks, both, off_y), lax.ppermute(marks, both, on_x)]  5.86 us
  transfers between devices with their start and end apart: 21, of which 12 were waited for; matrix products, arithmetic and copies ran while one was open for 43% of the time, Pallas kernels for 0%

profile of v5, /device:TPU:0, one launch (start us, length us, event | category | flops | bytes accessed | tf_op | source)
XLA Modules:
  0.0 182.6 jit_solution(8636588856043813191)
XLA Ops:
  0.0 0.5 collective-permute-start.4
  0.5 1.1 slice_bitcast_fusion.8
  1.6 2.7 %collective-permute-start = (bf16[128,2048]{1,0:T(8,128)(2,1)S(1)}, bf16[128,2048]{1,0:T(8,128)(2,1)S(1)}, u32[]{:S(2)}, u32[]{:S(2)}) collective-permute-start(bf16[128,2048]{1,0:T(8,128)(2,1)S(1)} %slice_bitcast_fusion.8), channel_id=1, source_target_pairs={{2,0},{3,1},{16,18},{17,19},{0,16},{1,17},{18,2},{19,3},{6,4},{7,5... | collective-permute-start | bytes 1572872 | tf_op jit(solution)/shard_map/ppermute | solution.py:46
  4.3 12.4 %collective-permute-done = bf16[128,2048]{1,0:T(8,128)(2,1)S(1)} collective-permute-done((bf16[128,2048]{1,0:T(8,128)(2,1)S(1)}, bf16[128,2048]{1,0:T(8,128)(2,1)S(1)}, u32[]{:S(2)}, u32[]{:S(2)}) %collective-permute-start) | collective-permute-done | bytes 524320 | tf_op jit(solution)/shard_map/ppermute | solution.py:46
  16.7 1.9 %slice_select_fusion.1 = bf16[128,2048]{1,0:T(8,128)(2,1)} fusion(bf16[128,2048]{1,0:T(8,128)(2,1)S(1)} %collective-permute-done, bf16[384,2048]{1,0:T(8,128)(2,1)} %bitcast.94, pred[]{:T(512)S(6)} %eq.7), kind=kLoop, calls=%fused_computation.63 | loop fusion | flops 262144 | bytes 1572865 | tf_op jit(solution)/shard_map/jit(_where)/select_n | solution.py:49
  18.6 1.8 collective-permute-start.1
  20.4 1.3 collective-permute-start.3
  21.7 4.6 %collective-permute-start.5 = (bf16[512,512]{1,0:T(8,128)(2,1)}, bf16[512,512]{1,0:T(8,128)(2,1)S(1)}, u32[]{:S(2)}, u32[]{:S(2)}) collective-permute-start(bf16[512,512]{1,0:T(8,128)(2,1)} %bitcast.99), channel_id=1, source_target_pairs={{0,2},{1,3},{18,16},{19,17},{4,6},{5,7},{22,20},{23,21},{8,10},{9,... | collective-permute-start | bytes 1572872 | tf_op jit(solution)/shard_map/ppermute | solution.py:84
  26.3 6.2 %collective-permute-done.1 = bf16[128,2048]{1,0:T(8,128)(2,1)S(1)} collective-permute-done((bf16[128,2048]{1,0:T(8,128)(2,1)}, bf16[128,2048]{1,0:T(8,128)(2,1)S(1)}, u32[]{:S(2)}, u32[]{:S(2)}) %collective-permute-start.1) | collective-permute-done | bytes 524320 | tf_op jit(solution)/shard_map/ppermute | solution.py:50
  32.5 1.6 collective-permute-start.2
  34.1 1.5 collective-permute-done.3
  35.6 1.7 collective-permute-start.6
  37.3 4.4 %fusion.8 = f32[128,3584]{1,0:T(8,128)S(1)} fusion(bf16[1024,7168]{1,0:T(8,128)(2,1)} %bitcast.90, pred[]{:T(512)S(6)} %eq.6, bf16[128,2048]{1,0:T(8,128)(2,1)S(1)} %broadcast_select_fusion.6), kind=kOutput, calls=%fused_computation.11 | convolution fusion | flops 939655168 | bytes 9699329 | tf_op jit(solution)/shard_map/dot_general | solution.py:14
  41.7 5.4 %fusion.19 = bf16[128,3584]{1,0:T(8,128)(2,1)} fusion(f32[128,3584]{1,0:T(8,128)S(1)} %fusion.8, bf16[1024,7168]{1,0:T(8,128)(2,1)} %collective-permute-done.4, pred[]{:T(512)S(6)} %eq.6, bf16[128,2048]{1,0:T(8,128)(2,1)S(1)} %broadcast_select_fusion.6), kind=kOutput, calls=%fused_computation.16 | convolution fusion | flops 940572672 | bytes 10616833 | tf_op jit(solution)/shard_map/dot_general | solution.py:14
  47.3 1.1 fusion.4
  48.4 5.3 %fusion.16 = bf16[128,3584]{1,0:T(8,128)(2,1)} fusion(f32[128,3584]{1,0:T(8,128)S(1)} %fusion.4, bf16[1024,7168]{1,0:T(8,128)(2,1)} %collective-permute-done.4, pred[]{:T(512)S(6)} %eq.6, bf16[128,2048]{1,0:T(8,128)(2,1)S(1)} %broadcast_select_fusion.5), kind=kOutput, calls=%fused_computation.15 | convolution fusion | flops 940572672 | bytes 10616833 | tf_op jit(solution)/shard_map/dot_general | solution.py:14
  53.7 2.0 %collective-permute-start.9 = (bf16[128,3584]{1,0:T(8,128)(2,1)}, bf16[128,3584]{1,0:T(8,128)(2,1)}, u32[]{:S(2)}, u32[]{:S(2)}) collective-permute-start(bf16[128,3584]{1,0:T(8,128)(2,1)} %fusion.16), channel_id=1, source_target_pairs={{0,2},{1,3},{2,0},{3,1},{4,6},{5,7},{6,4},{7,5},{8,10},{9,11},{10,... | collective-permute-start | bytes 2752520 | tf_op jit(solution)/shard_map/ppermute | solution.py:30
  55.7 2.2 %collective-permute-start.7 = (bf16[128,2048]{1,0:T(8,128)(2,1)S(1)}, bf16[128,2048]{1,0:T(8,128)(2,1)S(1)}, u32[]{:S(2)}, u32[]{:S(2)}) collective-permute-start(bf16[128,2048]{1,0:T(8,128)(2,1)S(1)} %collective-permute-done.2), channel_id=1, source_target_pairs={{0,16},{1,17},{18,2},{19,3},{4,20},{5,21},{22,6},{23,7},{8,24},{9,... | collective-permute-start | bytes 1572872 | tf_op jit(solution)/shard_map/ppermute | solution.py:54
  58.1 2.1 %fusion.49 = f32[128,7168]{1,0:T(8,128)S(1)} fusion(pred[]{:T(512)S(6)} %eq.6, bf16[128,2048]{1,0:T(8,128)(2,1)S(1)} %broadcast_select_fusion.4, bf16[1,1024,7168]{2,1,0:T(8,128)(2,1)S(1)} %bitcast.92), kind=kOutput, calls=%fused_computation.74 | convolution fusion | flops 1879179264 | bytes 18874368 | tf_op jit(solution)/shard_map/dot_general | solution.py:14
  60.1 8.5 %fusion = bf16[128,7168]{1,0:T(8,128)(2,1)} fusion(f32[128,7168]{1,0:T(8,128)S(1)} %fusion.49, bf16[1024,7168]{1,0:T(8,128)(2,1)} %collective-permute-done.4, pred[]{:T(512)S(6)} %eq.6, bf16[128,2048]{1,0:T(8,128)(2,1)S(1)} %broadcast_select_fusion.4), kind=kOutput, calls=%fused_computation.3 | convolution fusion | flops 1881014272 | bytes 20709376 | tf_op jit(solution)/shard_map/dot_general | solution.py:14
  68.8 3.0 %collective-permute-start.8 = (bf16[256,2048]{1,0:T(8,128)(2,1)S(1)}, bf16[256,2048]{1,0:T(8,128)(2,1)S(1)}, u32[]{:S(2)}, u32[]{:S(2)}) collective-permute-start(bf16[256,2048]{1,0:T(8,128)(2,1)S(1)} %slice.146), channel_id=1, source_target_pairs={{0,16},{1,17},{18,2},{19,3},{4,20},{5,21},{22,6},{23,7},{8,24},{9,... | collective-permute-start | bytes 3145736 | tf_op jit(solution)/shard_map/ppermute | solution.py:61
  71.8 2.1 %fusion.46 = f32[128,7168]{1,0:T(8,128)S(1)} fusion(pred[]{:T(512)S(6)} %eq.6, bf16[128,2048]{1,0:T(8,128)(2,1)S(1)} %broadcast_select_fusion.3, bf16[1,1024,7168]{2,1,0:T(8,128)(2,1)S(1)} %bitcast.92), kind=kOutput, calls=%fused_computation.71 | convolution fusion | flops 1879179264 | bytes 18874368 | tf_op jit(solution)/shard_map/dot_general | solution.py:14
  73.9 7.3 %fusion.1 = bf16[128,7168]{1,0:T(8,128)(2,1)S(1)} fusion(f32[128,7168]{1,0:T(8,128)S(1)} %fusion.46, bf16[1024,7168]{1,0:T(8,128)(2,1)} %collective-permute-done.4, pred[]{:T(512)S(6)} %eq.6, bf16[128,2048]{1,0:T(8,128)(2,1)S(1)} %broadcast_select_fusion.3), kind=kOutput, calls=%fused_computation.4 | convolution fusion | flops 1881014272 | bytes 20709376 | tf_op jit(solution)/shard_map/dot_general | solution.py:14
  81.2 0.8 slice.190
  82.0 1.2 slice.189
  83.2 0.2 maximum_select_fusion.2
  83.5 1.8 collective-permute-start.11
  85.3 5.2 %collective-permute-done.9 = bf16[128,3584]{1,0:T(8,128)(2,1)} collective-permute-done((bf16[128,3584]{1,0:T(8,128)(2,1)}, bf16[128,3584]{1,0:T(8,128)(2,1)}, u32[]{:S(2)}, u32[]{:S(2)}) %collective-permute-start.9) | collective-permute-done | bytes 917536 | tf_op jit(solution)/shard_map/ppermute | solution.py:30
  90.4 4.7 %collective-permute-done.8 = bf16[256,2048]{1,0:T(8,128)(2,1)S(1)} collective-permute-done((bf16[256,2048]{1,0:T(8,128)(2,1)S(1)}, bf16[256,2048]{1,0:T(8,128)(2,1)S(1)}, u32[]{:S(2)}, u32[]{:S(2)}) %collective-permute-start.8) | collective-permute-done | bytes 1048608 | tf_op jit(solution)/shard_map/ppermute | solution.py:61
  95.1 0.6 maximum_select_fusion.1
  95.7 8.6 %fusion.38 = f32[384,7168]{1,0:T(8,128)} fusion(pred[]{:T(512)S(6)} %eq.6, bf16[384,2048]{1,0:T(8,128)(2,1)S(1)} %maximum_select_fusion.1, bf16[1,1024,7168]{2,1,0:T(8,128)(2,1)S(1)} %bitcast.92), kind=kOutput, calls=%fused_computation.48 | convolution fusion | flops 5637537792 | bytes 27262976 | tf_op jit(solution)/shard_map/dot_general | solution.py:14
  104.3 0.6 fusion.81
  104.9 2.5 %collective-permute-start.12 = (f32[384,32]{0,1:T(8,128)S(1)}, f32[384,32]{0,1:T(8,128)S(1)}, u32[]{:S(2)}, u32[]{:S(2)}) collective-permute-start(f32[384,32]{0,1:T(8,128)S(1)} %fusion.81), channel_id=1, source_target_pairs={{0,16},{16,0},{1,17},{17,1},{2,18},{18,2},{3,19},{19,3},{4,20},{20... | collective-permute-start | bytes 147464 | tf_op jit(solution)/shard_map/ppermute | solution.py:183
  107.5 6.6 %collective-permute-done.13 = bf16[2,512,512]{2,1,0:T(8,128)(2,1)S(1)} collective-permute-done((bf16[2,512,512]{2,1,0:T(8,128)(2,1)S(1)}, bf16[2,512,512]{2,1,0:T(8,128)(2,1)S(1)}, u32[]{:S(2)}, u32[]{:S(2)}) %collective-permute-start.13) | collective-permute-done | bytes 1048608 | tf_op jit(solution)/shard_map/ppermute | solution.py:98
  114.0 0.3 select_bitcast_fusion.1
  114.4 1.6 maximum_select_fusion
  116.0 2.3 %collective-permute-start.15 = (bf16[96,7168]{1,0:T(8,128)(2,1)}, bf16[96,7168]{1,0:T(8,128)(2,1)}, u32[]{:S(2)}, u32[]{:S(2)}) collective-permute-start(bf16[96,7168]{1,0:T(8,128)(2,1)} %slice.189), channel_id=1, source_target_pairs={{0,2},{1,3},{2,0},{3,1},{4,6},{5,7},{6,4},{7,5},{8,10},{9,11},{10,... | collective-permute-start | bytes 4128776 | tf_op jit(solution)/shard_map/ppermute | solution.py:30
  118.3 11.5 %collective-permute-done.11 = bf16[128,7168]{1,0:T(8,128)(2,1)} collective-permute-done((bf16[128,7168]{1,0:T(8,128)(2,1)}, bf16[128,7168]{1,0:T(8,128)(2,1)}, u32[]{:S(2)}, u32[]{:S(2)}) %collective-permute-start.11) | collective-permute-done | bytes 1835040 | tf_op jit(solution)/shard_map/ppermute | solution.py:30
  129.8 13.0 %convolution_add_fusion = f32[384,7168]{1,0:T(8,128)S(1)} fusion(f32[384,7168]{1,0:T(8,128)} %fusion.38, bf16[384,1024]{1,0:T(8,128)(2,1)S(1)} %broadcast_select_fusion.2, bf16[1024,7168]{1,0:T(8,128)(2,1)} %collective-permute-done.4), kind=kOutput, calls=%fused_computation | convolution fusion | flops 5639897088 | bytes 37486592 | tf_op jit(solution)/shard_map/dot_general | solution.py:14
  142.7 1.1 collective-permute-start.16
  143.9 2.2 %fusion.37 = f32[128,32]{0,1:T(8,128)S(1)} fusion(bf16[128,3584]{1,0:T(8,128)(2,1)} %collective-permute-done.9, f32[384,7168]{1,0:T(8,128)S(1)} %convolution_add_fusion, bf16[384,7168]{1,0:T(8,128)(2,1)} %bitcast.109, bf16[32,7168]{1,0:T(8,128)(2,1)S(1)} %copy-done.8), kind=kOutput, calls=%fused_computation.47 | convolution fusion | flops 33488896 | bytes 3915776 | tf_op jit(solution)/shard_map/dot_general | solution.py:14
  146.1 2.2 %convolution_add_fusion.3 = f32[128,32]{0,1:T(8,128)S(1)} fusion(f32[128,32]{0,1:T(8,128)S(1)} %fusion.37, bf16[128,3584]{1,0:T(8,128)(2,1)} %collective-permute-done.10, f32[384,7168]{1,0:T(8,128)S(1)} %convolution_add_fusion, bf16[384,7168]{1,0:T(8,128)(2,1)} %bitcast.110, bf16[32,7168]{1,0:T(8,128)(2,1)S(1)} %copy-done.8), kind=kOutput, calls=%fused_computation.37 | convolution fusion | flops 33492992 | bytes 3932160 | tf_op jit(solution)/shard_map/dot_general | solution.py:14
  148.3 0.5 broadcast_select_fusion
  148.8 0.3 slice_bitcast_fusion.1
  149.1 0.1 pad_maximum_fusion.3
  149.4 0.1 pad_maximum_fusion
  149.5 1.1 pad_maximum_fusion.2
  150.6 0.8 slice-done.4
  151.4 0.5 slice-done.5
  151.9 2.8 %fusion.32 = f32[128,32]{0,1:T(8,128)S(1)} fusion(bf16[32,7168]{1,0:T(8,128)(2,1)S(1)} %copy-done.9, bf16[128,7168]{1,0:T(8,128)(2,1)} %collective-permute-done.11, f32[384,7168]{1,0:T(8,128)S(1)} %convolution_add_fusion, bf16[1,384,7168]{2,1,0:T(8,128)(2,1)S(1)} %bitcast.112), kind=kOutput, calls=%fused_computation.34 | convolution fusion | flops 66977792 | bytes 7815168 | tf_op jit(solution)/shard_map/dot_general | solution.py:14
  154.8 4.5 %collective-permute-done.15 = bf16[96,7168]{1,0:T(8,128)(2,1)} collective-permute-done((bf16[96,7168]{1,0:T(8,128)(2,1)}, bf16[96,7168]{1,0:T(8,128)(2,1)}, u32[]{:S(2)}, u32[]{:S(2)}) %collective-permute-start.15) | collective-permute-done | bytes 1376288 | tf_op jit(solution)/shard_map/ppermute | solution.py:30
  159.2 2.4 %fusion.34 = f32[96,32]{0,1:T(8,128)S(1)} fusion(bf16[32,7168]{1,0:T(8,128)(2,1)S(1)} %copy-done.9, bf16[96,7168]{1,0:T(8,128)(2,1)} %collective-permute-done.15, f32[384,7168]{1,0:T(8,128)S(1)} %convolution_add_fusion, bf16[1,384,7168]{2,1,0:T(8,128)(2,1)S(1)} %bitcast.112), kind=kOutput, calls=%fused_computation.36 | convolution fusion | flops 50233344 | bytes 5976064 | tf_op jit(solution)/shard_map/dot_general | solution.py:14
  161.6 4.4 %collective-permute-done.16 = bf16[32,7168]{1,0:T(8,128)(2,1)S(1)} collective-permute-done((bf16[32,7168]{1,0:T(8,128)(2,1)}, bf16[32,7168]{1,0:T(8,128)(2,1)S(1)}, u32[]{:S(2)}, u32[]{:S(2)}) %collective-permute-start.16) | collective-permute-done | bytes 458784 | tf_op jit(solution)/shard_map/ppermute | solution.py:30
  166.1 0.5 fusion.43
  166.5 0.3 fusion.83
  166.9 2.4 %fusion.22 = f32[6,2048]{1,0:T(8,128)S(1)} fusion(bf16[512,1024]{1,0:T(8,128)(2,1)S(1)} %pad_maximum_fusion.3, bf16[512,1024]{1,0:T(8,128)(2,1)} %pad_maximum_fusion.2, bf16[512,1024]{1,0:T(8,128)(2,1)S(1)} %pad_maximum_fusion.1, bf16[512,1024]{1,0:T(8,128)(2,1)S(1)} %pad_maximum_fusion, bf16[3,1024]{1,0:T(4,128)(2,1)S(1)} %get-tuple-element.93, ...), kind=kOutput, calls=%fused_computation.17 | convolution fusion | flops 41967616 | bytes 4255744 | tf_op jit(solution)/shard_map/dot_general | solution.py:14
  169.4 2.5 %collective-permute-start.17 = (f32[3,1024]{1,0:T(4,128)S(1)}, f32[3,1024]{1,0:T(4,128)S(1)}, u32[]{:S(2)}, u32[]{:S(2)}) collective-permute-start(f32[3,1024]{1,0:T(4,128)S(1)} %bitcast.108), channel_id=1, source_target_pairs={{0,16},{16,0},{1,17},{17,1},{2,18},{18,2},{3,19},{19,3},{4,20},{20... | collective-permute-start | bytes 36872 | tf_op jit(solution)/shard_map/ppermute | solution.py:119
  171.9 1.7 collective-permute-done.17
  173.7 1.6 collective-permute-start.18
  175.3 2.2 %collective-permute-start.20 = (f32[3,256]{1,0:T(4,128)S(1)}, f32[3,256]{1,0:T(4,128)S(1)}, u32[]{:S(2)}, u32[]{:S(2)}) collective-permute-start(f32[3,256]{1,0:T(4,128)S(1)} %get-tuple-element.90), channel_id=1, source_target_pairs={{0,12},{4,0},{8,4},{12,8},{1,13},{5,1},{9,5},{13,9},{2,14},{6,2},{... | collective-permute-start | bytes 9224 | tf_op jit(solution)/shard_map/ppermute | solution.py:119
  177.5 0.8 collective-permute-start.19
  178.3 0.8 collective-permute-done.18
  179.1 2.9 %collective-permute-done.19 = f32[3,256]{1,0:T(4,128)S(1)} collective-permute-done((f32[3,256]{1,0:T(4,128)S(1)}, f32[3,256]{1,0:T(4,128)S(1)}, u32[]{:S(2)}, u32[]{:S(2)}) %collective-permute-start.19) | collective-permute-done | bytes 3104 | tf_op jit(solution)/shard_map/ppermute | solution.py:119
  182.0 0.6 fusion.93
  (61 shorter events, 1.1 us)
Async XLA Ops:
  0.0 104.3 %copy-start = (bf16[32,4096]{1,0:T(8,128)(2,1)S(1)}, bf16[32,4096]{1,0:T(8,128)(2,1)}, u32[]{:S(2)}) copy-start(bf16[32,4096]{1,0:T(8,128)(2,1)} %param.9) | copy-start | bytes 786436
  0.0 32.4 %copy-start.2 = (bf16[1,384,2048]{2,1,0:T(8,128)(2,1)S(1)}, bf16[1,384,2048]{2,1,0:T(8,128)(2,1)}, u32[]{:S(2)}) copy-start(bf16[1,384,2048]{2,1,0:T(8,128)(2,1)} %param.6) | copy-start | bytes 4718596
  0.0 41.7 %collective-permute-start.4 = (bf16[1024,7168]{1,0:T(8,128)(2,1)}, bf16[1024,7168]{1,0:T(8,128)(2,1)}, u32[]{:S(2)}, u32[]{:S(2)}) collective-permute-start(bf16[1024,7168]{1,0:T(8,128)(2,1)} %bitcast.89), channel_id=1, source_target_pairs={{0,1},{1,0},{2,3},{3,2},{4,5},{5,4},{6,7},{7,6},{8,9},{9,8},{10,11... | collective-permute-start | bytes 44040200 | tf_op jit(solution)/shard_map/ppermute | solution.py:26
  1.6 15.1 %collective-permute-start = (bf16[128,2048]{1,0:T(8,128)(2,1)S(1)}, bf16[128,2048]{1,0:T(8,128)(2,1)S(1)}, u32[]{:S(2)}, u32[]{:S(2)}) collective-permute-start(bf16[128,2048]{1,0:T(8,128)(2,1)S(1)} %slice_bitcast_fusion.8), channel_id=1, source_target_pairs={{2,0},{3,1},{16,18},{17,19},{0,16},{1,17},{18,2},{19,3},{6,4},{7,5... | collective-permute-start | bytes 1572872 | tf_op jit(solution)/shard_map/ppermute | solution.py:46
  18.6 13.8 %collective-permute-start.1 = (bf16[128,2048]{1,0:T(8,128)(2,1)}, bf16[128,2048]{1,0:T(8,128)(2,1)S(1)}, u32[]{:S(2)}, u32[]{:S(2)}) collective-permute-start(bf16[128,2048]{1,0:T(8,128)(2,1)} %slice_select_fusion.1), channel_id=1, source_target_pairs={{2,0},{3,1},{16,18},{17,19},{0,16},{1,17},{18,2},{19,3},{6,4},{7,5... | collective-permute-start | bytes 1572872 | tf_op jit(solution)/shard_map/ppermute | solution.py:50
  20.4 15.2 %collective-permute-start.3 = (bf16[512,512]{1,0:T(8,128)(2,1)}, bf16[512,512]{1,0:T(8,128)(2,1)S(1)}, u32[]{:S(2)}, u32[]{:S(2)}) collective-permute-start(bf16[512,512]{1,0:T(8,128)(2,1)} %bitcast.98), channel_id=1, source_target_pairs={{2,18},{3,19},{16,0},{17,1},{6,22},{7,23},{20,4},{21,5},{10,26},{1... | collective-permute-start | bytes 1572872 | tf_op jit(solution)/shard_map/ppermute | solution.py:84
  21.7 25.5 %collective-permute-start.5 = (bf16[512,512]{1,0:T(8,128)(2,1)}, bf16[512,512]{1,0:T(8,128)(2,1)S(1)}, u32[]{:S(2)}, u32[]{:S(2)}) collective-permute-start(bf16[512,512]{1,0:T(8,128)(2,1)} %bitcast.99), channel_id=1, source_target_pairs={{0,2},{1,3},{18,16},{19,17},{4,6},{5,7},{22,20},{23,21},{8,10},{9,... | collective-permute-start | bytes 1572872 | tf_op jit(solution)/shard_map/ppermute | solution.py:84
  32.4 14.8 %slice-start = ((s8[14680064]{0:T(1024)(128)(4,1)}), s8[4194304]{0:T(1024)(128)(4,1)S(1)}, s32[]{:S(2)}) async-start(s8[14680064]{0:T(1024)(128)(4,1)} %bitcast.91), calls=%async_computation | async-start | bytes 8388608
  32.5 23.3 %collective-permute-start.2 = (bf16[128,2048]{1,0:T(8,128)(2,1)S(1)}, bf16[128,2048]{1,0:T(8,128)(2,1)S(1)}, u32[]{:S(2)}, u32[]{:S(2)}) collective-permute-start(bf16[128,2048]{1,0:T(8,128)(2,1)S(1)} %slice_select_fusion), channel_id=1, source_target_pairs={{2,0},{3,1},{16,18},{17,19},{0,16},{1,17},{18,2},{19,3},{6,4},{7,5... | collective-permute-start | bytes 1572872 | tf_op jit(solution)/shard_map/ppermute | solution.py:50
  35.6 20.2 %collective-permute-start.6 = (bf16[512,512]{1,0:T(8,128)(2,1)S(1)}, bf16[512,512]{1,0:T(8,128)(2,1)S(1)}, u32[]{:S(2)}, u32[]{:S(2)}) collective-permute-start(bf16[512,512]{1,0:T(8,128)(2,1)S(1)} %collective-permute-done.3), channel_id=1, source_target_pairs={{0,2},{1,3},{18,16},{19,17},{4,6},{5,7},{22,20},{23,21},{8,10},{9,... | collective-permute-start | bytes 1572872 | tf_op jit(solution)/shard_map/ppermute | solution.py:87
  37.3 10.0 %slice-start.1 = ((s8[14680064]{0:T(1024)(128)(4,1)}), s8[4194304]{0:T(1024)(128)(4,1)S(1)}, s32[]{:S(2)}) async-start(s8[14680064]{0:T(1024)(128)(4,1)} %bitcast.91), calls=%async_computation.1 | async-start | bytes 8388608
  37.3 9.9 %slice-start.2 = ((s8[14680064]{0:T(1024)(128)(4,1)}), s8[4194304]{0:T(1024)(128)(4,1)S(1)}, s32[]{:S(2)}) async-start(s8[14680064]{0:T(1024)(128)(4,1)} %bitcast.91), calls=%async_computation.2 | async-start | bytes 8388608
  41.7 5.6 %slice-start.3 = ((s8[14680064]{0:T(1024)(128)(4,1)}), s8[2097152]{0:T(1024)(128)(4,1)S(1)}, s32[]{:S(2)}) async-start(s8[14680064]{0:T(1024)(128)(4,1)} %bitcast.91), calls=%async_computation.3 | async-start | bytes 4194304
  47.2 36.3 %collective-permute-start.10 = (bf16[128,3584]{1,0:T(8,128)(2,1)}, bf16[128,3584]{1,0:T(8,128)(2,1)}, u32[]{:S(2)}, u32[]{:S(2)}) collective-permute-start(bf16[128,3584]{1,0:T(8,128)(2,1)} %fusion.19), channel_id=1, source_target_pairs={{0,2},{1,3},{2,0},{3,1},{4,6},{5,7},{6,4},{7,5},{8,10},{9,11},{10,... | collective-permute-start | bytes 2752520 | tf_op jit(solution)/shard_map/ppermute | solution.py:30
  47.2 36.1 %copy-start.4 = (bf16[512,512]{1,0:T(8,128)(2,1)}, bf16[512,512]{1,0:T(8,128)(2,1)S(1)}, u32[]{:S(2)}) copy-start(bf16[512,512]{1,0:T(8,128)(2,1)S(1)} %collective-permute-done.5) | copy-start | bytes 1572868
  53.7 36.7 %collective-permute-start.9 = (bf16[128,3584]{1,0:T(8,128)(2,1)}, bf16[128,3584]{1,0:T(8,128)(2,1)}, u32[]{:S(2)}, u32[]{:S(2)}) collective-permute-start(bf16[128,3584]{1,0:T(8,128)(2,1)} %fusion.16), channel_id=1, source_target_pairs={{0,2},{1,3},{2,0},{3,1},{4,6},{5,7},{6,4},{7,5},{8,10},{9,11},{10,... | collective-permute-start | bytes 2752520 | tf_op jit(solution)/shard_map/ppermute | solution.py:30
  55.7 27.5 %copy-start.6 = (bf16[512,512]{1,0:T(8,128)(2,1)}, bf16[512,512]{1,0:T(8,128)(2,1)S(1)}, u32[]{:S(2)}) copy-start(bf16[512,512]{1,0:T(8,128)(2,1)S(1)} %collective-permute-done.6) | copy-start | bytes 1572868
  55.7 12.9 %collective-permute-start.7 = (bf16[128,2048]{1,0:T(8,128)(2,1)S(1)}, bf16[128,2048]{1,0:T(8,128)(2,1)S(1)}, u32[]{:S(2)}, u32[]{:S(2)}) collective-permute-start(bf16[128,2048]{1,0:T(8,128)(2,1)S(1)} %collective-permute-done.2), channel_id=1, source_target_pairs={{0,16},{1,17},{18,2},{19,3},{4,20},{5,21},{22,6},{23,7},{8,24},{9,... | collective-permute-start | bytes 1572872 | tf_op jit(solution)/shard_map/ppermute | solution.py:54
  68.8 26.4 %collective-permute-start.8 = (bf16[256,2048]{1,0:T(8,128)(2,1)S(1)}, bf16[256,2048]{1,0:T(8,128)(2,1)S(1)}, u32[]{:S(2)}, u32[]{:S(2)}) collective-permute-start(bf16[256,2048]{1,0:T(8,128)(2,1)S(1)} %slice.146), channel_id=1, source_target_pairs={{0,16},{1,17},{18,2},{19,3},{4,20},{5,21},{22,6},{23,7},{8,24},{9,... | collective-permute-start | bytes 3145736 | tf_op jit(solution)/shard_map/ppermute | solution.py:61
  81.2 2.0 %copy-start.3 = (bf16[1,512,512]{2,1,0:T(8,128)(2,1)S(1)}, bf16[1,512,512]{2,1,0:T(8,128)(2,1)}, u32[]{:S(2)}) copy-start(bf16[1,512,512]{2,1,0:T(8,128)(2,1)} %param.11) | copy-start | bytes 1572868
  83.4 30.6 %collective-permute-start.13 = (bf16[2,512,512]{2,1,0:T(8,128)(2,1)S(1)}, bf16[2,512,512]{2,1,0:T(8,128)(2,1)S(1)}, u32[]{:S(2)}, u32[]{:S(2)}) collective-permute-start(bf16[2,512,512]{2,1,0:T(8,128)(2,1)S(1)} %maximum_select_fusion.2), channel_id=1, source_target_pairs={{0,16},{1,17},{18,2},{19,3},{2,18},{3,19},{16,0},{17,1},{4,20},{5,... | collective-permute-start | bytes 3145736 | tf_op jit(solution)/shard_map/ppermute | solution.py:98
  83.5 46.2 %collective-permute-start.11 = (bf16[128,7168]{1,0:T(8,128)(2,1)}, bf16[128,7168]{1,0:T(8,128)(2,1)}, u32[]{:S(2)}, u32[]{:S(2)}) collective-permute-start(bf16[128,7168]{1,0:T(8,128)(2,1)} %fusion), channel_id=1, source_target_pairs={{0,2},{1,3},{2,0},{3,1},{4,6},{5,7},{6,4},{7,5},{8,10},{9,11},{10,... | collective-permute-start | bytes 5505032 | tf_op jit(solution)/shard_map/ppermute | solution.py:30
  104.3 9.7 %copy-start.5 = (bf16[512,512]{1,0:T(8,128)(2,1)S(1)}, bf16[512,512]{1,0:T(8,128)(2,1)}, u32[]{:S(2)}) copy-start(bf16[512,512]{1,0:T(8,128)(2,1)} %copy-done.4) | copy-start | bytes 1572868
  104.3 9.7 %copy-start.7 = (bf16[512,512]{1,0:T(8,128)(2,1)S(1)}, bf16[512,512]{1,0:T(8,128)(2,1)}, u32[]{:S(2)}) copy-start(bf16[512,512]{1,0:T(8,128)(2,1)} %copy-done.6) | copy-start | bytes 1572868
  104.9 13.4 %collective-permute-start.12 = (f32[384,32]{0,1:T(8,128)S(1)}, f32[384,32]{0,1:T(8,128)S(1)}, u32[]{:S(2)}, u32[]{:S(2)}) collective-permute-start(f32[384,32]{0,1:T(8,128)S(1)} %fusion.81), channel_id=1, source_target_pairs={{0,16},{16,0},{1,17},{17,1},{2,18},{18,2},{3,19},{19,3},{4,20},{20... | collective-permute-start | bytes 147464 | tf_op jit(solution)/shard_map/ppermute | solution.py:183
  116.0 32.3 %collective-permute-start.14 = (bf16[2,2,512,512]{3,2,1,0:T(8,128)(2,1)}, bf16[2,2,512,512]{3,2,1,0:T(8,128)(2,1)S(1)}, u32[]{:S(2)}, u32[]{:S(2)}) collective-permute-start(bf16[2,2,512,512]{3,2,1,0:T(8,128)(2,1)} %maximum_select_fusion), channel_id=1, source_target_pairs={{0,1},{1,0},{2,3},{3,2},{4,5},{5,4},{6,7},{7,6},{8,9},{9,8},{10,11... | collective-permute-start | bytes 6291464 | tf_op jit(solution)/shard_map/ppermute | solution.py:102
  116.0 43.2 %collective-permute-start.15 = (bf16[96,7168]{1,0:T(8,128)(2,1)}, bf16[96,7168]{1,0:T(8,128)(2,1)}, u32[]{:S(2)}, u32[]{:S(2)}) collective-permute-start(bf16[96,7168]{1,0:T(8,128)(2,1)} %slice.189), channel_id=1, source_target_pairs={{0,2},{1,3},{2,0},{3,1},{4,6},{5,7},{6,4},{7,5},{8,10},{9,11},{10,... | collective-permute-start | bytes 4128776 | tf_op jit(solution)/shard_map/ppermute | solution.py:30
  118.3 25.6 %copy-start.8 = (bf16[32,7168]{1,0:T(8,128)(2,1)S(1)}, bf16[32,7168]{1,0:T(8,128)(2,1)}, u32[]{:S(2)}) copy-start(bf16[32,7168]{1,0:T(8,128)(2,1)} %param.10) | copy-start | bytes 1376260
  142.7 23.3 %collective-permute-start.16 = (bf16[32,7168]{1,0:T(8,128)(2,1)}, bf16[32,7168]{1,0:T(8,128)(2,1)S(1)}, u32[]{:S(2)}, u32[]{:S(2)}) collective-permute-start(bf16[32,7168]{1,0:T(8,128)(2,1)} %slice.190), channel_id=1, source_target_pairs={{0,2},{1,3},{2,0},{3,1},{4,6},{5,7},{6,4},{7,5},{8,10},{9,11},{10,... | collective-permute-start | bytes 1376264 | tf_op jit(solution)/shard_map/ppermute | solution.py:30
  148.8 2.6 %slice-start.4 = ((s8[5505024]{0:T(1024)(128)(4,1)}), s8[4194304]{0:T(1024)(128)(4,1)S(1)}, s32[]{:S(2)}) async-start(s8[5505024]{0:T(1024)(128)(4,1)} %bitcast.111), calls=%async_computation.4 | async-start | bytes 8388608
  149.1 2.7 %slice-start.5 = ((s8[5505024]{0:T(1024)(128)(4,1)}), s8[1310720]{0:T(1024)(128)(4,1)S(1)}, s32[]{:S(2)}) async-start(s8[5505024]{0:T(1024)(128)(4,1)} %bitcast.111), calls=%async_computation.5 | async-start | bytes 2621440
  149.2 2.7 %copy-start.9 = (bf16[32,7168]{1,0:T(8,128)(2,1)S(1)}, bf16[32,7168]{1,0:T(8,128)(2,1)}, u32[]{:S(2)}) copy-start(bf16[32,7168]{1,0:T(8,128)(2,1)} %param.10) | copy-start | bytes 1376260
  166.9 15.7 %copy-start.1 = (bf16[32,4096]{1,0:T(8,128)(2,1)S(1)}, bf16[32,4096]{1,0:T(8,128)(2,1)}, u32[]{:S(2)}) copy-start(bf16[32,4096]{1,0:T(8,128)(2,1)} %param.9) | copy-start | bytes 786436
  169.4 4.2 %collective-permute-start.17 = (f32[3,1024]{1,0:T(4,128)S(1)}, f32[3,1024]{1,0:T(4,128)S(1)}, u32[]{:S(2)}, u32[]{:S(2)}) collective-permute-start(f32[3,1024]{1,0:T(4,128)S(1)} %bitcast.108), channel_id=1, source_target_pairs={{0,16},{16,0},{1,17},{17,1},{2,18},{18,2},{3,19},{19,3},{4,20},{20... | collective-permute-start | bytes 36872 | tf_op jit(solution)/shard_map/ppermute | solution.py:119
  173.7 5.5 %collective-permute-start.18 = (f32[3,256]{1,0:T(4,128)S(1)}, f32[3,256]{1,0:T(4,128)S(1)}, u32[]{:S(2)}, u32[]{:S(2)}) collective-permute-start(f32[3,256]{1,0:T(4,128)S(1)} %get-tuple-element.89), channel_id=1, source_target_pairs={{0,4},{4,8},{8,12},{12,0},{1,5},{5,9},{9,13},{13,1},{2,6},{6,10},{... | collective-permute-start | bytes 9224 | tf_op jit(solution)/shard_map/ppermute | solution.py:119
  175.3 3.8 %collective-permute-start.20 = (f32[3,256]{1,0:T(4,128)S(1)}, f32[3,256]{1,0:T(4,128)S(1)}, u32[]{:S(2)}, u32[]{:S(2)}) collective-permute-start(f32[3,256]{1,0:T(4,128)S(1)} %get-tuple-element.90), channel_id=1, source_target_pairs={{0,12},{4,0},{8,4},{12,8},{1,13},{5,1},{9,5},{13,9},{2,14},{6,2},{... | collective-permute-start | bytes 9224 | tf_op jit(solution)/shard_map/ppermute | solution.py:119
  177.5 4.5 %collective-permute-start.19 = (f32[3,256]{1,0:T(4,128)S(1)}, f32[3,256]{1,0:T(4,128)S(1)}, u32[]{:S(2)}, u32[]{:S(2)}) collective-permute-start(f32[3,256]{1,0:T(4,128)S(1)} %get-tuple-element.91), channel_id=1, source_target_pairs={{0,8},{4,12},{8,0},{12,4},{1,9},{5,13},{9,1},{13,5},{2,10},{6,14},... | collective-permute-start | bytes 9224 | tf_op jit(solution)/shard_map/ppermute | solution.py:119
